TPU v7x, 32 devices: a whole 2x2x4 slice. The times are simulated.
32 devices in a mesh: dp: 8 (over y, x, core), seq: 4 (over z).
Axes of the slice: x: 2, y: 2, z: 4, core: 2. Of those that a mesh axis runs over, the one named last changes fastest.
Arguments:
- frames_in: bfloat16 [2, 16, 16, 208, 768], P(None, 'dp', 'seq'), may hold values from -6 to 6
- qkv_spatial: bfloat16 [768, 2304], P(('dp', 'seq')), may hold values from -0.21875 to 0.21875
- out_spatial: bfloat16 [768, 768], P(('dp', 'seq')), may hold values from -0.875 to 0.875
- qkv_temporal: bfloat16 [768, 2304], P(('dp', 'seq')), may hold values from -0.21875 to 0.21875
- out_temporal: bfloat16 [768, 768], P(('dp', 'seq')), may hold values from -0.4375 to 0.4375
- mlp_in: bfloat16 [768, 3072], P(('dp', 'seq')), may hold values from -0.21875 to 0.21875
- mlp_out: bfloat16 [3072, 768], P(('dp', 'seq')), may hold values from -0.109375 to 0.109375
- gains: bfloat16 [768, 3], P(('dp', 'seq')), may hold values from 0.099609375 to 1.8984375
- place_mask: int32 [208], replicated, may hold values from 0 to 1, as said below
- cotangent: bfloat16 [2, 16, 16, 208, 768], P(None, 'dp', 'seq'), may hold values from -6 to 6
Outputs:
- frames_out: bfloat16 [2, 16, 16, 208, 768], P(None, 'dp', 'seq')
- frames_grad: float32 [2, 16, 16, 208, 768], P(None, 'dp', 'seq')
- qkv_spatial_grad: float32 [768, 2304], P(('dp', 'seq'))
- out_spatial_grad: float32 [768, 768], P(('dp', 'seq'))
- qkv_temporal_grad: float32 [768, 2304], P(('dp', 'seq'))
- out_temporal_grad: float32 [768, 768], P(('dp', 'seq'))
- mlp_in_grad: float32 [768, 3072], P(('dp', 'seq'))
- mlp_out_grad: float32 [3072, 768], P(('dp', 'seq'))
- gains_grad: float32 [768, 3], P(('dp', 'seq'))
Inputs may be any that keep to these rules, and one draw needn't show every extreme that they name: `place_mask`: exactly 196 of the 208 entries are 1; which slots are padding varies with the seed.
All inputs are finite; a program needn't handle non-finite values.
Results may differ from a plain program's by a relative error of at most 0.028.
Values may be sent and summed in bfloat16 or wider, within the bound.
No kernel may reach another device: no remote copies, remote signals or barrier semaphores. Data moves between devices by JAX's collectives and lax.ppermute only.
A program may use at most 576 MiB of HBM per device.

v0:
```python
import jax
import jax.numpy as jnp
from jax import lax
from jax.sharding import PartitionSpec as P

HEAD_DIM = 64


epsilon = 1e-06


def layer_norm(values_in, norm_gain):
    centered = values_in - jnp.mean(values_in, axis=-1, keepdims=True)
    spread = jnp.mean(centered * centered, axis=-1, keepdims=True)
    return centered * lax.rsqrt(spread + epsilon) * norm_gain


def norm_back(values_in, norm_gain, upstream):
    pullback = jax.vjp(layer_norm, values_in, norm_gain)[1]
    return pullback(upstream)


def attend_forward(query_rows, key_rows, value_rows, allowed):
    scaling = query_rows.shape[-1] ** (-0.5)
    scores = (
        jnp.einsum("cqphe,ckphe->cphqk", query_rows, key_rows, preferred_element_type=jnp.float32)
        * scaling
    )
    scores = jnp.where(allowed, scores, -1000000000.0)
    largest = jnp.max(scores, axis=-1, keepdims=True)
    exponent = jnp.exp(scores - largest)
    denominator = jnp.sum(exponent, axis=-1, keepdims=True)
    weights_low = (exponent / denominator).astype(jnp.bfloat16)
    result = jnp.einsum(
        "cphqk,ckphe->cqphe", weights_low, value_rows, preferred_element_type=jnp.float32
    )
    return (result, largest + jnp.log(denominator))


def attend_backward(query_rows, key_rows, value_rows, allowed, log_norm, grad_result):
    scaling = query_rows.shape[-1] ** (-0.5)
    scores = (
        jnp.einsum("cqphe,ckphe->cphqk", query_rows, key_rows, preferred_element_type=jnp.float32)
        * scaling
    )
    scores = jnp.where(allowed, scores, -1000000000.0)
    weights = jnp.exp(scores - log_norm)
    grad_weights = jnp.einsum(
        "cqphe,ckphe->cphqk", grad_result, value_rows, preferred_element_type=jnp.float32
    )
    row_inner = jnp.sum(weights * grad_weights, axis=-1, keepdims=True)
    grad_scores = (weights * (grad_weights - row_inner)).astype(jnp.bfloat16)
    grad_query = (
        jnp.einsum("cphqk,ckphe->cqphe", grad_scores, key_rows, preferred_element_type=jnp.float32)
        * scaling
    )
    grad_key = (
        jnp.einsum(
            "cphqk,cqphe->ckphe", grad_scores, query_rows, preferred_element_type=jnp.float32
        )
        * scaling
    )
    grad_value = jnp.einsum(
        "cphqk,cqphe->ckphe",
        weights.astype(jnp.bfloat16),
        grad_result,
        preferred_element_type=jnp.float32,
    )
    return (grad_query, grad_key, grad_value)


def branch_back(
    upstream, stream, normed, mixed, log_norm, attended, qkv_weight, out_weight, norm_gain, allowed
):
    upstream_low = upstream.astype(jnp.bfloat16)
    grad_out = jnp.einsum(
        "abcd,abce->de", attended, upstream_low, preferred_element_type=jnp.float32
    )
    grad_attended = jnp.einsum(
        "abce,de->abcd", upstream_low, out_weight, preferred_element_type=jnp.float32
    )
    grad_attended = grad_attended.astype(jnp.bfloat16).reshape(mixed.shape[:3] + mixed.shape[4:])
    grad_query, grad_key, grad_value = attend_backward(
        mixed[:, :, :, 0], mixed[:, :, :, 1], mixed[:, :, :, 2], allowed, log_norm, grad_attended
    )
    grad_mixed = jnp.stack([grad_query, grad_key, grad_value], axis=3).astype(jnp.bfloat16)
    grad_mixed = grad_mixed.reshape(normed.shape[:3] + (qkv_weight.shape[1],))
    grad_qkv = jnp.einsum("abcd,abce->de", normed, grad_mixed, preferred_element_type=jnp.float32)
    grad_normed = jnp.einsum(
        "abce,de->abcd", grad_mixed, qkv_weight, preferred_element_type=jnp.float32
    )
    grad_stream, grad_gain = norm_back(stream, norm_gain, grad_normed)
    return (grad_stream + upstream, grad_qkv, grad_out, grad_gain)


def forward_pass(inputs_low, gathered, allowed, keep_rows):
    space_qkv, space_out, time_qkv, time_out, grow_in, shrink_out, gain_cols = gathered
    gain_cols = gain_cols.astype(jnp.float32)
    inputs = inputs_low.astype(jnp.float32)
    clip_count, local_frames, slot_count, width = inputs.shape
    head_count = width // HEAD_DIM
    normed_space = layer_norm(inputs, gain_cols[:, 0]).astype(jnp.bfloat16)
    mixed_space = jnp.dot(normed_space, space_qkv, preferred_element_type=jnp.float32).astype(
        jnp.bfloat16
    )
    mixed_space = mixed_space.reshape(
        clip_count * local_frames, slot_count, 1, 3, head_count, HEAD_DIM
    )
    attended, log_space = attend_forward(
        mixed_space[:, :, :, 0], mixed_space[:, :, :, 1], mixed_space[:, :, :, 2], allowed
    )
    attended_space = attended.astype(jnp.bfloat16).reshape(
        clip_count, local_frames, slot_count, width
    )
    after_space = inputs + jnp.dot(attended_space, space_out, preferred_element_type=jnp.float32)
    across = lax.all_to_all(
        after_space.astype(jnp.bfloat16), "seq", split_axis=2, concat_axis=1, tiled=True
    ).astype(after_space.dtype)
    all_frames, local_places = (across.shape[1], across.shape[2])
    normed_time = layer_norm(across, gain_cols[:, 1]).astype(jnp.bfloat16)
    mixed_time = jnp.dot(normed_time, time_qkv, preferred_element_type=jnp.float32).astype(
        jnp.bfloat16
    )
    mixed_time = mixed_time.reshape(clip_count, all_frames, local_places, 3, head_count, HEAD_DIM)
    attended, log_time = attend_forward(
        mixed_time[:, :, :, 0], mixed_time[:, :, :, 1], mixed_time[:, :, :, 2], True
    )
    attended_time = attended.astype(jnp.bfloat16).reshape(
        clip_count, all_frames, local_places, width
    )
    second_places = across + jnp.dot(attended_time, time_out, preferred_element_type=jnp.float32)
    second = lax.all_to_all(
        second_places.astype(jnp.bfloat16), "seq", split_axis=1, concat_axis=2, tiled=True
    ).astype(second_places.dtype)
    normed_mlp = layer_norm(second, gain_cols[:, 2]).astype(jnp.bfloat16)
    hidden = jnp.dot(normed_mlp, grow_in, preferred_element_type=jnp.float32)
    active = jax.nn.gelu(hidden).astype(jnp.bfloat16)
    result = second + jnp.dot(active, shrink_out, preferred_element_type=jnp.float32)
    frames_out = (result * keep_rows).astype(jnp.bfloat16)
    saved = (
        inputs,
        normed_space,
        mixed_space,
        log_space,
        attended_space,
        across,
        normed_time,
        mixed_time,
        log_time,
        attended_time,
        second,
        normed_mlp,
        hidden,
        active,
    )
    return (saved, frames_out)


def backward_pass(saved, upstream_in, gathered, allowed, keep_rows):
    (
        inputs,
        normed_space,
        mixed_space,
        log_space,
        attended_space,
        across,
        normed_time,
        mixed_time,
        log_time,
        attended_time,
        second,
        normed_mlp,
        hidden,
        active,
    ) = saved
    space_qkv, space_out, time_qkv, time_out, grow_in, shrink_out, gain_cols = gathered
    gain_cols = gain_cols.astype(jnp.float32)
    upstream = upstream_in.astype(jnp.float32) * keep_rows
    upstream_low = upstream.astype(jnp.bfloat16)
    grad_shrink = jnp.einsum(
        "cfsk,cfsd->kd", active, upstream_low, preferred_element_type=jnp.float32
    )
    grad_active = jnp.einsum(
        "cfsd,kd->cfsk", upstream_low, shrink_out, preferred_element_type=jnp.float32
    )
    gelu_pull = jax.vjp(jax.nn.gelu, hidden)[1]
    grad_hidden = gelu_pull(grad_active)[0].astype(jnp.bfloat16)
    grad_grow = jnp.einsum(
        "cfsd,cfsk->dk", normed_mlp, grad_hidden, preferred_element_type=jnp.float32
    )
    grad_normed = jnp.einsum(
        "cfsk,dk->cfsd", grad_hidden, grow_in, preferred_element_type=jnp.float32
    )
    grad_second, gain_mlp = norm_back(second, gain_cols[:, 2], grad_normed)
    grad_second = grad_second + upstream
    grad_places = lax.all_to_all(
        grad_second.astype(jnp.bfloat16), "seq", split_axis=2, concat_axis=1, tiled=True
    ).astype(grad_second.dtype)
    grad_across, grad_time_qkv, grad_time_out, gain_time = branch_back(
        grad_places,
        across,
        normed_time,
        mixed_time,
        log_time,
        attended_time,
        time_qkv,
        time_out,
        gain_cols[:, 1],
        True,
    )
    grad_after = lax.all_to_all(
        grad_across.astype(jnp.bfloat16), "seq", split_axis=1, concat_axis=2, tiled=True
    ).astype(grad_across.dtype)
    input_grad, grad_space_qkv, grad_space_out, gain_space = branch_back(
        grad_after,
        inputs,
        normed_space,
        mixed_space,
        log_space,
        attended_space,
        space_qkv,
        space_out,
        gain_cols[:, 0],
        allowed,
    )
    gain_grads = jnp.stack([gain_space, gain_time, gain_mlp], axis=1)
    return (
        input_grad,
        (
            grad_space_qkv,
            grad_space_out,
            grad_time_qkv,
            grad_time_out,
            grad_grow,
            grad_shrink,
            gain_grads,
        ),
    )


def shards(
    frames_in,
    qkv_spatial,
    out_spatial,
    qkv_temporal,
    out_temporal,
    mlp_in,
    mlp_out,
    gains,
    place_mask,
    cotangent,
):
    batches = frames_in.shape[0]
    allowed = (place_mask > 0)[None, None, None, None, :]
    keep_rows = place_mask.astype(jnp.float32)[None, None, :, None]
    shard_list = (qkv_spatial, out_spatial, qkv_temporal, out_temporal, mlp_in, mlp_out, gains)
    totals = tuple((jnp.zeros(shard_piece.shape, jnp.float32) for shard_piece in shard_list))
    outputs = []
    input_grads = []
    for micro in range(batches):
        gathered = (
            lax.all_gather(qkv_spatial, ("dp", "seq"), axis=0, tiled=True),
            lax.all_gather(out_spatial, ("dp", "seq"), axis=0, tiled=True),
            lax.all_gather(qkv_temporal, ("dp", "seq"), axis=0, tiled=True),
            lax.all_gather(out_temporal, ("dp", "seq"), axis=0, tiled=True),
            lax.all_gather(mlp_in, ("dp", "seq"), axis=0, tiled=True),
            lax.all_gather(mlp_out, ("dp", "seq"), axis=0, tiled=True),
            lax.all_gather(gains, ("dp", "seq"), axis=0, tiled=True),
        )
        saved, result = forward_pass(frames_in[micro], gathered, allowed, keep_rows)
        outputs.append(result)
        gathered = (
            lax.all_gather(qkv_spatial, ("dp", "seq"), axis=0, tiled=True),
            lax.all_gather(out_spatial, ("dp", "seq"), axis=0, tiled=True),
            lax.all_gather(qkv_temporal, ("dp", "seq"), axis=0, tiled=True),
            lax.all_gather(out_temporal, ("dp", "seq"), axis=0, tiled=True),
            lax.all_gather(mlp_in, ("dp", "seq"), axis=0, tiled=True),
            lax.all_gather(mlp_out, ("dp", "seq"), axis=0, tiled=True),
            lax.all_gather(gains, ("dp", "seq"), axis=0, tiled=True),
        )
        input_grad, grads = backward_pass(saved, cotangent[micro], gathered, allowed, keep_rows)
        input_grads.append(input_grad)
        owned = (
            lax.psum_scatter(grads[0], ("dp", "seq"), scatter_dimension=0, tiled=True),
            lax.psum_scatter(grads[1], ("dp", "seq"), scatter_dimension=0, tiled=True),
            lax.psum_scatter(grads[2], ("dp", "seq"), scatter_dimension=0, tiled=True),
            lax.psum_scatter(grads[3], ("dp", "seq"), scatter_dimension=0, tiled=True),
            lax.psum_scatter(grads[4], ("dp", "seq"), scatter_dimension=0, tiled=True),
            lax.psum_scatter(grads[5], ("dp", "seq"), scatter_dimension=0, tiled=True),
            lax.psum_scatter(grads[6], ("dp", "seq"), scatter_dimension=0, tiled=True),
        )
        totals = tuple((earlier + later for earlier, later in zip(totals, owned)))
    return (
        jnp.stack(outputs),
        jnp.stack(input_grads),
        totals[0],
        totals[1],
        totals[2],
        totals[3],
        totals[4],
        totals[5],
        totals[6],
    )


def solution(mesh):
    return jax.shard_map(
        shards,
        mesh=mesh,
        in_specs=(
            P(None, "dp", "seq", None, None),
            P(("dp", "seq"), None),
            P(("dp", "seq"), None),
            P(("dp", "seq"), None),
            P(("dp", "seq"), None),
            P(("dp", "seq"), None),
            P(("dp", "seq"), None),
            P(("dp", "seq"), None),
            P(),
            P(None, "dp", "seq", None, None),
        ),
        out_specs=(
            P(None, "dp", "seq", None, None),
            P(None, "dp", "seq", None, None),
            P(("dp", "seq"), None),
            P(("dp", "seq"), None),
            P(("dp", "seq"), None),
            P(("dp", "seq"), None),
            P(("dp", "seq"), None),
            P(("dp", "seq"), None),
            P(("dp", "seq"), None),
        ),
        check_vma=False,
    )
```

profile of v0, /device:TPU:0, one launch (start us, length us, event | category | flops | bytes accessed | tf_op | source)
XLA Modules:
  0.0 1918.6 jit_solution(10908582661739097094)
XLA Ops:
  17.0 69.9 %all-gather = bf16[32,24,3]{1,2,0:T(4,128)(2,1)S(1)} all-gather(bf16[1,24,3]{1,2,0:T(4,128)(2,1)S(1)} %bitcast.600), channel_id=1, replica_groups=mesh['dp'=8,'seq'=4] {'dp','seq'}, dimensions={0}, use_global_device_ids=true | all-gather | bytes 4752 | tf_op jit(solution)/shard_map/all_gather | solution.py:268
  224.8 17.8 all-to-all-done
  265.4 42.4 %all-to-all-done.2 = bf16[2,4,208,768]{3,1,0,2:T(4,128)(2,1)S(1)} async-done(((bf16[2,4,208,768]{3,1,0,2:T(4,128)(2,1)}), bf16[2,4,208,768]{3,1,0,2:T(4,128)(2,1)S(1)}, u32[]{:S(2)}, u32[]{:S(2)}) %all-to-all-start.2) | async-done | bytes 2555936 | tf_op jit(solution)/shard_map/all_to_all | solution.py:116
  338.5 19.4 %reshape.722 = bf16[2,16,52,3,12,64]{5,4,3,2,1,0:T(8,128)(2,1)} reshape(bf16[2,16,52,2304]{3,2,1,0:T(8,128)(2,1)} %convolution_convert_fusion.1) | data formatting | bytes 15335424 | tf_op jit(solution)/shard_map/reshape | solution.py:124
  372.2 16.2 multiply_reduce_fusion.5
  449.8 19.3 %reshape.723 = bf16[2,16,52,3,12,64]{5,4,3,2,1,0:T(8,128)(2,1)} reshape(bf16[2,16,52,2304]{3,2,1,0:T(8,128)(2,1)} %convolution_convert_fusion) | data formatting | bytes 15335424 | tf_op jit(solution)/shard_map/reshape | solution.py:124
  483.1 17.1 multiply_reduce_fusion.4
  568.0 41.0 %all-to-all-done.3 = bf16[2,16,52,768]{3,0,2,1:T(2,128)(2,1)} async-done(((bf16[2,16,52,768]{3,0,2,1:T(2,128)(2,1)}), bf16[2,16,52,768]{3,0,2,1:T(2,128)(2,1)}, u32[]{:S(2)}, u32[]{:S(2)}) %all-to-all-start.3) | async-done | bytes 2555936 | tf_op jit(solution)/shard_map/all_to_all | solution.py:132
  623.5 16.5 fusion.98
  640.0 26.1 %fusion.6 = bf16[2,4,208,3072]{3,2,1,0:T(8,128)(2,1)} fusion(f32[2,4,208,3072]{3,2,1,0:T(8,128)} %fusion.98, bf16[3072,768]{1,0:T(8,128)(2,1)} %all-gather.18.cloned.1.call-done, f32[208]{0:T(256)S(1)} %convert_element_type.407, bf16[2,2,4,208,768]{4,3,2,1,0:T(8,128)(2,1)} %param.19), kind=kOutput, calls=%fused_computation.12 | convolution fusion | flops 7957807104 | bytes 37946176 | tf_op jit(solution)/shard_map/cfsd,kd->cfsk/dot_general | solution.py:183
  699.4 22.9 %fusion.13 = bf16[2,4,208,3072]{3,2,1,0:T(8,128)(2,1)} fusion(f32[2,4,208,3072]{3,2,1,0:T(8,128)} %fusion.96, bf16[3072,768]{1,0:T(8,128)(2,1)} %all-gather.18.cloned.1.call-done, f32[208]{0:T(256)S(1)} %convert_element_type.407, bf16[2,2,4,208,768]{4,3,2,1,0:T(8,128)(2,1)S(1)} %bitcast.585), kind=kOutput, calls=%fused_computation.19 | convolution fusion | flops 7957807104 | bytes 37946368 | tf_op jit(solution)/shard_map/cfsd,kd->cfsk/dot_general | solution.py:183
  722.3 18.4 multiply_reduce_fusion.11
  767.4 52.6 %all-to-all-done.4 = bf16[2,4,208,768]{3,1,0,2:T(4,128)(2,1)} async-done(((bf16[2,4,208,768]{3,1,0,2:T(4,128)(2,1)}), bf16[2,4,208,768]{3,1,0,2:T(4,128)(2,1)}, u32[]{:S(2)}, u32[]{:S(2)}) %all-to-all-start.4) | async-done | bytes 2555936 | tf_op jit(solution)/shard_map/all_to_all | solution.py:196
  842.2 17.6 multiply_reduce_fusion.3
  910.8 17.7 multiply_reduce_fusion.2
  982.9 24.6 %convert_element_type.464 = bf16[2,16,52,2304]{3,1,2,0:T(8,128)(2,1)} reshape(bf16[2,16,52,3,12,64]{5,4,3,1,2,0:T(8,128)(2,1)} %copy.650) | data formatting | bytes 15335424 | tf_op jit(solution)/shard_map/convert_element_type | solution.py:86
  1021.7 24.7 %convert_element_type.446 = bf16[2,16,52,2304]{3,1,2,0:T(8,128)(2,1)} reshape(bf16[2,16,52,3,12,64]{5,4,3,1,2,0:T(8,128)(2,1)} %copy.631) | data formatting | bytes 15335424 | tf_op jit(solution)/shard_map/convert_element_type | solution.py:86
  1046.5 16.1 multiply_reduce_fusion.9
  1062.7 18.5 multiply_reduce_fusion.7
  1112.3 49.2 %all-to-all-done.7 = bf16[2,16,52,768]{3,0,2,1:T(2,128)(2,1)} async-done(((bf16[2,16,52,768]{3,0,2,1:T(2,128)(2,1)}), bf16[2,16,52,768]{3,0,2,1:T(2,128)(2,1)}, u32[]{:S(2)}, u32[]{:S(2)}) %all-to-all-start.7) | async-done | bytes 2555936 | tf_op jit(solution)/shard_map/all_to_all | solution.py:211
  1175.1 48.5 %all-to-all-done.5 = bf16[2,16,52,768]{3,0,2,1:T(2,128)(2,1)} async-done(((bf16[2,16,52,768]{3,0,2,1:T(2,128)(2,1)}), bf16[2,16,52,768]{3,0,2,1:T(2,128)(2,1)}, u32[]{:S(2)}, u32[]{:S(2)}) %all-to-all-start.5) | async-done | bytes 2555936 | tf_op jit(solution)/shard_map/all_to_all | solution.py:211
  1233.6 19.1 fusion.206
  1252.7 20.5 %bitcast_add_fusion = f32[3072,768]{1,0:T(8,128)} fusion(f32[3072,768,1,1]{1,0,3,2:T(8,128)} %fusion.206, f32[208]{0:T(256)S(1)} %copy-done.84, bf16[2,2,4,208,768]{4,3,2,1,0:T(8,128)(2,1)} %param.19, f32[2,4,208,3072]{3,2,1,0:T(8,128)} %fusion.96), kind=kOutput, calls=%fused_computation.61 | convolution fusion | flops 7903936512 | bytes 41878336 | tf_op jit(solution)/shard_map/cfsk,cfsd->kd/dot_general | solution.py:180
  1309.8 16.6 bitcast_add_fusion.1
  1326.5 21.2 %fusion.146 = bf16[1,2,4,208,768]{4,3,2,1,0:T(8,128)(2,1)} fusion(f32[2,4,208,768]{3,1,2,0:T(4,128)} %bitcast.564, f32[208]{0:T(256)S(1)} %copy-done.84, bf16[3072,768]{1,0:T(8,128)(2,1)} %all-gather.18.cloned.1.call-done, f32[2,4,208,3072]{3,2,1,0:T(8,128)} %fusion.98), kind=kOutput, calls=%fused_computation.244 | convolution fusion | flops 7901577216 | bytes 32834368 | tf_op jit(solution)/shard_map/dot_general | solution.py:138
  1403.3 19.8 %multiply_convert_fusion = bf16[8,12,208,208]{2,3,1,0:T(8,128)(2,1)} fusion(f32[8,12,208,208]{2,3,1,0:T(8,128)} %get-tuple-element.73, f32[8,12,208,208]{2,3,1,0:T(8,128)} %get-tuple-element.53, f32[8,12,208]{2,1,0:T(8,128)S(1)} %get-tuple-element.72, f32[8,12,208]{2,1,0:T(8,128)S(1)} %copy-done.36), kind=kLoop, calls=%fused_computation.20 | loop fusion | flops 16613376 | bytes 41693184 | tf_op jit(solution)/shard_map/convert_element_type | solution.py:52
  1484.2 17.9 multiply_convert_fusion.1
  1551.1 16.1 fusion.151
  1583.6 19.6 %fusion.147 = bf16[1,2,4,208,768]{4,3,2,1,0:T(8,128)(2,1)S(1)} fusion(f32[2,4,208,768]{3,1,2,0:T(4,128)} %bitcast.542, f32[208]{0:T(256)S(1)} %copy-done.85, bf16[3072,768]{1,0:T(8,128)(2,1)} %all-gather.18.cloned.1.call-done, f32[2,4,208,3072]{3,2,1,0:T(8,128)} %fusion.96), kind=kOutput, calls=%fused_computation.245 | convolution fusion | flops 7901577216 | bytes 32834368 | tf_op jit(solution)/shard_map/dot_general | solution.py:138
  1638.8 38.4 %all-reduce = f32[768,3]{0,1:T(4,128)S(1)} all-reduce(f32[768,3]{0,1:T(4,128)S(1)} %maximum_add_fusion), channel_id=15, replica_groups=mesh['dp'=8,'seq'=4] {'dp','seq'}, use_global_device_ids=true, to_apply=%region_51.52.clone | all-reduce | flops 2304 | bytes 18432
  1691.7 94.2 %reduce-scatter.12.cloned.1.call-done = f32[24,2304]{1,0:T(8,128)} async-done(((f32[768,2304]{1,0:T(8,128)}), f32[24,2304]{1,0:T(8,128)}) %reduce-scatter.12.cloned.1.call-update) | async-done | bytes 221200 | tf_op jit(solution)/shard_map/reduce_scatter | solution.py:286
  1785.9 125.4 %reduce-scatter.8.cloned.1.call-done = f32[24,2304]{1,0:T(8,128)} async-done(((f32[768,2304]{1,0:T(8,128)}), f32[24,2304]{1,0:T(8,128)}) %reduce-scatter.8.cloned.1.call-update) | async-done | bytes 221200 | tf_op jit(solution)/shard_map/reduce_scatter | solution.py:284
  (474 shorter events, 897.0 us)
Async XLA Ops:
  7.2 80.6 %all-gather.8.cloned.1.call-start = ((), (), s32[]{:S(2)}) async-start(), calls=%async_computation.14 | async-start | bytes 3649536 | tf_op jit(solution)/shard_map/all_gather | solution.py:262
  7.9 161.2 %all-gather.10.cloned.1.call-start = ((), (), s32[]{:S(2)}) async-start(), calls=%async_computation.15 | async-start | bytes 1216512 | tf_op jit(solution)/shard_map/all_gather | solution.py:263
  8.7 317.7 %all-gather.12.cloned.1.call-start = ((), (), s32[]{:S(2)}) async-start(), calls=%async_computation.16 | async-start | bytes 3649536 | tf_op jit(solution)/shard_map/all_gather | solution.py:264
  9.4 412.4 %all-gather.14.cloned.1.call-start = ((), (), s32[]{:S(2)}) async-start(), calls=%async_computation.17 | async-start | bytes 1216512 | tf_op jit(solution)/shard_map/all_gather | solution.py:265
  10.0 613.5 %all-gather.16.cloned.1.call-start = ((), (), s32[]{:S(2)}) async-start(), calls=%async_computation.18 | async-start | bytes 4866048 | tf_op jit(solution)/shard_map/all_gather | solution.py:266
  15.1 83.6 %copy-start.49 = (f32[2,4,208]{2,1,0:T(4,128)}, f32[2,4,208]{2,1,0:T(4,128)S(1)}, u32[]{:S(2)}) copy-start(f32[2,4,208]{2,1,0:T(4,128)S(1)} %get-tuple-element.76) | copy-start | bytes 19972
  15.1 131.5 %copy-start.47 = (f32[2,4,208]{2,1,0:T(4,128)}, f32[2,4,208]{2,1,0:T(4,128)S(1)}, u32[]{:S(2)}) copy-start(f32[2,4,208]{2,1,0:T(4,128)S(1)} %get-tuple-element.75) | copy-start | bytes 19972
  16.9 81.8 %copy-start.51 = (f32[2,4,208]{2,1,0:T(4,128)}, f32[2,4,208]{2,1,0:T(4,128)S(1)}, u32[]{:S(2)}) copy-start(f32[2,4,208]{2,1,0:T(4,128)S(1)} %get-tuple-element.26) | copy-start | bytes 19972
  16.9 81.8 %copy-start.53 = (f32[2,4,208]{2,1,0:T(4,128)}, f32[2,4,208]{2,1,0:T(4,128)S(1)}, u32[]{:S(2)}) copy-start(f32[2,4,208]{2,1,0:T(4,128)S(1)} %get-tuple-element.25) | copy-start | bytes 19972
  16.9 81.8 %copy-start.59 = (f32[2,4,208]{2,1,0:T(4,128)}, f32[2,4,208]{2,1,0:T(4,128)S(1)}, u32[]{:S(2)}) copy-start(f32[2,4,208]{2,1,0:T(4,128)S(1)} %fusion.218) | copy-start | bytes 19972
  16.9 129.6 %copy-start.61 = (f32[2,4,208]{2,1,0:T(4,128)}, f32[2,4,208]{2,1,0:T(4,128)S(1)}, u32[]{:S(2)}) copy-start(f32[2,4,208]{2,1,0:T(4,128)S(1)} %fusion.219) | copy-start | bytes 19972
  176.2 66.5 %all-to-all-start = ((bf16[2,4,208,768]{3,1,0,2:T(4,128)(2,1)}), bf16[2,4,208,768]{3,1,0,2:T(4,128)(2,1)}, u32[]{:S(2)}, u32[]{:S(2)}) async-start(bf16[2,4,208,768]{3,1,0,2:T(4,128)(2,1)} %copy.576), calls=%async_computation | async-start | bytes 5111808 | tf_op jit(solution)/shard_map/all_to_all | solution.py:116
  242.7 65.1 %all-to-all-start.2 = ((bf16[2,4,208,768]{3,1,0,2:T(4,128)(2,1)}), bf16[2,4,208,768]{3,1,0,2:T(4,128)(2,1)S(1)}, u32[]{:S(2)}, u32[]{:S(2)}) async-start(bf16[2,4,208,768]{3,1,0,2:T(4,128)(2,1)} %copy.603), calls=%async_computation.2 | async-start | bytes 5111808 | tf_op jit(solution)/shard_map/all_to_all | solution.py:116
  246.3 393.7 %all-gather.18.cloned.1.call-start = ((), (), s32[]{:S(2)}) async-start(), calls=%async_computation.19 | async-start | bytes 4866048 | tf_op jit(solution)/shard_map/all_gather | solution.py:267
  317.5 119.6 %copy-start.41 = (f32[2,4,4,52]{3,2,1,0:T(4,128)}, f32[2,4,4,52]{3,2,1,0:T(4,128)S(1)}, u32[]{:S(2)}) copy-start(f32[2,4,4,52]{3,2,1,0:T(4,128)S(1)} %copy.741) | copy-start | bytes 19972
  432.6 113.5 %all-to-all-start.1 = ((bf16[2,16,52,768]{3,0,2,1:T(2,128)(2,1)}), bf16[2,16,52,768]{3,0,2,1:T(2,128)(2,1)S(1)}, u32[]{:S(2)}, u32[]{:S(2)}) async-start(bf16[2,16,52,768]{3,0,2,1:T(2,128)(2,1)} %copy.590), calls=%async_computation.1 | async-start | bytes 5111808 | tf_op jit(solution)/shard_map/all_to_all | solution.py:132
  546.1 62.9 %all-to-all-start.3 = ((bf16[2,16,52,768]{3,0,2,1:T(2,128)(2,1)}), bf16[2,16,52,768]{3,0,2,1:T(2,128)(2,1)}, u32[]{:S(2)}, u32[]{:S(2)}) async-start(bf16[2,16,52,768]{3,0,2,1:T(2,128)(2,1)} %copy.617), calls=%async_computation.3 | async-start | bytes 5111808 | tf_op jit(solution)/shard_map/all_to_all | solution.py:132
  551.6 194.4 %copy-start.83 = (f32[208]{0:T(256)}, f32[208]{0:T(256)S(1)}, u32[]{:S(2)}) copy-start(f32[208]{0:T(256)S(1)} %convert_element_type.407) | copy-start | bytes 2500
  558.0 188.1 %copy-start.75 = (f32[2,4,208]{2,1,0:T(4,128)}, f32[2,4,208]{2,1,0:T(4,128)S(1)}, u32[]{:S(2)}) copy-start(f32[2,4,208]{2,1,0:T(4,128)S(1)} %div.172) | copy-start | bytes 19972
  564.6 181.4 %copy-start.77 = (f32[2,4,208]{2,1,0:T(4,128)}, f32[2,4,208]{2,1,0:T(4,128)S(1)}, u32[]{:S(2)}) copy-start(f32[2,4,208]{2,1,0:T(4,128)S(1)} %rsqrt.74) | copy-start | bytes 19972
  680.5 65.6 %copy-start.55 = (f32[2,4,208]{2,1,0:T(4,128)}, f32[2,4,208]{2,1,0:T(4,128)S(1)}, u32[]{:S(2)}) copy-start(f32[2,4,208]{2,1,0:T(4,128)S(1)} %div.184) | copy-start | bytes 19972
  757.9 62.1 %all-to-all-start.4 = ((bf16[2,4,208,768]{3,1,0,2:T(4,128)(2,1)}), bf16[2,4,208,768]{3,1,0,2:T(4,128)(2,1)}, u32[]{:S(2)}, u32[]{:S(2)}) async-start(bf16[2,4,208,768]{3,1,0,2:T(4,128)(2,1)} %copy.624), calls=%async_computation.4 | async-start | bytes 5111808 | tf_op jit(solution)/shard_map/all_to_all | solution.py:196
  820.0 74.5 %all-to-all-start.6 = ((bf16[2,4,208,768]{3,1,0,2:T(4,128)(2,1)}), bf16[2,4,208,768]{3,1,0,2:T(4,128)(2,1)}, u32[]{:S(2)}, u32[]{:S(2)}) async-start(bf16[2,4,208,768]{3,1,0,2:T(4,128)(2,1)} %copy.643), calls=%async_computation.6 | async-start | bytes 5111808 | tf_op jit(solution)/shard_map/all_to_all | solution.py:196
  1099.3 62.2 %all-to-all-start.7 = ((bf16[2,16,52,768]{3,0,2,1:T(2,128)(2,1)}), bf16[2,16,52,768]{3,0,2,1:T(2,128)(2,1)}, u32[]{:S(2)}, u32[]{:S(2)}) async-start(bf16[2,16,52,768]{3,0,2,1:T(2,128)(2,1)} %copy.652), calls=%async_computation.7 | async-start | bytes 5111808 | tf_op jit(solution)/shard_map/all_to_all | solution.py:211
  1161.5 62.1 %all-to-all-start.5 = ((bf16[2,16,52,768]{3,0,2,1:T(2,128)(2,1)}), bf16[2,16,52,768]{3,0,2,1:T(2,128)(2,1)}, u32[]{:S(2)}, u32[]{:S(2)}) async-start(bf16[2,16,52,768]{3,0,2,1:T(2,128)(2,1)} %copy.633), calls=%async_computation.5 | async-start | bytes 5111808 | tf_op jit(solution)/shard_map/all_to_all | solution.py:211
  1166.0 525.6 %reduce-scatter.14.cloned.1.call-start = ((), (), s32[]{:S(2)}) async-start(), calls=%async_computation.23 | async-start | bytes 2433024 | tf_op jit(solution)/shard_map/reduce_scatter | solution.py:287
  1172.4 519.3 %reduce-scatter.10.cloned.1.call-start = ((), (), s32[]{:S(2)}) async-start(), calls=%async_computation.21 | async-start | bytes 2433024 | tf_op jit(solution)/shard_map/reduce_scatter | solution.py:285
  1175.1 194.3 %copy-start.20 = (bf16[2,4,4,52,768]{4,2,3,1,0:T(4,128)(2,1)}, bf16[2,4,4,52,768]{4,2,3,1,0:T(4,128)(2,1)S(1)}, u32[]{:S(2)}) copy-start(bf16[2,4,4,52,768]{4,2,3,1,0:T(4,128)(2,1)S(1)} %copy.653) | copy-start | bytes 7667716
  1233.2 458.5 %reduce-scatter.18.cloned.1.call-start = ((), (), s32[]{:S(2)}) async-start(), calls=%async_computation.25 | async-start | bytes 9732096 | tf_op jit(solution)/shard_map/reduce_scatter | solution.py:289
  1273.2 418.4 %reduce-scatter.16.cloned.1.call-start = ((), (), s32[]{:S(2)}) async-start(), calls=%async_computation.24 | async-start | bytes 9732096 | tf_op jit(solution)/shard_map/reduce_scatter | solution.py:288
  1326.4 459.5 %reduce-scatter.12.cloned.1.call-start = ((), (), s32[]{:S(2)}) async-start(), calls=%async_computation.22 | async-start | bytes 7299072 | tf_op jit(solution)/shard_map/reduce_scatter | solution.py:286
  1369.2 542.1 %reduce-scatter.8.cloned.1.call-start = ((), (), s32[]{:S(2)}) async-start(), calls=%async_computation.20 | async-start | bytes 7299072 | tf_op jit(solution)/shard_map/reduce_scatter | solution.py:284
  (111 other events, 1550.5 us)
Sparse Core Ops, SparseCore 0:
  10.8 62.9 all-gather.7
  76.6 52.8 all-gather.9
  132.3 73.0 all-gather.11
  208.1 88.1 all-gather.13
  299.0 65.0 all-gather.15
  366.8 62.3 all-gather.17
  1172.7 100.7 reduce-scatter.13
  1280.2 98.0 reduce-scatter.9
  1384.8 134.6 reduce-scatter.17
  1526.8 134.6 reduce-scatter.15
  1667.8 118.0 reduce-scatter.11
  1792.9 118.3 reduce-scatter.7
where the time goes:
time: 1930 us; the launch traced here: 1920 us
  matrix products  727 us (38%)
  waiting for transfers between devices  475 us (25%)
  local copies, waits for them, and re-layouts  320 us (17%)
  other arithmetic  235 us (12%)
  blocking collectives  108 us (6%)
  starting transfers between devices  37.9 us (2%)
    reduce_scatter x1, waiting for transfers between devices, shards(): lax.psum_scatter(grads[0], ('dp', 'seq'), scatter_dimension=0, tiled=True)  125 us
    all_to_all x2, waiting for transfers between devices, backward_pass(): lax.all_to_all(grad_across.astype(jnp.bfloat16), 'seq', split_axis=1, con...  97.7 us
    reduce_scatter x1, waiting for transfers between devices, shards(): lax.psum_scatter(grads[2], ('dp', 'seq'), scatter_dimension=0, tiled=True)  94.2 us
    convert_element_type x6, local copies, waits for them, and re-layouts, branch_back(): jnp.stack([grad_query, grad_key, grad_value], axis=3).astype(jnp.bfloat16)  83.3 us
    all_gather x1, blocking collectives, shards(): lax.all_gather(gains, ('dp', 'seq'), axis=0, tiled=True)  69.9 us
    dot_general x4, matrix products, attend_backward(): jnp.einsum('cqphe,ckphe->cphqk', grad_result, value_rows, preferred_eleme...  66.5 us
    dot_general x4, matrix products, attend_forward(): jnp.einsum('cqphe,ckphe->cphqk', query_rows, key_rows, preferred_element_...  63.1 us
    dot_general x4, matrix products, branch_back(): jnp.einsum('abce,de->abcd', grad_mixed, qkv_weight, preferred_element_typ...  60.8 us
  transfers between devices with their start and end apart: 20, of which 8 were waited for; matrix products, arithmetic and copies ran while one was open for 49% of the time, Pallas kernels for 0%

commit v1 on v0

v1 whole, which is shorter than its diff:
```python
import functools

import jax
import jax.numpy as jnp
from jax import lax
from jax.experimental import pallas as pl
from jax.experimental.pallas import tpu as pltpu
from jax.sharding import PartitionSpec as P

HEAD_DIM = 64
PAIR = 2 * HEAD_DIM
QUAD = 4 * HEAD_DIM
EPSILON = 1e-06
LOW = jnp.bfloat16
F32 = jnp.float32
VMEM_LIMIT = 60 * 1024 * 1024
GELU_A = 0.7978845608028654
GELU_B = 0.044715


def dot(a, b):
    return lax.dot_general(a, b, (((1,), (0,)), ((), ())), preferred_element_type=F32)


def dot_nt(a, b):
    return lax.dot_general(a, b, (((1,), (1,)), ((), ())), preferred_element_type=F32)


def dot_tn(a, b):
    return lax.dot_general(a, b, (((0,), (0,)), ((), ())), preferred_element_type=F32)


def row_block(rows, most=512):
    for parts in range(1, rows + 1):
        if rows % parts == 0 and rows // parts <= most and (rows // parts) % 16 == 0:
            return rows // parts
    return rows


def loop_rows(total, size, body):
    @pl.loop(0, total // size)
    def _(step):
        body(pl.ds(pl.multiple_of(step * size, size), size))


def normalise(v):
    centered = v - jnp.mean(v, axis=-1, keepdims=True)
    spread = jnp.mean(centered * centered, axis=-1, keepdims=True)
    inverse = lax.rsqrt(spread + EPSILON)
    return centered * inverse, inverse


def norm_back(v, gain, grad):
    n, inverse = normalise(v)
    scaled = grad * gain
    back = scaled - jnp.mean(scaled, axis=-1, keepdims=True) - n * jnp.mean(scaled * n, axis=-1, keepdims=True)
    return back * inverse, jnp.sum(grad * n, axis=0, keepdims=True)


def half_masks(kind):
    lane = lax.broadcasted_iota(jnp.int32, (1, PAIR), 1)
    first = (lane < HEAD_DIM).astype(F32)
    return first.astype(kind), (1.0 - first).astype(kind)


def spread_pair(v):
    first, second = half_masks(v.dtype)
    return jnp.concatenate([v * first, v * second], axis=0)


def join_pair(v):
    tile = v.shape[0] // 2
    first, second = half_masks(v.dtype)
    return v[:tile] * first + v[tile:] * second


def attend_fwd(tile, x_ref, gain_ref, bias_ref, wq_ref, wk_ref, wv_ref, wo_ref,
               out_ref, n_ref, q_ref, k_ref, v_ref, p_ref, att_ref, acc_ref):
    step, steps = pl.program_id(0), pl.num_programs(0)
    rows = x_ref.shape[0]
    rb = row_block(rows)
    small = row_block(rows, 64)

    @pl.when(step == 0)
    def _():
        def body(at):
            x = x_ref[at, :].astype(F32)
            n_ref[at, :] = (normalise(x)[0] * gain_ref[...]).astype(LOW)
            acc_ref[at, :] = x
        loop_rows(rows, small, body)

    def project(at):
        n = n_ref[at, :]
        q_ref[at, :] = (dot(n, wq_ref[...]).astype(LOW) * (HEAD_DIM ** -0.5)).astype(LOW)
        k_ref[at, :] = dot(n, wk_ref[...]).astype(LOW)
        v_ref[at, :] = dot(n, wv_ref[...]).astype(LOW)
    loop_rows(rows, rb, project)

    @pl.loop(0, rows // tile)
    def _(t):
        at = pl.ds(pl.multiple_of(t * tile, tile), tile)
        for pair in range(2):
            cols = pl.ds(pair * PAIR, PAIR)
            qs = spread_pair(q_ref[at, cols])
            s = dot_nt(qs, k_ref[at, cols]) + bias_ref[...]
            e = jnp.exp(s - jnp.max(s, axis=-1, keepdims=True))
            p = (e * (1.0 / jnp.sum(e, axis=-1, keepdims=True))).astype(LOW)
            p_ref[0, pl.ds(pl.multiple_of((t * 2 + pair) * 2 * tile, 2 * tile), 2 * tile), :] = p
            att_ref[at, cols] = join_pair(dot(p, v_ref[at, cols])).astype(LOW)

    def project_out(at):
        acc_ref[at, :] += dot(att_ref[at, :], wo_ref[...])
    loop_rows(rows, rb, project_out)

    @pl.when(step == steps - 1)
    def _():
        out_ref[...] = acc_ref[...].astype(out_ref.dtype)


def attend_bwd(tile, prior, g_ref, x_ref, gain_ref, n_ref, q_ref, k_ref, v_ref, p_ref, att_ref,
               wq_ref, wk_ref, wv_ref, wo_ref, *rest):
    if prior:
        old_ref, oldo_ref, oldg_ref, gx_ref, dw_ref, dwo_ref, dgain_ref = rest[:7]
        rest = rest[7:]
    else:
        gx_ref, dw_ref, dwo_ref, dgain_ref = rest[:4]
        rest = rest[4:]
    low_ref, nt_ref, do_ref, dq_ref, dk_ref, dv_ref, acc_ref = rest
    step, steps = pl.program_id(0), pl.num_programs(0)
    rows, width = x_ref.shape
    rb = row_block(rows)
    small = row_block(rows, 64)

    @pl.when(step == 0)
    def _():
        low_ref[...] = g_ref[...].astype(LOW)
        nt_ref[...] = n_ref[...].T

    def back_out(at):
        do_ref[at, :] = dot_nt(low_ref[at, :], wo_ref[...]).astype(LOW)
    loop_rows(rows, rb, back_out)
    total = dot_tn(att_ref[...], low_ref[...])
    if prior:
        total += oldo_ref[...]
    dwo_ref[...] = total.astype(dwo_ref.dtype)

    @pl.loop(0, rows // tile)
    def _(t):
        at = pl.ds(pl.multiple_of(t * tile, tile), tile)
        for pair in range(2):
            cols = pl.ds(pair * PAIR, PAIR)
            dos = spread_pair(do_ref[at, cols])
            att = att_ref[at, cols].astype(F32)
            inner = jnp.sum(dos.astype(F32) * jnp.concatenate([att, att], axis=0), axis=-1, keepdims=True)
            p = p_ref[0, pl.ds(pl.multiple_of((t * 2 + pair) * 2 * tile, 2 * tile), 2 * tile), :]
            ds = (p.astype(F32) * (dot_nt(dos, v_ref[at, cols]) - inner)).astype(LOW)
            dq_ref[at, cols] = (join_pair(dot(ds, k_ref[at, cols])) * (HEAD_DIM ** -0.5)).astype(LOW)
            dk_ref[at, cols] = dot_tn(ds, spread_pair(q_ref[at, cols])).astype(LOW)
            dv_ref[at, cols] = dot_tn(p, dos).astype(LOW)

    def back_in(at):
        part = dot_nt(dq_ref[at, :], wq_ref[...]) + dot_nt(dk_ref[at, :], wk_ref[...]) + dot_nt(dv_ref[at, :], wv_ref[...])

        @pl.when(step == 0)
        def _():
            acc_ref[at, :] = part

        @pl.when(step != 0)
        def _():
            acc_ref[at, :] += part
    loop_rows(rows, rb, back_in)
    for at, grad_ref in enumerate((dq_ref, dk_ref, dv_ref)):
        total = dot(nt_ref[...], grad_ref[...])
        if prior:
            total += old_ref[at]
        dw_ref[at] = total.astype(dw_ref.dtype)

    @pl.when(step == steps - 1)
    def _():
        if prior:
            dgain_ref[...] = oldg_ref[...]
        else:
            dgain_ref[...] = jnp.zeros_like(dgain_ref)

        def body(at):
            back, gains = norm_back(x_ref[at, :].astype(F32), gain_ref[...], acc_ref[at, :])
            dgain_ref[...] += gains
            gx_ref[at, :] = (g_ref[at, :].astype(F32) + back).astype(gx_ref.dtype)
        loop_rows(rows, small, body)


def mlp_both(prior, second_ref, cot_ref, keep_ref, gain_ref, w1_ref, w2_ref, *rest):
    if prior:
        old1_ref, old2_ref, oldg_ref, out_ref, grad_ref, dw1_ref, dw2_ref, dgain_ref = rest[:8]
        rest = rest[8:]
    else:
        out_ref, grad_ref, dw1_ref, dw2_ref, dgain_ref = rest[:5]
        rest = rest[5:]
    n_ref, nt_ref, up_ref, sum_ref, acc_ref, act_ref, gh_ref = rest
    step, steps = pl.program_id(0), pl.num_programs(0)
    rows = second_ref.shape[0]
    rb = row_block(rows, 256)
    small = row_block(rows, 64)

    @pl.when(step == 0)
    def _():
        def body(at):
            v = second_ref[at, :]
            n_ref[at, :] = (normalise(v)[0] * gain_ref[...]).astype(LOW)
            up_ref[at, :] = (cot_ref[at, :].astype(F32) * keep_ref[at, :]).astype(LOW)
            sum_ref[at, :] = v
            acc_ref[at, :] = jnp.zeros_like(v)
        loop_rows(rows, small, body)
        nt_ref[...] = n_ref[...].T

    def body(at):
        h = dot(n_ref[at, :], w1_ref[...])
        ga = dot_nt(up_ref[at, :], w2_ref[...])
        square = h * h
        t = jnp.tanh(GELU_A * h * (1.0 + GELU_B * square))
        half = 0.5 + 0.5 * t
        act = (h * half).astype(LOW)
        slope = half + h * (0.5 - 0.5 * t * t) * (GELU_A + (3.0 * GELU_A * GELU_B) * square)
        gh = (ga * slope).astype(LOW)
        act_ref[at, :] = act
        gh_ref[at, :] = gh
        sum_ref[at, :] += dot(act, w2_ref[...])
        acc_ref[at, :] += dot_nt(gh, w1_ref[...])
    loop_rows(rows, rb, body)
    total = dot(nt_ref[...], gh_ref[...])
    if prior:
        total += old1_ref[...]
    dw1_ref[...] = total.astype(dw1_ref.dtype)
    total = dot_tn(act_ref[...], up_ref[...])
    if prior:
        total += old2_ref[...]
    dw2_ref[...] = total.astype(dw2_ref.dtype)

    @pl.when(step == steps - 1)
    def _():
        if prior:
            dgain_ref[...] = oldg_ref[...]
        else:
            dgain_ref[...] = jnp.zeros_like(dgain_ref)

        def last(at):
            out_ref[at, :] = (keep_ref[at, :] * sum_ref[at, :]).astype(LOW)
            back, gains = norm_back(second_ref[at, :], gain_ref[...], acc_ref[at, :])
            dgain_ref[...] += gains
            grad_ref[at, :] = up_ref[at, :].astype(F32) + back
        loop_rows(rows, small, last)


def whole(shape):
    return pl.BlockSpec(shape, lambda i: (0,) * len(shape), pipeline_mode=pl.Buffered(1))


def fixed(shape):
    return pl.BlockSpec(shape, lambda i: (0,) * len(shape))


def params():
    return pltpu.CompilerParams(dimension_semantics=("arbitrary",), vmem_limit_bytes=VMEM_LIMIT)


def spec_cols(shape, offset=0):
    return pl.BlockSpec(shape, lambda i, o=offset: (0, o + i))


def spec_rows(shape, offset=0):
    return pl.BlockSpec(shape, lambda i, o=offset: (o + i, 0))


def weight_specs(width, quads):
    return [spec_cols((width, QUAD), at * quads) for at in range(3)] + [spec_rows((QUAD, width))]


def run_attend_fwd(x, gain, bias, qkv, out_weight, tile, out_type):
    rows, width = x.shape
    quads = width // QUAD
    tiles = rows // tile
    probs_rows = tiles * 4 * tile
    low = jax.ShapeDtypeStruct((rows, width), LOW)
    cost = pl.CostEstimate(flops=2 * rows * width * (4 * width + 8 * tile), bytes_accessed=rows * width * 14 + 8 * width * width + 2 * rows * tile * (width // HEAD_DIM), transcendentals=rows * tile * (width // HEAD_DIM))
    return pl.pallas_call(
        functools.partial(attend_fwd, tile),
        grid=(quads,),
        in_specs=[whole((rows, width)), whole((1, width)), whole(bias.shape)] + weight_specs(width, quads),
        out_specs=[fixed((rows, width)), fixed((rows, width))] + [spec_cols((rows, QUAD))] * 3
        + [pl.BlockSpec((1, probs_rows, tile), lambda i: (i, 0, 0)), spec_cols((rows, QUAD))],
        out_shape=[jax.ShapeDtypeStruct((rows, width), out_type), low, low, low, low,
                   jax.ShapeDtypeStruct((quads, probs_rows, tile), LOW), low],
        scratch_shapes=[pltpu.VMEM((rows, width), F32)],
        compiler_params=params(),
        cost_estimate=cost,
    )(x, gain, bias, qkv, qkv, qkv, out_weight)


def run_attend_bwd(grad, x, gain, saved, qkv, out_weight, tile, out_type, old=None, weight_type=F32):
    n, q, k, v, probs, att = saved
    rows, width = x.shape
    quads = width // QUAD
    probs_rows = probs.shape[1]
    cost = pl.CostEstimate(flops=2 * rows * width * (8 * width + 20 * tile), bytes_accessed=rows * width * 20 + 24 * width * width + 2 * rows * tile * (width // HEAD_DIM), transcendentals=0)
    weight_out = [pl.BlockSpec((3, width, QUAD), lambda i: (0, 0, i)), spec_rows((QUAD, width)), fixed((1, width))]
    extra = [] if old is None else list(old)
    return pl.pallas_call(
        functools.partial(attend_bwd, tile, old is not None),
        grid=(quads,),
        in_specs=[whole((rows, width)), whole((rows, width)), whole((1, width)), whole((rows, width))]
        + [spec_cols((rows, QUAD))] * 3 + [pl.BlockSpec((1, probs_rows, tile), lambda i: (i, 0, 0)), spec_cols((rows, QUAD))]
        + weight_specs(width, quads) + (weight_out if extra else []),
        out_specs=[fixed((rows, width))] + weight_out,
        out_shape=[jax.ShapeDtypeStruct((rows, width), out_type), jax.ShapeDtypeStruct((3, width, width), weight_type),
                   jax.ShapeDtypeStruct((width, width), weight_type), jax.ShapeDtypeStruct((1, width), F32)],
        scratch_shapes=[pltpu.VMEM((rows, width), LOW), pltpu.VMEM((width, rows), LOW)]
        + [pltpu.VMEM((rows, QUAD), LOW)] * 4 + [pltpu.VMEM((rows, width), F32)],
        compiler_params=params(),
        cost_estimate=cost,
    )(grad, x, gain, n, q, k, v, probs, att, qkv, qkv, qkv, out_weight, *extra)


FF_TILE = 512


def run_mlp(second, cot, keep, gain, w1, w2, old=None, weight_type=F32):
    rows, width = second.shape
    hidden = w1.shape[1]
    steps = hidden // FF_TILE
    cost = pl.CostEstimate(flops=12 * rows * width * hidden, bytes_accessed=rows * width * 14 + 12 * width * hidden, transcendentals=rows * hidden)
    weight_out = [spec_cols((width, FF_TILE)), spec_rows((FF_TILE, width)), fixed((1, width))]
    extra = [] if old is None else list(old)
    return pl.pallas_call(
        functools.partial(mlp_both, old is not None),
        grid=(steps,),
        in_specs=[whole((rows, width)), whole((rows, width)), whole((rows, 1)), whole((1, width)),
                  spec_cols((width, FF_TILE)), spec_rows((FF_TILE, width))] + (weight_out if extra else []),
        out_specs=[fixed((rows, width)), fixed((rows, width))] + weight_out,
        out_shape=[jax.ShapeDtypeStruct((rows, width), LOW), jax.ShapeDtypeStruct((rows, width), F32),
                   jax.ShapeDtypeStruct((width, hidden), weight_type), jax.ShapeDtypeStruct((hidden, width), weight_type),
                   jax.ShapeDtypeStruct((1, width), F32)],
        scratch_shapes=[pltpu.VMEM((rows, width), LOW), pltpu.VMEM((width, rows), LOW), pltpu.VMEM((rows, width), LOW),
                        pltpu.VMEM((rows, width), F32), pltpu.VMEM((rows, width), F32),
                        pltpu.VMEM((rows, FF_TILE), LOW), pltpu.VMEM((rows, FF_TILE), LOW)],
        compiler_params=params(),
        cost_estimate=cost,
    )(second, cot, keep, gain, w1, w2, *extra)


GROUP = 8


def to_blocks(v):
    frames, places, width = v.shape
    groups = -(-places // GROUP)
    v = jnp.pad(v, ((0, 0), (0, groups * GROUP - places), (0, 0)))
    return v.reshape(frames, groups, GROUP, width).transpose(1, 0, 2, 3).reshape(groups * frames * GROUP, width)


def from_blocks(v, frames, places):
    width = v.shape[-1]
    v = v.reshape(-1, frames, GROUP, width).transpose(1, 0, 2, 3).reshape(frames, -1, width)
    return v[:, :places]


def to_places(v, parts):
    clips, frames, slots, width = v.shape
    v = v.transpose(1, 0, 2, 3).reshape(frames, parts, clips * slots // parts, width).transpose(1, 0, 2, 3)
    v = lax.all_to_all(v, "seq", split_axis=0, concat_axis=0, tiled=True)
    return v.reshape(parts * frames, clips * slots // parts, width)


def to_frames(v, parts, clips):
    frames, places, width = v.shape
    v = v.reshape(parts, frames // parts, places, width)
    v = lax.all_to_all(v, "seq", split_axis=0, concat_axis=0, tiled=True)
    return v.transpose(1, 0, 2, 3).reshape(frames // parts, clips, parts * places // clips, width).transpose(1, 0, 2, 3)


def shards(parts, frames_in, qkv_spatial, out_spatial, qkv_temporal, out_temporal, mlp_in, mlp_out, gains, place_mask, cotangent):
    both = ("dp", "seq")
    micros, clips, local_frames, slots, width = frames_in.shape
    frames = local_frames * parts
    places = clips * slots // parts
    here = clips * local_frames * slots

    def gather(w):
        return lax.all_gather(w, both, axis=0, tiled=True)

    space_qkv, space_out = gather(qkv_spatial), gather(out_spatial)
    gain_rows = gather(gains).astype(F32).T
    time_qkv, time_out = gather(qkv_temporal), gather(out_temporal)
    grow, shrink = gather(mlp_in), gather(mlp_out)
    gain_space, gain_time, gain_mlp = gain_rows[0:1], gain_rows[1:2], gain_rows[2:3]

    bias_space = jnp.where(place_mask > 0, 0.0, -1000000000.0).astype(F32)[None, :]
    tile_time = frames * GROUP
    spot = jnp.arange(tile_time) % GROUP
    bias_time = jnp.where(spot[:, None] == spot[None, :], 0.0, -1000000000.0).astype(F32)
    bias_time = jnp.concatenate([bias_time, bias_time], axis=0)
    keep = jnp.tile(place_mask.astype(F32), clips)
    keep = lax.dynamic_slice_in_dim(keep, lax.axis_index("seq") * places, places)
    keep = to_blocks(jnp.broadcast_to(keep[None, :, None], (frames, places, 1)))

    spatial, temporal = [], []
    cots = [to_blocks(to_places(cotangent[m], parts)) for m in range(micros)]
    for m in range(micros):
        x = frames_in[m].reshape(here, width)
        out, *saved = run_attend_fwd(x, gain_space, bias_space, space_qkv, space_out, slots, LOW)
        across = to_blocks(to_places(out.reshape(clips, local_frames, slots, width), parts))
        spatial.append((x, saved, across))
    outputs, afters = [], []
    old_mlp = old_time = None
    for m in range(micros):
        last = LOW if m == micros - 1 else F32
        across = spatial[m][2]
        second, *saved = run_attend_fwd(across, gain_time, bias_time, time_qkv, time_out, tile_time, F32)
        out, grad, *old_mlp = run_mlp(second, cots[m], keep, gain_mlp, grow, shrink, old_mlp, last)
        outputs.append(to_frames(from_blocks(out, frames, places), parts, clips))
        after, *old_time = run_attend_bwd(grad, across, gain_time, saved, time_qkv, time_out, tile_time, LOW, old_time, last)
        afters.append(to_frames(from_blocks(after, frames, places), parts, clips))
    input_grads = []
    old_space = None
    for m in range(micros):
        last = LOW if m == micros - 1 else F32
        x, saved, _ = spatial[m]
        grad, *old_space = run_attend_bwd(afters[m].reshape(here, width), x, gain_space, saved, space_qkv, space_out, slots, F32, old_space, last)
        input_grads.append(grad.reshape(clips, local_frames, slots, width))

    def scatter(w, axis=0):
        return lax.psum_scatter(w, both, scatter_dimension=axis, tiled=True)

    def scatter_qkv(w):
        return scatter(w, 1).transpose(1, 0, 2).reshape(-1, 3 * width).astype(F32)

    gain_sum = lax.psum_scatter(jnp.concatenate([old_space[2], old_time[2], old_mlp[2]], axis=0).T, both, scatter_dimension=0, tiled=True)
    return (
        jnp.stack(outputs),
        jnp.stack(input_grads),
        scatter_qkv(old_space[0]),
        scatter(old_space[1]).astype(F32),
        scatter_qkv(old_time[0]),
        scatter(old_time[1]).astype(F32),
        scatter(old_mlp[0]).astype(F32),
        scatter(old_mlp[1]).astype(F32),
        gain_sum,
    )


def solution(mesh):
    rows = P(("dp", "seq"), None)
    tokens = P(None, "dp", "seq", None, None)
    return jax.shard_map(
        functools.partial(shards, mesh.shape["seq"]),
        mesh=mesh,
        in_specs=(tokens,) + (rows,) * 7 + (P(), tokens),
        out_specs=(tokens, tokens) + (rows,) * 7,
        check_vma=False,
    )
```

time: 1930 us -> 1600 us (0.83)
  matrix products: 727 us -> 0 us
  Pallas kernels: 0 us -> 665 us
  local copies, waits for them, and re-layouts: 320 us -> 79.6 us
  other arithmetic: 235 us -> 17.1 us
  waiting for transfers between devices: 475 us -> 617 us
  blocking collectives: 108 us -> 157 us
    dot_general x60 -> x0, matrix products: 727 us -> none  [the longest x4 66.5 us: attend_backward(): jnp.einsum('cqphe,ckphe->cphqk', grad_result, value_rows, preferred_eleme...]
    pallas_call x0 -> x10, Pallas kernels: none -> 665 us  [the longest x4 269 us: run_attend_bwd(): pl.pallas_call(functools.partial(attend_bwd, tile, old is not None), grid...]
    convert_element_type x30 -> x2, local copies, waits for them, and re-layouts: 186 us -> 1.4 us  [scatter_qkv(): return scatter(w, 1).transpose(1, 0, 2).reshape(-1, 3 * width).astype(F32)]
    convert_element_type x16 -> x5, other arithmetic: 120 us -> 6.1 us  [the longest x1 1.64 us: shards(): scatter(old_mlp[0]).astype(F32)]
    unnamed x12 -> x14, waiting for transfers between devices: 3.56 us -> 111 us
    all_gather x6, waiting for transfers between devices: 0.07 us -> 97.8 us  [gather(): return lax.all_gather(w, both, axis=0, tiled=True)]
    reduce_sum x17 -> x0, other arithmetic: 91.1 us -> none  [the longest x4 38.2 us: attend_forward(): denominator = jnp.sum(exponent, axis=-1, keepdims=True)]
    reshape x6, local copies, waits for them, and re-layouts: 73.2 us -> 15.6 us  [the longest x4 11.8 us: from_blocks(): v.reshape(-1, frames, GROUP, width).transpose(1, 0, 2, 3)]
  transfers between devices with their start and end apart: 20 -> 20, of which waited for: 8 -> 10; matrix products, arithmetic and copies ran while one was open for 49% -> 6% of each run, Pallas kernels for 0% -> 42%
where the time goes in v1:
time: 1600 us; the launch traced here: 1590 us
  Pallas kernels  665 us (42%)
  waiting for transfers between devices  617 us (39%)
  blocking collectives  157 us (10%)
  local copies, waits for them, and re-layouts  79.6 us (5%)
  starting transfers between devices  36.4 us (2%)
  other arithmetic  17.1 us (1%)
    pallas_call x4, Pallas kernels, run_attend_bwd(): pl.pallas_call(functools.partial(attend_bwd, tile, old is not None), grid...  269 us
    pallas_call x4, Pallas kernels, run_attend_fwd(): pl.pallas_call(functools.partial(attend_fwd, tile), grid=(quads,), in_spe...  212 us
    reduce_scatter x4, waiting for transfers between devices, scatter(): return lax.psum_scatter(w, both, scatter_dimension=axis, tiled=True)  189 us
    pallas_call x2, Pallas kernels, run_mlp(): pl.pallas_call(functools.partial(mlp_both, old is not None), grid=(steps,...  184 us
    all_to_all x4, waiting for transfers between devices, to_frames(): v = lax.all_to_all(v, 'seq', split_axis=0, concat_axis=0, tiled=True)  154 us
    all_gather x1, blocking collectives, gather(): return lax.all_gather(w, both, axis=0, tiled=True)  120 us
    unnamed x14, waiting for transfers between devices  111 us
    all_gather x6, waiting for transfers between devices, gather(): return lax.all_gather(w, both, axis=0, tiled=True)  97.8 us
  transfers between devices with their start and end apart: 20, of which 10 were waited for; matrix products, arithmetic and copies ran while one was open for 6% of the time, Pallas kernels for 42%

profile of v1, /device:TPU:0, one launch (start us, length us, event | category | flops | bytes accessed | tf_op | source)
XLA Modules:
  0.0 1587.7 jit_solution(8596920386516645047)
XLA Ops:
  15.2 6.3 all-to-all-start.1
  23.9 57.8 %all-to-all-done.1 = bf16[4,4,104,768]{3,2,1,0:T(8,128)(2,1)} async-done(((bf16[4,4,104,768]{3,2,1,0:T(8,128)(2,1)}), bf16[4,4,104,768]{3,2,1,0:T(8,128)(2,1)}, u32[]{:S(2)}, u32[]{:S(2)}) %all-to-all-start.1) | async-done | bytes 2555936 | tf_op jit(solution)/shard_map/all_to_all | solution.py:369
  85.3 120.1 %all-gather = bf16[32,24,3]{1,2,0:T(4,128)(2,1)S(1)} all-gather(bf16[1,24,3]{1,2,0:T(4,128)(2,1)S(1)} %bitcast.154), channel_id=1, replica_groups=mesh['dp'=8,'seq'=4] {'dp','seq'}, dimensions={0}, use_global_device_ids=true | all-gather | bytes 4752 | tf_op jit(solution)/shard_map/all_gather | solution.py:388
  206.8 5.1 fusion.1
  211.9 50.2 %shard_map.169 = (bf16[1664,768]{1,0:T(8,128)(2,1)}, bf16[1664,768]{1,0:T(8,128)(2,1)}, bf16[1664,768]{1,0:T(8,128)(2,1)}, bf16[1664,768]{1,0:T(8,128)(2,1)}, bf...) custom-call(bf16[1664,768]{1,0:T(8,128)(2,1)} %bitcast.133, ...), custom_call_target="tpu_custom_call" | custom-call | flops 12104761344 | bytes 30916608 | tf_op jit(solution)/shard_map/pallas_call | solution.py:285
  265.6 4.5 all-to-all-start
  277.5 50.1 %shard_map.172 = (bf16[1664,768]{1,0:T(8,128)(2,1)}, bf16[1664,768]{1,0:T(8,128)(2,1)}, bf16[1664,768]{1,0:T(8,128)(2,1)}, bf16[1664,768]{1,0:T(8,128)(2,1)}, bf...) custom-call(bf16[1664,768]{1,0:T(8,128)(2,1)} %bitcast.131, ...), custom_call_target="tpu_custom_call" | custom-call | flops 12104761344 | bytes 30916608 | tf_op jit(solution)/shard_map/pallas_call | solution.py:285
  331.2 7.0 all-to-all-done
  338.2 3.8 all-to-all-start.3
  345.4 56.0 %shard_map.170 = (f32[1664,768]{1,0:T(8,128)}, bf16[1664,768]{1,0:T(8,128)(2,1)}, bf16[1664,768]{1,0:T(8,128)(2,1)}, bf16[1664,768]{1,0:T(8,128)(2,1)}, bf16[166...) custom-call(bf16[1664,768]{1,0:T(8,128)(2,1)} %bitcast.141, ...), custom_call_target="tpu_custom_call" | custom-call | flops 10468982784 | bytes 27721728 | tf_op jit(solution)/shard_map/pallas_call | solution.py:285
  401.4 32.7 %all-gather.16.cloned.1.call-done.w1_ref = bf16[768,3072]{1,0:T(8,128)(2,1)} async-done(((bf16[24,3072]{1,0:T(8,128)(2,1)}), bf16[768,3072]{1,0:T(8,128)(2,1)}) %all-gather.16.cloned.1.call-update) | async-done | bytes 4718608 | tf_op jit(solution)/shard_map/all_gather | solution.py:388
  434.1 65.1 %all-gather.18.cloned.1.call-done.w2_ref = bf16[3072,768]{1,0:T(8,128)(2,1)} async-done(((bf16[96,768]{1,0:T(8,128)(2,1)}), bf16[3072,768]{1,0:T(8,128)(2,1)}) %all-gather.18.cloned.1.call-update) | async-done | bytes 4718608 | tf_op jit(solution)/shard_map/all_gather | solution.py:388
  499.2 91.9 %shard_map.171 = (bf16[1664,768]{1,0:T(8,128)(2,1)}, f32[1664,768]{1,0:T(8,128)}, f32[768,3072]{1,0:T(8,128)}, f32[3072,768]{1,0:T(8,128)}, f32[1,768]{1,0:T(1,128)}) custom-call(f32[1664,768]{1,0:T(8,128)} %get-tuple-element.64.second_ref, bf16[1664,768]{1,0:T(8,128)(2,1)} %bitcast.138, f32[1664,1]{1,0:T(8,128)} %transpose.140.keep_ref, ...), custom_call_target="tpu_custom_call" | custom-call | flops 47110422528 | bytes 46202880 | tf_op jit(solution)/shard_map/pallas_call | solution.py:333
  591.1 67.0 %shard_map.175 = (bf16[1664,768]{1,0:T(8,128)(2,1)}, f32[3,768,768]{2,1,0:T(8,128)}, f32[768,768]{1,0:T(8,128)}, f32[1,768]{1,0:T(1,128)}) custom-call(f32[1664,768]{1,0:T(8,128)} %get-tuple-element.72.g_ref, bf16[1664,768]{1,0:T(8,128)(2,1)} %bitcast.142, f32[1,768]{1,0:T(1,128)} %get-tuple-element.149.gain_ref, bf16[1664,768]{1,0:T(8,128)(2,1)} %get-tuple-element.73.n_ref, ...), custom_call_target="tpu_custom_call" | custom-call | flops 22246588416 | bytes 44826624 | tf_op jit(solution)/shard_map/pallas_call | solution.py:307
  663.0 4.1 all-to-all-start.6
  670.5 56.0 %shard_map.173 = (f32[1664,768]{1,0:T(8,128)}, bf16[1664,768]{1,0:T(8,128)(2,1)}, bf16[1664,768]{1,0:T(8,128)(2,1)}, bf16[1664,768]{1,0:T(8,128)(2,1)}, bf16[166...) custom-call(bf16[1664,768]{1,0:T(8,128)(2,1)} %bitcast.139, ...), custom_call_target="tpu_custom_call" | custom-call | flops 10468982784 | bytes 27721728 | tf_op jit(solution)/shard_map/pallas_call | solution.py:285
  726.6 92.5 %shard_map.174 = (bf16[1664,768]{1,0:T(8,128)(2,1)}, f32[1664,768]{1,0:T(8,128)}, bf16[768,3072]{1,0:T(8,128)(2,1)}, bf16[3072,768]{1,0:T(8,128)(2,1)}, f32[1,768]{1,0:T(1,128)}) custom-call(f32[1664,768]{1,0:T(8,128)} %get-tuple-element.67.second_ref, bf16[1664,768]{1,0:T(8,128)(2,1)} %bitcast.137, f32[1664,1]{1,0:T(8,128)} %transpose.140.keep_ref, ...), custom_call_target="tpu_custom_call" | custom-call | flops 47110422528 | bytes 46202880 | tf_op jit(solution)/shard_map/pallas_call | solution.py:333
  819.1 68.1 %shard_map.177 = (bf16[1664,768]{1,0:T(8,128)(2,1)}, bf16[3,768,768]{2,1,0:T(8,128)(2,1)}, bf16[768,768]{1,0:T(8,128)(2,1)}, f32[1,768]{1,0:T(1,128)}) custom-call(f32[1664,768]{1,0:T(8,128)} %get-tuple-element.87.g_ref, bf16[1664,768]{1,0:T(8,128)(2,1)} %bitcast.140, f32[1,768]{1,0:T(1,128)} %get-tuple-element.149.gain_ref, ...), custom_call_target="tpu_custom_call" | custom-call | flops 22246588416 | bytes 44826624 | tf_op jit(solution)/shard_map/pallas_call | solution.py:307
  890.6 5.1 all-to-all-start.7
  896.5 5.0 copy.107
  906.1 49.0 %all-to-all-done.7 = bf16[4,4,104,768]{3,2,1,0:T(8,128)(2,1)} async-done(((bf16[4,4,104,768]{3,2,1,0:T(8,128)(2,1)}), bf16[4,4,104,768]{3,2,1,0:T(8,128)(2,1)}, u32[]{:S(2)}, u32[]{:S(2)}) %all-to-all-start.7) | async-done | bytes 2555936 | tf_op jit(solution)/shard_map/all_to_all | solution.py:376
  958.7 65.9 %shard_map.176 = (f32[1664,768]{1,0:T(8,128)}, f32[3,768,768]{2,1,0:T(8,128)}, f32[768,768]{1,0:T(8,128)}, f32[1,768]{1,0:T(1,128)}) custom-call(bf16[1664,768]{1,0:T(8,128)(2,1)} %bitcast.144, bf16[1664,768]{1,0:T(8,128)(2,1)} %bitcast.134, f32[1,768]{1,0:T(1,128)} %get-tuple-element.150.gain_ref, bf16[1664,768]{1,0:T(8,128)(2,1)} %get-tuple-element.80.n_ref, ...), custom_call_target="tpu_custom_call" | custom-call | flops 26336034816 | bytes 48021504 | tf_op jit(solution)/shard_map/pallas_call | solution.py:307
  1024.5 67.5 %shard_map.178 = (f32[1664,768]{1,0:T(8,128)}, bf16[3,768,768]{2,1,0:T(8,128)(2,1)}, bf16[768,768]{1,0:T(8,128)(2,1)}, f32[1,768]{1,0:T(1,128)}) custom-call(bf16[1664,768]{1,0:T(8,128)(2,1)} %bitcast.143, bf16[1664,768]{1,0:T(8,128)(2,1)} %bitcast.132, f32[1,768]{1,0:T(1,128)} %get-tuple-element.150.gain_ref, bf16[1664,768]{1,0:T(8,128)(2,1)} %get-tuple-element.98.n_ref, ...), custom_call_target="tpu_custom_call" | custom-call | flops 26336034816 | bytes 48021504 | tf_op jit(solution)/shard_map/pallas_call | solution.py:307
  1103.0 54.1 %all-to-all-done.5 = bf16[4,4,104,768]{3,2,1,0:T(8,128)(2,1)S(1)} async-done(((bf16[4,4,104,768]{3,2,1,0:T(8,128)(2,1)}), bf16[4,4,104,768]{3,2,1,0:T(8,128)(2,1)S(1)}, u32[]{:S(2)}, u32[]{:S(2)}) %all-to-all-start.5) | async-done | bytes 2555936 | tf_op jit(solution)/shard_map/all_to_all | solution.py:376
  1158.6 4.5 all-to-all-start.2
  1163.4 5.0 copy.105
  1174.4 50.8 %all-to-all-done.2 = bf16[4,4,104,768]{3,2,1,0:T(8,128)(2,1)} async-done(((bf16[4,4,104,768]{3,2,1,0:T(8,128)(2,1)}), bf16[4,4,104,768]{3,2,1,0:T(8,128)(2,1)}, u32[]{:S(2)}, u32[]{:S(2)}) %all-to-all-start.2) | async-done | bytes 2555936 | tf_op jit(solution)/shard_map/all_to_all | solution.py:376
  1230.4 37.4 %all-reduce = f32[768,3]{0,1:T(4,128)S(1)} all-reduce(f32[768,3]{0,1:T(4,128)S(1)} %maximum_bitcast_fusion), channel_id=8, replica_groups=mesh['dp'=8,'seq'=4] {'dp','seq'}, use_global_device_ids=true, to_apply=%region_6.7.clone | all-reduce | flops 2304 | bytes 18432
  1268.5 9.1 pad_maximum_fusion
  1280.7 78.5 %reduce-scatter.16.cloned.1.call-done = bf16[24,3072]{1,0:T(8,128)(2,1)} async-done(((bf16[768,3072]{1,0:T(8,128)(2,1)}), bf16[24,3072]{1,0:T(8,128)(2,1)}) %reduce-scatter.16.cloned.1.call-update) | async-done | bytes 147472 | tf_op jit(solution)/shard_map/reduce_scatter | solution.py:431
  1360.8 110.9 %reduce-scatter.18.cloned.1.call-done = bf16[96,768]{1,0:T(8,128)(2,1)} async-done(((bf16[3072,768]{1,0:T(8,128)(2,1)}), bf16[96,768]{1,0:T(8,128)(2,1)}) %reduce-scatter.18.cloned.1.call-update) | async-done | bytes 147472 | tf_op jit(solution)/shard_map/reduce_scatter | solution.py:431
  1473.3 105.7 %reduce-scatter.20.cloned.1.call-done = bf16[24,2304]{1,0:T(8,128)(2,1)} async-done(((bf16[768,2304]{1,0:T(8,128)(2,1)}), bf16[24,2304]{1,0:T(8,128)(2,1)}) %reduce-scatter.20.cloned.1.call-update) | async-done | bytes 110608
  (106 shorter events, 86.2 us)
Async XLA Ops:
  7.2 204.7 %all-gather.10.cloned.1.call-start = ((), (), s32[]{:S(2)}) async-start(), calls=%async_computation.15 | async-start | bytes 1216512 | tf_op jit(solution)/shard_map/all_gather | solution.py:388
  7.9 204.0 %all-gather.8.cloned.1.call-start = ((), (), s32[]{:S(2)}) async-start(), calls=%async_computation.14 | async-start | bytes 3649536 | tf_op jit(solution)/shard_map/all_gather | solution.py:388
  8.7 336.8 %all-gather.14.cloned.1.call-start = ((), (), s32[]{:S(2)}) async-start(), calls=%async_computation.17 | async-start | bytes 1216512 | tf_op jit(solution)/shard_map/all_gather | solution.py:388
  9.4 336.0 %all-gather.12.cloned.1.call-start = ((), (), s32[]{:S(2)}) async-start(), calls=%async_computation.16 | async-start | bytes 3649536 | tf_op jit(solution)/shard_map/all_gather | solution.py:388
  10.0 424.1 %all-gather.16.cloned.1.call-start = ((), (), s32[]{:S(2)}) async-start(), calls=%async_computation.18 | async-start | bytes 4866048 | tf_op jit(solution)/shard_map/all_gather | solution.py:388
  15.2 66.5 %all-to-all-start.1 = ((bf16[4,4,104,768]{3,2,1,0:T(8,128)(2,1)}), bf16[4,4,104,768]{3,2,1,0:T(8,128)(2,1)}, u32[]{:S(2)}, u32[]{:S(2)}) async-start(bf16[4,4,104,768]{3,2,1,0:T(8,128)(2,1)} %copy.82), calls=%async_computation.1 | async-start | bytes 5111808 | tf_op jit(solution)/shard_map/all_to_all | solution.py:369
  21.5 477.7 %all-gather.18.cloned.1.call-start = ((), (), s32[]{:S(2)}) async-start(), calls=%async_computation.19 | async-start | bytes 4866048 | tf_op jit(solution)/shard_map/all_gather | solution.py:388
  23.9 61.4 %copy-start.7 = (bf16[24,3]{0,1:T(4,128)(2,1)S(1)}, bf16[24,3]{0,1:T(4,128)(2,1)}, u32[]{:S(2)}) copy-start(bf16[24,3]{0,1:T(4,128)(2,1)} %param.17) | copy-start | bytes 436
  23.9 181.8 %copy-start.3 = (s32[208]{0:T(256)S(1)}, s32[208]{0:T(256)}, u32[]{:S(2)}) copy-start(s32[208]{0:T(256)} %param.18) | copy-start | bytes 2500
  81.6 184.0 %all-to-all-start.4 = ((bf16[4,4,104,768]{3,2,1,0:T(8,128)(2,1)}), bf16[4,4,104,768]{3,2,1,0:T(8,128)(2,1)S(1)}, u32[]{:S(2)}, u32[]{:S(2)}) async-start(bf16[4,4,104,768]{3,2,1,0:T(8,128)(2,1)} %copy.91), calls=%async_computation.4 | async-start | bytes 5111808 | tf_op jit(solution)/shard_map/all_to_all | solution.py:369
  265.6 72.6 %all-to-all-start = ((bf16[4,4,104,768]{3,2,1,0:T(8,128)(2,1)}), bf16[4,4,104,768]{3,2,1,0:T(8,128)(2,1)}, u32[]{:S(2)}, u32[]{:S(2)}) async-start(bf16[4,4,104,768]{3,2,1,0:T(8,128)(2,1)} %copy.79), calls=%async_computation | async-start | bytes 5111808 | tf_op jit(solution)/shard_map/all_to_all | solution.py:369
  338.2 323.4 %all-to-all-start.3 = ((bf16[4,4,104,768]{3,2,1,0:T(8,128)(2,1)}), bf16[4,4,104,768]{3,2,1,0:T(8,128)(2,1)S(1)}, u32[]{:S(2)}, u32[]{:S(2)}) async-start(bf16[4,4,104,768]{3,2,1,0:T(8,128)(2,1)} %copy.88), calls=%async_computation.3 | async-start | bytes 5111808 | tf_op jit(solution)/shard_map/all_to_all | solution.py:369
  661.5 1.5 copy-start
  663.0 227.6 %all-to-all-start.6 = ((bf16[4,4,104,768]{3,2,1,0:T(8,128)(2,1)}), bf16[4,4,104,768]{3,2,1,0:T(8,128)(2,1)S(1)}, u32[]{:S(2)}, u32[]{:S(2)}) async-start(bf16[4,4,104,768]{3,2,1,0:T(8,128)(2,1)} %bitcast.118), calls=%async_computation.6 | async-start | bytes 5111808 | tf_op jit(solution)/shard_map/all_to_all | solution.py:376
  890.6 64.5 %all-to-all-start.7 = ((bf16[4,4,104,768]{3,2,1,0:T(8,128)(2,1)}), bf16[4,4,104,768]{3,2,1,0:T(8,128)(2,1)}, u32[]{:S(2)}, u32[]{:S(2)}) async-start(bf16[4,4,104,768]{3,2,1,0:T(8,128)(2,1)} %bitcast.121), calls=%async_computation.7 | async-start | bytes 5111808 | tf_op jit(solution)/shard_map/all_to_all | solution.py:376
  895.7 275.4 %reduce-scatter.14.cloned.1.call-start = ((), (), s32[]{:S(2)}) async-start(), calls=%async_computation.21 | async-start | bytes 1216512 | tf_op jit(solution)/shard_map/reduce_scatter | solution.py:431
  896.4 381.2 %reduce-scatter.22.cloned.1.call-start = ((), (), s32[]{:S(2)}) async-start(), calls=%async_computation.25 | async-start | bytes 3649536
  904.1 375.2 %reduce-scatter.12.cloned.1.call-start = ((), (), s32[]{:S(2)}) async-start(), calls=%async_computation.20 | async-start | bytes 1216512 | tf_op jit(solution)/shard_map/reduce_scatter | solution.py:431
  1092.0 267.1 %reduce-scatter.16.cloned.1.call-start = ((), (), s32[]{:S(2)}) async-start(), calls=%async_computation.22 | async-start | bytes 4866048 | tf_op jit(solution)/shard_map/reduce_scatter | solution.py:431
  1092.6 1.7 copy-start.2
  1092.7 379.0 %reduce-scatter.18.cloned.1.call-start = ((), (), s32[]{:S(2)}) async-start(), calls=%async_computation.23 | async-start | bytes 4866048 | tf_op jit(solution)/shard_map/reduce_scatter | solution.py:431
  1096.0 61.1 %all-to-all-start.5 = ((bf16[4,4,104,768]{3,2,1,0:T(8,128)(2,1)}), bf16[4,4,104,768]{3,2,1,0:T(8,128)(2,1)S(1)}, u32[]{:S(2)}, u32[]{:S(2)}) async-start(bf16[4,4,104,768]{3,2,1,0:T(8,128)(2,1)} %bitcast.122), calls=%async_computation.5 | async-start | bytes 5111808 | tf_op jit(solution)/shard_map/all_to_all | solution.py:376
  1157.1 1.5 copy-start.1
  1158.6 66.7 %all-to-all-start.2 = ((bf16[4,4,104,768]{3,2,1,0:T(8,128)(2,1)}), bf16[4,4,104,768]{3,2,1,0:T(8,128)(2,1)}, u32[]{:S(2)}, u32[]{:S(2)}) async-start(bf16[4,4,104,768]{3,2,1,0:T(8,128)(2,1)} %bitcast.120), calls=%async_computation.2 | async-start | bytes 5111808 | tf_op jit(solution)/shard_map/all_to_all | solution.py:376
  1163.2 415.8 %reduce-scatter.20.cloned.1.call-start = ((), (), s32[]{:S(2)}) async-start(), calls=%async_computation.24 | async-start | bytes 3649536
  1227.7 2.7 copy-start.4
  1227.7 2.7 copy-start.5
  1227.7 2.7 copy-start.6
Sparse Core Ops, SparseCore 0:
  10.8 97.8 all-gather.9
  111.6 77.0 all-gather.7
  191.4 53.0 all-gather.13
  247.2 91.3 all-gather.11
  341.2 92.8 all-gather.15
  436.8 62.3 all-gather.17
  901.6 96.6 reduce-scatter.13
  1003.7 112.9 reduce-scatter.21
  1121.8 125.8 reduce-scatter.11
  1253.1 106.0 reduce-scatter.15
  1365.6 106.0 reduce-scatter.17
  1477.0 101.9 reduce-scatter.19

commit v2 on v1

v2 whole, which is shorter than its diff:
```python
import functools

import jax
import jax.numpy as jnp
from jax import lax
from jax.experimental import pallas as pl
from jax.experimental.pallas import tpu as pltpu
from jax.sharding import PartitionSpec as P

HEAD_DIM = 64
PAIR = 2 * HEAD_DIM
QUAD = 4 * HEAD_DIM
EPSILON = 1e-06
LOW = jnp.bfloat16
F32 = jnp.float32
VMEM_LIMIT = 60 * 1024 * 1024
COST_SHARE = 10
GELU_A = 0.7978845608028654
GELU_B = 0.044715


def dot(a, b):
    return lax.dot_general(a, b, (((1,), (0,)), ((), ())), preferred_element_type=F32)


def dot_nt(a, b):
    return lax.dot_general(a, b, (((1,), (1,)), ((), ())), preferred_element_type=F32)


def dot_tn(a, b):
    return lax.dot_general(a, b, (((0,), (0,)), ((), ())), preferred_element_type=F32)


def row_block(rows, most=512):
    for parts in range(1, rows + 1):
        if rows % parts == 0 and rows // parts <= most and (rows // parts) % 16 == 0:
            return rows // parts
    return rows


def loop_rows(total, size, body):
    @pl.loop(0, total // size)
    def _(step):
        body(pl.ds(pl.multiple_of(step * size, size), size))


def normalise(v):
    centered = v - jnp.mean(v, axis=-1, keepdims=True)
    spread = jnp.mean(centered * centered, axis=-1, keepdims=True)
    inverse = lax.rsqrt(spread + EPSILON)
    return centered * inverse, inverse


def norm_back(v, gain, grad):
    n, inverse = normalise(v)
    scaled = grad * gain
    back = scaled - jnp.mean(scaled, axis=-1, keepdims=True) - n * jnp.mean(scaled * n, axis=-1, keepdims=True)
    return back * inverse, jnp.sum(grad * n, axis=0, keepdims=True)


def gain_row(gains_ref, column):
    return gains_ref[...].astype(F32).T[column:column + 1]


def half_masks(kind):
    lane = lax.broadcasted_iota(jnp.int32, (1, PAIR), 1)
    first = (lane < HEAD_DIM).astype(F32)
    return first.astype(kind), (1.0 - first).astype(kind)


def spread_pair(v):
    first, second = half_masks(v.dtype)
    return jnp.concatenate([v * first, v * second], axis=0)


def join_pair(v):
    tile = v.shape[0] // 2
    first, second = half_masks(v.dtype)
    return v[:tile] * first + v[tile:] * second


def store_pieces(me, pieces, source_ref, plan):
    for at, piece_ref in enumerate(pieces):
        starts = plan.starts(lax.bitwise_xor(me, at))

        @pl.loop(0, plan.groups)
        def _(group):
            for low in range(0, plan.frames, plan.joint):
                rows = [source_ref[pl.ds(pl.multiple_of(starts[low + more] + group * plan.group, plan.group), plan.group), :] for more in range(plan.joint)]
                piece_ref[group, pl.ds(low * plan.group, 16), :] = jnp.concatenate(rows, axis=0).astype(piece_ref.dtype)


def load_pieces(me, pieces, target_ref, plan):
    for at, piece_ref in enumerate(pieces):
        starts = plan.starts(lax.bitwise_xor(me, at))

        @pl.loop(0, plan.groups)
        def _(group):
            for low in range(0, plan.frames, plan.joint):
                rows = piece_ref[group, pl.ds(low * plan.group, 16), :].astype(F32)
                for more in range(plan.joint):
                    target_ref[pl.ds(pl.multiple_of(starts[low + more] + group * plan.group, plan.group), plan.group), :] = rows[more * plan.group:(more + 1) * plan.group]


class Plan:
    def __init__(self, parts, clips, frames, slots):
        self.parts, self.clips, self.frames = parts, clips, frames
        self.joint = 2 if frames % 2 == 0 else 1
        self.group = 16 // self.joint
        self.per_clip = parts // clips
        self.places = slots // self.per_clip
        self.groups = -(-self.places // self.group)
        self.room = self.groups * self.group
        self.slots = self.room * self.per_clip
        self.span = frames * self.group
        self.tile_time = parts * self.span
        self.rows = clips * frames * self.slots

    def starts(self, part):
        clip, place = part // self.per_clip, part % self.per_clip
        return [(clip * self.frames + frame) * self.slots + place * self.room for frame in range(self.frames)]

    def fill(self, v):
        v = v.reshape(v.shape[:2] + (self.per_clip, self.places) + v.shape[3:])
        return jnp.pad(v, [(0, 0)] * 3 + [(0, self.room - self.places)] + [(0, 0)] * (v.ndim - 4))

    def fill_all(self, v):
        return self.fill(v.reshape((-1,) + v.shape[2:]))

    def strip(self, v, lead):
        v = v.reshape(lead + (self.frames, self.per_clip, self.room, v.shape[-1]))
        return v[..., :self.places, :].reshape(lead + (self.frames, self.per_clip * self.places, v.shape[-1]))


def attend_fwd(plan, space, *refs):
    if space:
        tile = plan.slots
        me_ref, x_ref = refs[0], refs[1].at[0]
        refs = refs[2:]
    else:
        tile = plan.tile_time
        pieces, refs = refs[:plan.parts], refs[plan.parts:]
    gains_ref, bias_ref, wq_ref, wk_ref, wv_ref, wo_ref = refs[:6]
    refs = refs[6:]
    if space:
        out_pieces, refs = refs[:plan.parts], refs[plan.parts:]
    else:
        out_ref, refs = refs[0], refs[1:]
    nt_ref, q_ref, k_ref, v_ref, p_ref, att_ref, n_ref, acc_ref, gain_ref = refs
    step, steps = pl.program_id(0), pl.num_programs(0)
    rows = n_ref.shape[0]
    rb = row_block(rows)
    small = row_block(rows, 64)

    @pl.when(step == 0)
    def _():
        gain_ref[...] = gain_row(gains_ref, 0 if space else 1)

        def take(at, x):
            x = x.astype(F32)
            n_ref[at, :] = (normalise(x)[0] * gain_ref[...]).astype(LOW)
            acc_ref[at, :] = x

        if space:
            loop_rows(rows, small, lambda at: take(at, x_ref[at, :]))
        else:
            @pl.loop(0, plan.groups)
            def _(group):
                for k, piece_ref in enumerate(pieces):
                    take(pl.ds(pl.multiple_of(group * tile + k * plan.span, 16), plan.span), piece_ref[group])
        nt_ref[...] = n_ref[...].T

    def project(at):
        n = n_ref[at, :]
        q_ref[at, :] = (dot(n, wq_ref[...]).astype(LOW) * (HEAD_DIM ** -0.5)).astype(LOW)
        k_ref[at, :] = dot(n, wk_ref[...]).astype(LOW)
        v_ref[at, :] = dot(n, wv_ref[...]).astype(LOW)
    loop_rows(rows, rb, project)

    @pl.loop(0, rows // tile)
    def _(t):
        at = pl.ds(pl.multiple_of(t * tile, tile), tile)
        for pair in range(2):
            cols = pl.ds(pair * PAIR, PAIR)
            qs = spread_pair(q_ref[at, cols])
            s = dot_nt(qs, k_ref[at, cols]) + bias_ref[...]
            e = jnp.exp(s - jnp.max(s, axis=-1, keepdims=True))
            p = (e * (1.0 / jnp.sum(e, axis=-1, keepdims=True))).astype(LOW)
            p_ref[0, pl.ds(pl.multiple_of((t * 2 + pair) * 2 * tile, 2 * tile), 2 * tile), :] = p
            att_ref[at, cols] = join_pair(dot(p, v_ref[at, cols])).astype(LOW)

    def project_out(at):
        acc_ref[at, :] += dot(att_ref[at, :], wo_ref[...])
    loop_rows(rows, rb, project_out)

    @pl.when(step == steps - 1)
    def _():
        if space:
            store_pieces(me_ref[0], out_pieces, acc_ref, plan)
        else:
            out_ref[...] = acc_ref[...]


def attend_bwd(plan, space, prior, again, *refs):
    parts = plan.parts
    if space:
        tile = plan.slots
        me_ref, g_pieces, done_pieces, x_ref, refs = refs[0], refs[1:1 + parts], refs[1 + parts:1 + 2 * parts], refs[1 + 2 * parts].at[0], refs[2 + 2 * parts:]
    else:
        tile = plan.tile_time
        g_ref, x_pieces, refs = refs[0], refs[1:1 + parts], refs[1 + parts:]
    gains_ref, nt_ref, q_ref, k_ref, v_ref, p_ref, att_ref, wq_ref, wk_ref, wv_ref, wo_ref = refs[:11]
    refs = refs[11:]
    if prior:
        old_ref, oldo_ref, oldg_ref = refs[:3]
        refs = refs[3:]
    if again:
        refs = refs[2:]
    if space:
        gx_ref, done_ref, refs = refs[0].at[0], refs[1].at[0], refs[2:]
    else:
        out_pieces, refs = refs[:parts], refs[parts:]
    dw_ref, dwo_ref, dgain_ref, low_ref, do_ref, dq_ref, dk_ref, dv_ref, acc_ref, gain_ref = refs
    step, steps = pl.program_id(0), pl.num_programs(0)
    rows, width = acc_ref.shape
    rb = row_block(rows)
    small = row_block(rows, 64)

    @pl.when(step == 0)
    def _():
        gain_ref[...] = gain_row(gains_ref, 0 if space else 1)
        if space:
            load_pieces(me_ref[0], g_pieces, gx_ref, plan)

            def lower(at):
                low_ref[at, :] = gx_ref[at, :].astype(LOW)
        else:
            def lower(at):
                low_ref[at, :] = g_ref[at, :].astype(LOW)
        loop_rows(rows, small, lower)

    def back_out(at):
        do_ref[at, :] = dot_nt(low_ref[at, :], wo_ref[...]).astype(LOW)
    loop_rows(rows, rb, back_out)
    total = dot_tn(att_ref[...], low_ref[...])
    if prior:
        total += oldo_ref[...]
    dwo_ref[...] = total.astype(dwo_ref.dtype)

    @pl.loop(0, rows // tile)
    def _(t):
        at = pl.ds(pl.multiple_of(t * tile, tile), tile)
        for pair in range(2):
            cols = pl.ds(pair * PAIR, PAIR)
            dos = spread_pair(do_ref[at, cols])
            att = att_ref[at, cols].astype(F32)
            inner = jnp.sum(dos.astype(F32) * jnp.concatenate([att, att], axis=0), axis=-1, keepdims=True)
            p = p_ref[0, pl.ds(pl.multiple_of((t * 2 + pair) * 2 * tile, 2 * tile), 2 * tile), :]
            ds = (p.astype(F32) * (dot_nt(dos, v_ref[at, cols]) - inner)).astype(LOW)
            dq_ref[at, cols] = (join_pair(dot(ds, k_ref[at, cols])) * (HEAD_DIM ** -0.5)).astype(LOW)
            dk_ref[at, cols] = dot_tn(ds, spread_pair(q_ref[at, cols])).astype(LOW)
            dv_ref[at, cols] = dot_tn(p, dos).astype(LOW)

    def back_in(at):
        part = dot_nt(dq_ref[at, :], wq_ref[...]) + dot_nt(dk_ref[at, :], wk_ref[...]) + dot_nt(dv_ref[at, :], wv_ref[...])

        @pl.when(step == 0)
        def _():
            acc_ref[at, :] = part

        @pl.when(step != 0)
        def _():
            acc_ref[at, :] += part
    loop_rows(rows, rb, back_in)
    for at, grad_ref in enumerate((dq_ref, dk_ref, dv_ref)):
        total = dot(nt_ref[...], grad_ref[...])
        if prior:
            total += old_ref[at]
        dw_ref[at] = total.astype(dw_ref.dtype)

    @pl.when(step == steps - 1)
    def _():
        if prior:
            dgain_ref[...] = oldg_ref[...]
        else:
            dgain_ref[...] = jnp.zeros_like(dgain_ref)

        if space:
            def finish(at):
                back, gains = norm_back(x_ref[at, :].astype(F32), gain_ref[...], acc_ref[at, :])
                dgain_ref[...] += gains
                gx_ref[at, :] += back
            loop_rows(rows, small, finish)
            load_pieces(me_ref[0], done_pieces, acc_ref, plan)

            def lower(at):
                done_ref[at, :] = acc_ref[at, :].astype(LOW)
            loop_rows(rows, small, lower)
        else:
            @pl.loop(0, plan.groups)
            def _(group):
                for k in range(parts):
                    at = pl.ds(pl.multiple_of(group * tile + k * plan.span, 16), plan.span)
                    back, gains = norm_back(x_pieces[k][group].astype(F32), gain_ref[...], acc_ref[at, :])
                    dgain_ref[...] += gains
                    out_pieces[k][group] = (g_ref[at, :] + back).astype(LOW)


def mlp_both(plan, prior, me_ref, second_ref, cot_ref, *refs):
    parts = plan.parts
    keep_ref, gains_ref, w1_ref, w2_ref = refs[:4]
    refs = refs[4:]
    if prior:
        old1_ref, old2_ref, oldg_ref = refs[:3]
        refs = refs[3:]
    out_pieces, refs = refs[:parts], refs[parts:]
    grad_ref, dw1_ref, dw2_ref, dgain_ref, n_ref, nt_ref, up_ref, sum_ref, act_ref, gh_ref, gain_ref = refs
    acc_ref = grad_ref
    step, steps = pl.program_id(0), pl.num_programs(0)
    rows = second_ref.shape[0]
    rb = row_block(rows, 256)

    def each_span(body):
        @pl.loop(0, plan.groups)
        def _(group):
            for k in range(parts):
                body(group, k, pl.ds(pl.multiple_of(group * plan.tile_time + k * plan.span, 16), plan.span))

    @pl.when(step == 0)
    def _():
        gain_ref[...] = gain_row(gains_ref, 2)

        def start(group, k, at):
            v = second_ref[at, :]
            n_ref[at, :] = (normalise(v)[0] * gain_ref[...]).astype(LOW)
            up_ref[at, :] = (cot_ref[lax.bitwise_xor(me_ref[0], k), group].astype(F32) * keep_ref[at, :]).astype(LOW)
            sum_ref[at, :] = v
            acc_ref[at, :] = jnp.zeros_like(v)
        each_span(start)
        nt_ref[...] = n_ref[...].T

    width = second_ref.shape[1]
    firsts = [pl.ds(at * UNITS, UNITS) for at in range(FF_TILE // UNITS)]
    seconds = [pl.ds(at * width, width) for at in range(FF_TILE // UNITS)]

    def body(at):
        h = dot(n_ref[at, :], w1_ref[...])
        ga = jnp.concatenate([dot_nt(up_ref[at, :], w2_ref[:, second]) for second in seconds], axis=1)
        square = h * h
        t = jnp.tanh(GELU_A * h * (1.0 + GELU_B * square))
        half = 0.5 + 0.5 * t
        act = (h * half).astype(LOW)
        slope = half + h * (0.5 - 0.5 * t * t) * (GELU_A + (3.0 * GELU_A * GELU_B) * square)
        gh = (ga * slope).astype(LOW)
        act_ref[at, :] = act
        gh_ref[at, :] = gh
        sum_ref[at, :] += sum(dot(act[:, first.start:first.start + first.size], w2_ref[:, second]) for first, second in zip(firsts, seconds))
        acc_ref[at, :] += dot_nt(gh, w1_ref[...])
    loop_rows(rows, rb, body)
    total = dot(nt_ref[...], gh_ref[...])
    if prior:
        total += old1_ref[...]
    dw1_ref[...] = total.astype(dw1_ref.dtype)
    for first, second in zip(firsts, seconds):
        total = dot_tn(act_ref[:, first], up_ref[...])
        if prior:
            total += old2_ref[:, second]
        dw2_ref[:, second] = total.astype(dw2_ref.dtype)

    @pl.when(step == steps - 1)
    def _():
        if prior:
            dgain_ref[...] = oldg_ref[...]
        else:
            dgain_ref[...] = jnp.zeros_like(dgain_ref)

        def last(group, k, at):
            out_pieces[k][group] = (keep_ref[at, :] * sum_ref[at, :]).astype(LOW)
            back, gains = norm_back(second_ref[at, :], gain_ref[...], acc_ref[at, :])
            dgain_ref[...] += gains
            grad_ref[at, :] = up_ref[at, :].astype(F32) + back
        each_span(last)


def whole(shape, at=None):
    spot = (0,) * len(shape) if at is None else at
    return pl.BlockSpec(shape, lambda i: spot, pipeline_mode=pl.Buffered(1))


def params():
    return pltpu.CompilerParams(dimension_semantics=("arbitrary",), vmem_limit_bytes=VMEM_LIMIT)


def spec_cols(shape, offset=0):
    return pl.BlockSpec(shape, lambda i, o=offset: (0, o + i))


def spec_rows(shape, column=0):
    return pl.BlockSpec(shape, lambda i: (i, column))


def weight_specs(width):
    quads = width // QUAD
    return [spec_cols((width, QUAD), at * quads) for at in range(3)] + [spec_rows((QUAD, width), 3)]


def piece_shapes(plan, width):
    return [jax.ShapeDtypeStruct((plan.groups, plan.span, width), LOW)] * plan.parts


def piece_specs(plan, width):
    return [whole((plan.groups, plan.span, width))] * plan.parts


def scalar():
    return pl.BlockSpec(memory_space=pltpu.SMEM)


LANES = 128


def gains_spec(bundle):
    rows, columns = bundle.shape
    return whole((rows, LANES), (0, columns // LANES - 1))


def run_attend_fwd(plan, space, micro, lead, gain, bias, weights):
    rows, width = plan.rows, gain.shape[0]
    tile = plan.slots if space else plan.tile_time
    quads = width // QUAD
    probs_rows = rows * 4
    low = jax.ShapeDtypeStruct((rows, width), LOW)
    cost = pl.CostEstimate(flops=rows * 4 // COST_SHARE * width * (4 * width + 8 * tile), bytes_accessed=rows * width, transcendentals=0)
    lead_specs = [scalar(), whole((1, rows, width), (micro, 0, 0))] if space else piece_specs(plan, width)
    out_specs = piece_specs(plan, width) if space else [whole((rows, width))]
    out_shape = piece_shapes(plan, width) if space else [jax.ShapeDtypeStruct((rows, width), F32)]
    result = pl.pallas_call(
        functools.partial(attend_fwd, plan, space),
        grid=(quads,),
        in_specs=lead_specs + [gains_spec(gain), whole(bias.shape)] + weight_specs(width),
        out_specs=out_specs + [whole((width, rows))] + [spec_cols((rows, QUAD))] * 3
        + [pl.BlockSpec((1, probs_rows, tile), lambda i: (i, 0, 0)), spec_cols((rows, QUAD))],
        out_shape=out_shape + [jax.ShapeDtypeStruct((width, rows), LOW), low, low, low,
                               jax.ShapeDtypeStruct((quads, probs_rows, tile), LOW), low],
        scratch_shapes=[pltpu.VMEM((rows, width), LOW), pltpu.VMEM((rows, width), F32), pltpu.VMEM((1, width), F32)],
        compiler_params=params(),
        cost_estimate=cost,
    )(*lead, gain, bias, weights, weights, weights, weights)
    return list(result[:len(out_shape)]), list(result[len(out_shape):])


def run_attend_bwd(plan, space, lead, gain, saved, weights, micro, micros, old=None, shared=None):
    rows, width = plan.rows, gain.shape[0]
    tile = plan.slots if space else plan.tile_time
    quads = width // QUAD
    probs_rows = rows * 4
    weight_type = LOW if micro == micros - 1 else F32
    cost = pl.CostEstimate(flops=rows * 4 // COST_SHARE * width * (8 * width + 20 * tile), bytes_accessed=rows * width, transcendentals=0)
    weight_out = [pl.BlockSpec((3, width, QUAD), lambda i: (0, 0, i)), spec_rows((QUAD, width)), whole((1, width))]
    token = whole((rows, width))
    lead_specs = [scalar()] + piece_specs(plan, width) * 2 + [whole((1, rows, width), (micro, 0, 0))] if space else [token] + piece_specs(plan, width)
    if space:
        out_specs = [whole((1, rows, width), (micro, 0, 0))] * 2
        out_shape = [jax.ShapeDtypeStruct((micros, rows, width), F32), jax.ShapeDtypeStruct((micros, rows, width), LOW)]
    else:
        out_specs, out_shape = piece_specs(plan, width), piece_shapes(plan, width)
    operands = [*lead, gain, *saved, weights, weights, weights, weights]
    in_specs = (lead_specs + [gains_spec(gain), whole((width, rows))] + [spec_cols((rows, QUAD))] * 3
                + [pl.BlockSpec((1, probs_rows, tile), lambda i: (i, 0, 0)), spec_cols((rows, QUAD))] + weight_specs(width))
    if old is not None:
        operands += old
        in_specs = in_specs + weight_out
    aliases = {}
    if shared is not None:
        aliases = {len(operands): 0, len(operands) + 1: 1}
        operands += shared
        in_specs = in_specs + [pl.BlockSpec(memory_space=pl.ANY)] * 2
    result = pl.pallas_call(
        functools.partial(attend_bwd, plan, space, old is not None, shared is not None),
        grid=(quads,),
        in_specs=in_specs,
        out_specs=out_specs + weight_out,
        out_shape=out_shape + [jax.ShapeDtypeStruct((3, width, width), weight_type),
                               jax.ShapeDtypeStruct((width, width), weight_type), jax.ShapeDtypeStruct((1, width), F32)],
        scratch_shapes=[pltpu.VMEM((rows, width), LOW)] + [pltpu.VMEM((rows, QUAD), LOW)] * 4 + [pltpu.VMEM((rows, width), F32), pltpu.VMEM((1, width), F32)],
        input_output_aliases=aliases,
        compiler_params=params(),
        cost_estimate=cost,
    )(*operands)
    return list(result[:len(out_shape)]), list(result[len(out_shape):])


FF_TILE = 512
UNITS = 256


def run_mlp(plan, me, second, cot, keep, gain, weights, last, old=None):
    rows, width = second.shape
    hidden = weights.shape[1] // 2
    steps = hidden // FF_TILE
    joint = FF_TILE // UNITS
    blocks = width // UNITS
    weight_type = LOW if last else F32
    cost = pl.CostEstimate(flops=rows * 14 // COST_SHARE * width * hidden, bytes_accessed=rows * width, transcendentals=0)

    def second_spec(start):
        return pl.BlockSpec((UNITS, joint * width), lambda i: (i % blocks, start // (joint * width) + i // blocks))
    weight_out = [spec_cols((width, FF_TILE)), second_spec(0), whole((1, width))]
    token = whole((rows, width))
    result = pl.pallas_call(
        functools.partial(mlp_both, plan, old is not None),
        grid=(steps,),
        in_specs=[scalar(), token, whole(cot.shape), whole((rows, 1)), gains_spec(gain),
                  spec_cols((width, FF_TILE)), second_spec(hidden)] + ([] if old is None else weight_out),
        out_specs=piece_specs(plan, width) + [token] + weight_out,
        out_shape=piece_shapes(plan, width) + [jax.ShapeDtypeStruct((rows, width), F32),
                   jax.ShapeDtypeStruct((width, hidden), weight_type), jax.ShapeDtypeStruct((width, hidden), weight_type),
                   jax.ShapeDtypeStruct((1, width), F32)],
        scratch_shapes=[pltpu.VMEM((rows, width), LOW), pltpu.VMEM((width, rows), LOW), pltpu.VMEM((rows, width), LOW),
                        pltpu.VMEM((rows, width), F32),
                        pltpu.VMEM((rows, FF_TILE), LOW), pltpu.VMEM((rows, FF_TILE), LOW), pltpu.VMEM((1, width), F32)],
        compiler_params=params(),
        cost_estimate=cost,
    )(me, second, cot, keep, gain, weights, weights, *([] if old is None else old))
    return list(result[:plan.parts]), result[plan.parts], list(result[plan.parts + 1:])


class Units:
    def __init__(self, devices, width, hidden):
        self.devices, self.rows = devices, width // devices
        self.ratio, self.joint = hidden // width, FF_TILE // UNITS
        self.blocks = width // UNITS

    def first_in(self, v):
        lead = v.shape[0]
        v = v.reshape(lead, self.devices, self.ratio, self.rows).transpose(0, 2, 1, 3)
        v = v.reshape(lead, self.ratio // self.joint, self.joint, self.blocks, UNITS).transpose(0, 1, 3, 2, 4)
        return v.reshape(lead, -1)

    def first_out(self, v):
        lead = v.shape[0]
        v = v.reshape(lead, self.ratio // self.joint, self.blocks, self.joint, UNITS).transpose(0, 1, 3, 2, 4)
        v = v.reshape(lead, self.ratio, self.devices, self.rows).transpose(0, 2, 1, 3)
        return v.reshape(lead, -1)

    def second_in(self, v):
        return v.reshape(self.ratio, self.rows, -1).transpose(1, 0, 2).reshape(self.rows, -1)

    def second_out(self, v):
        return v.reshape(self.rows, self.ratio, -1).transpose(1, 0, 2).reshape(self.rows * self.ratio, -1)


def swap(v, axis, size, by):
    return lax.ppermute(v, axis, [(i, i ^ by) for i in range(size)])


def exchange(pieces):
    return [piece if at == 0 else swap(piece, "seq", len(pieces), at) for at, piece in enumerate(pieces)]


def pick(v, at):
    return lax.dynamic_index_in_dim(v, at, 0, False)


def collect(v, axis, size, me, stride=1):
    count = size * stride
    out = jnp.zeros((size,) + v.shape, v.dtype)
    for at in range(size):
        out = lax.dynamic_update_index_in_dim(out, v if at == 0 else swap(v, axis, count, at * stride), lax.bitwise_xor(me, at), 0)
    return out


def reduce_blocks(v, axis, size, me, stride=1):
    count = size * stride
    parts = [swap(pick(v, lax.bitwise_xor(me, at)), axis, count, at * stride) for at in range(1, size)]
    total = pick(v, me).astype(F32)
    for part in parts:
        total += part.astype(F32)
    return total


def gather_rows(v, dp, seq):
    rows, width = v.shape
    device, place = lax.axis_index("dp"), lax.axis_index("seq")
    v = collect(v, "seq", seq, place)
    v = collect(v, "dp", dp // 2, device // 2, 2)
    other = swap(v, "dp", dp, 1)
    core = (device % 2) == 0
    v = jnp.stack([jnp.where(core, v, other), jnp.where(core, other, v)], axis=1)
    return v.reshape(dp * seq * rows, width)


def scatter_rows(v, dp, seq):
    device, place = lax.axis_index("dp"), lax.axis_index("seq")
    rows, width = v.shape
    v = v.reshape(dp // 2, 2, rows // dp, width)
    core = device % 2
    own = lax.dynamic_index_in_dim(v, core, 1, False)
    got = swap(lax.dynamic_index_in_dim(v, 1 - core, 1, False), "dp", dp, 1)
    v = (own.astype(F32) + got.astype(F32)).astype(LOW)
    v = reduce_blocks(v, "dp", dp // 2, device // 2, 2).astype(LOW)
    return reduce_blocks(v.reshape(seq, rows // (dp * seq), width), "seq", seq, place)


def shards(dp, seq, frames_in, qkv_spatial, out_spatial, qkv_temporal, out_temporal, mlp_in, mlp_out, gains, place_mask, cotangent):
    both = ("dp", "seq")
    micros, clips, local_frames, slots, width = frames_in.shape
    hidden = mlp_in.shape[1]
    plan = Plan(seq, clips, local_frames, slots)
    place = lax.axis_index("seq")
    me = place.astype(jnp.int32).reshape(1)

    units = Units(dp * seq, width, hidden)
    after = lax.optimization_barrier

    def send_cot(v):
        v = plan.fill(v).transpose(0, 2, 1, 3, 4).reshape(seq, local_frames, plan.groups, plan.group, width)
        v = v.transpose(0, 2, 1, 3, 4).reshape(seq, plan.groups, plan.span, width)
        return lax.all_to_all(v, "seq", split_axis=0, concat_axis=0, tiled=True)

    padded_gains = jnp.pad(gains, ((0, 0), (0, LANES - gains.shape[1])))
    cots = [send_cot(cotangent[0])]
    space = gather_rows(jnp.concatenate([qkv_spatial, out_spatial, padded_gains], axis=1), dp, seq)
    time = lax.all_gather(jnp.concatenate([qkv_temporal, out_temporal], axis=1), both, axis=0, tiled=True)
    mlp = lax.all_gather(jnp.concatenate([units.first_in(mlp_in), units.second_in(mlp_out)], axis=1), both, axis=0, tiled=True)

    bias_space = jnp.where(place_mask > 0, 0.0, -1000000000.0).astype(F32).reshape(plan.per_clip, plan.places)
    bias_space = jnp.pad(bias_space, ((0, 0), (0, plan.room - plan.places)), constant_values=-1000000000.0).reshape(1, plan.slots)
    spot = jnp.arange(plan.tile_time) % plan.group
    bias_time = jnp.where(spot[:, None] == spot[None, :], 0.0, -1000000000.0).astype(F32)
    bias_time = jnp.concatenate([bias_time, bias_time], axis=0)
    keep = pick(place_mask.astype(F32).reshape(plan.per_clip, plan.places), place % plan.per_clip)
    keep = jnp.pad(keep, (0, plan.room - plan.places)).reshape(plan.groups, 1, plan.group)
    keep = jnp.broadcast_to(keep, (plan.groups, seq * local_frames, plan.group)).reshape(plan.rows, 1)

    inputs = plan.fill_all(frames_in).reshape(micros, plan.rows, width)
    space_saved, across = [], []
    for m in range(micros):
        out, saved = run_attend_fwd(plan, True, m, [me, inputs], space, bias_space, space)
        space_saved.append(saved)
        across.append(exchange(out))
        if m == 0:
            me, cots[0] = after((me, cots[0]))
    def scatter(parts):
        return lax.psum_scatter(jnp.concatenate(parts, axis=1), both, scatter_dimension=0, tiled=True).astype(F32)

    def attend_parts(old):
        return [old[0][0], old[0][1], old[0][2], old[1]]

    done, afters, time_saved, grads = [], [], [], []
    old_mlp = old_time = old_space = shared = None
    for m in range(micros):
        (second,), saved = run_attend_fwd(plan, False, m, across[m], space, bias_time, time)
        time_saved.append(saved)
        if m > 0:
            second, done[m - 1] = after((second, done[m - 1]))
        if m + 1 < micros:
            second, across, cot = after((second, across, cotangent[m + 1]))
            cots.append(send_cot(cot))
            across[m + 1], cots[m + 1] = after((across[m + 1], cots[m + 1]))
        out, grad, old_mlp = run_mlp(plan, me, second, cots[m], keep, space, mlp, m == micros - 1, old_mlp)
        done.append(exchange(out))
        grads.append(grad)
    owned_mlp = scatter(old_mlp[:2])
    for m in range(micros):
        grads[m], old_mlp[2] = after((grads[m], old_mlp[2]))
        if m > 0:
            grads[m], done[-1] = after((grads[m], done[-1]))
        back, old_time = run_attend_bwd(plan, False, [grads[m], *across[m]], space, time_saved[m], time, m, micros, old_time)
        afters.append(exchange(back))
    owned_time = scatter(attend_parts(old_time))
    afters[0], old_time[2] = after((afters[0], old_time[2]))
    for m in range(micros):
        if m == micros - 1:
            afters[m], owned_mlp = after((afters[m], owned_mlp))
        shared, old_space = run_attend_bwd(plan, True, [me, *afters[m], *done[m], inputs], space, space_saved[m], space, m, micros, old_space, shared)

    gain_grads = jnp.concatenate([old_space[2], old_time[2], old_mlp[2]], axis=0).T.astype(LOW)
    owned = scatter_rows(jnp.concatenate(attend_parts(old_space) + [jnp.pad(gain_grads, ((0, 0), (0, LANES - gain_grads.shape[1])))], axis=1), dp, seq)
    return (
        plan.strip(shared[1], (micros, clips)),
        plan.strip(shared[0], (micros, clips)),
        owned[:, :3 * width],
        owned[:, 3 * width:4 * width],
        owned_time[:, :3 * width],
        owned_time[:, 3 * width:],
        units.first_out(owned_mlp[:, :hidden]),
        units.second_out(owned_mlp[:, hidden:]),
        owned[:, 4 * width:4 * width + gains.shape[1]],
    )


def solution(mesh):
    rows = P(("dp", "seq"), None)
    tokens = P(None, "dp", "seq", None, None)
    return jax.shard_map(
        functools.partial(shards, mesh.shape["dp"], mesh.shape["seq"]),
        mesh=mesh,
        in_specs=(tokens,) + (rows,) * 7 + (P(), tokens),
        out_specs=(tokens, tokens) + (rows,) * 7,
        check_vma=False,
    )
```

time: 1600 us -> 924 us (0.58)
  waiting for transfers between devices: 617 us -> 96.2 us
  blocking collectives: 157 us -> 0 us
  starting transfers between devices: 36.4 us -> 76.4 us
  local copies, waits for them, and re-layouts: 79.6 us -> 41.1 us
    all_to_all x8 -> x2, waiting for transfers between devices: 219 us -> 6.74 us  [send_cot(): return lax.all_to_all(v, 'seq', split_axis=0, concat_axis=0, tiled=True)]
    reduce_scatter x4 -> x2, waiting for transfers between devices: 189 us -> 0.02 us  [scatter(): lax.psum_scatter(jnp.concatenate(parts, axis=1), both, scatter_dimension=...]
    all_gather x1 -> x0, blocking collectives: 120 us -> none  [gather(): return lax.all_gather(w, both, axis=0, tiled=True)]
    unnamed x14 -> x4, waiting for transfers between devices: 111 us -> 0.07 us
    all_gather x6 -> x2, waiting for transfers between devices: 97.8 us -> 0.01 us  [the longest x1 0.01 us: shards(): lax.all_gather(jnp.concatenate([qkv_temporal, out_temporal], axis=1), bot...]
    ppermute x0 -> x32, waiting for transfers between devices: none -> 89.4 us  [swap(): return lax.ppermute(v, axis, [(i, i ^ by) for i in range(size)])]
    ppermute x0 -> x32, starting transfers between devices: none -> 52.5 us  [swap(): return lax.ppermute(v, axis, [(i, i ^ by) for i in range(size)])]
    unnamed x1 -> x0, blocking collectives: 37.4 us -> none
  transfers between devices with their start and end apart: 20 -> 38, of which waited for: 10 -> 10; matrix products, arithmetic and copies ran while one was open for 6% -> 5% of each run, Pallas kernels for 42% -> 62%
where the time goes in v2:
time: 924 us; the launch traced here: 919 us
  Pallas kernels  662 us (72%)
  waiting for transfers between devices  96.2 us (10%)
  starting transfers between devices  76.4 us (8%)
  local copies, waits for them, and re-layouts  41.1 us (4%)
  other arithmetic  28.6 us (3%)
  between operations  14.8 us (2%)
    pallas_call x4, Pallas kernels, run_attend_bwd(): pl.pallas_call(functools.partial(attend_bwd, plan, space, old is not None...  266 us
    pallas_call x4, Pallas kernels, run_attend_fwd(): pl.pallas_call(functools.partial(attend_fwd, plan, space), grid=(quads,),...  215 us
    pallas_call x2, Pallas kernels, run_mlp(): pl.pallas_call(functools.partial(mlp_both, plan, old is not None), grid=(...  181 us
    ppermute x32, waiting for transfers between devices, swap(): return lax.ppermute(v, axis, [(i, i ^ by) for i in range(size)])  89.4 us
    ppermute x32, starting transfers between devices, swap(): return lax.ppermute(v, axis, [(i, i ^ by) for i in range(size)])  52.5 us
    all_to_all x2, starting transfers between devices, send_cot(): return lax.all_to_all(v, 'seq', split_axis=0, concat_axis=0, tiled=True)  23.1 us
  transfers between devices with their start and end apart: 38, of which 10 were waited for; matrix products, arithmetic and copies ran while one was open for 5% of the time, Pallas kernels for 62%

profile of v2, /device:TPU:0, one launch (start us, length us, event | category | flops | bytes accessed | tf_op | source)
XLA Modules:
  0.0 919.4 jit_solution(5398308465791437805)
XLA Ops:
  13.7 3.1 collective-permute-start
  19.5 3.4 collective-permute-done
  22.9 10.1 %collective-permute-done.1 = bf16[24,3200]{1,0:T(8,128)(2,1)S(1)} collective-permute-done((bf16[24,3200]{1,0:T(8,128)(2,1)S(1)}, bf16[24,3200]{1,0:T(8,128)(2,1)S(1)}, u32[]{:S(2)}, u32[]{:S(2)}) %collective-permute-start.1) | collective-permute-done | bytes 153632 | tf_op jit(solution)/shard_map/ppermute | solution.py:554
  39.2 15.0 %collective-permute-done.3 = bf16[4,24,3200]{2,1,0:T(8,128)(2,1)S(1)} collective-permute-done((bf16[4,24,3200]{2,1,0:T(8,128)(2,1)S(1)}, bf16[4,24,3200]{2,1,0:T(8,128)(2,1)S(1)}, u32[]{:S(2)}, u32[]{:S(2)}) %collective-permute-start.3) | collective-permute-done | bytes 614432 | tf_op jit(solution)/shard_map/ppermute | solution.py:554
  56.0 7.7 collective-permute-done.5
  68.4 7.6 all-to-all-start
  76.5 2.9 select_bitcast_fusion.1
  79.4 2.8 pad_maximum_fusion.1
  82.2 51.3 %shard_map.169 = (bf16[13,32,768]{2,1,0:T(8,128)(2,1)}, bf16[13,32,768]{2,1,0:T(8,128)(2,1)}, bf16[13,32,768]{2,1,0:T(8,128)(2,1)}, bf16[13,32,768]{2,1,0:T(8,12...) custom-call(s32[1]{0:T(128)} %bitcast.refs_0_.me_ref, ...), custom_call_target="tpu_custom_call" | custom-call | flops 2418769920 | bytes 1277952 | tf_op jit(solution)/shard_map/pallas_call | solution.py:437
  138.1 6.7 all-to-all-done.cot_ref
  144.8 52.6 %shard_map.171 = (bf16[13,32,768]{2,1,0:T(8,128)(2,1)}, bf16[13,32,768]{2,1,0:T(8,128)(2,1)}, bf16[13,32,768]{2,1,0:T(8,128)(2,1)}, bf16[13,32,768]{2,1,0:T(8,12...) custom-call(s32[1]{0:T(128)} %bitcast.refs_0_.me_ref, ...), custom_call_target="tpu_custom_call" | custom-call | flops 2418769920 | bytes 1277952 | tf_op jit(solution)/shard_map/pallas_call | solution.py:437
  199.0 2.8 collective-permute-start.12
  202.6 56.0 %shard_map.170 = (f32[1664,768]{1,0:T(8,128)}, bf16[768,1664]{1,0:T(8,128)(2,1)}, bf16[1664,768]{1,0:T(8,128)(2,1)}, bf16[1664,768]{1,0:T(8,128)(2,1)}, bf16[166...) custom-call(bf16[13,32,768]{2,1,0:T(8,128)(2,1)} %get-tuple-element.172.refs_0_.refs_1_, ...), custom_call_target="tpu_custom_call" | custom-call | flops 2091909120 | bytes 1277952 | tf_op jit(solution)/shard_map/pallas_call | solution.py:437
  258.7 19.9 %collective-permute-done.11.refs_2_.refs_3_ = bf16[13,32,768]{2,1,0:T(8,128)(2,1)} collective-permute-done((bf16[13,32,768]{2,1,0:T(8,128)(2,1)}, bf16[13,32,768]{2,1,0:T(8,128)(2,1)}, u32[]{:S(2)}, u32[]{:S(2)}) %collective-permute-start.11) | collective-permute-done | bytes 639008 | tf_op jit(solution)/shard_map/ppermute | solution.py:554
  280.6 15.5 %all-to-all-start.1 = ((bf16[4,13,32,768]{3,2,1,0:T(8,128)(2,1)}), bf16[4,13,32,768]{3,2,1,0:T(8,128)(2,1)S(1)}, u32[]{:S(2)}, u32[]{:S(2)}) async-start(bf16[4,13,32,768]{3,2,1,0:T(8,128)(2,1)} %bitcast.135), calls=%async_computation.1 | async-start | bytes 5111808 | tf_op jit(solution)/shard_map/all_to_all | solution.py:619
  298.0 90.1 %shard_map.173 = (bf16[13,32,768]{2,1,0:T(8,128)(2,1)}, bf16[13,32,768]{2,1,0:T(8,128)(2,1)}, bf16[13,32,768]{2,1,0:T(8,128)(2,1)}, bf16[13,32,768]{2,1,0:T(8,12...) custom-call(s32[1]{0:T(128)} %bitcast.refs_0_.me_ref, ...), custom_call_target="tpu_custom_call" | custom-call | flops 5494800384 | bytes 1277952 | tf_op jit(solution)/shard_map/pallas_call | solution.py:510
  393.0 55.4 %shard_map.172 = (f32[1664,768]{1,0:T(8,128)}, bf16[768,1664]{1,0:T(8,128)(2,1)}, bf16[1664,768]{1,0:T(8,128)(2,1)}, bf16[1664,768]{1,0:T(8,128)(2,1)}, bf16[166...) custom-call(bf16[13,32,768]{2,1,0:T(8,128)(2,1)} %get-tuple-element.139.refs_0_.refs_1_, ...), custom_call_target="tpu_custom_call" | custom-call | flops 2091909120 | bytes 1277952 | tf_op jit(solution)/shard_map/pallas_call | solution.py:437
  448.5 90.8 %shard_map.174 = (bf16[13,32,768]{2,1,0:T(8,128)(2,1)}, bf16[13,32,768]{2,1,0:T(8,128)(2,1)}, bf16[13,32,768]{2,1,0:T(8,128)(2,1)}, bf16[13,32,768]{2,1,0:T(8,12...) custom-call(s32[1]{0:T(128)} %bitcast.refs_0_.me_ref, ...), custom_call_target="tpu_custom_call" | custom-call | flops 5494800384 | bytes 1277952 | tf_op jit(solution)/shard_map/pallas_call | solution.py:510
  539.3 9.0 pad_maximum_fusion
  549.7 2.9 collective-permute-start.17
  553.1 64.6 %shard_map.175 = (bf16[13,32,768]{2,1,0:T(8,128)(2,1)}, bf16[13,32,768]{2,1,0:T(8,128)(2,1)}, bf16[13,32,768]{2,1,0:T(8,128)(2,1)}, bf16[13,32,768]{2,1,0:T(8,12...) custom-call(f32[1664,768]{1,0:T(8,128)} %get-tuple-element.171.refs_0_, ...), custom_call_target="tpu_custom_call" | custom-call | flops 4445306880 | bytes 1277952 | tf_op jit(solution)/shard_map/pallas_call | solution.py:478
  617.8 3.9 collective-permute-start.23
  622.3 65.0 %shard_map.176 = (bf16[13,32,768]{2,1,0:T(8,128)(2,1)}, bf16[13,32,768]{2,1,0:T(8,128)(2,1)}, bf16[13,32,768]{2,1,0:T(8,128)(2,1)}, bf16[13,32,768]{2,1,0:T(8,12...) custom-call(f32[1664,768]{1,0:T(8,128)} %get-tuple-element.164.refs_0_, ...), custom_call_target="tpu_custom_call" | custom-call | flops 4445306880 | bytes 1277952 | tf_op jit(solution)/shard_map/pallas_call | solution.py:478
  687.7 3.8 collective-permute-start.20
  697.6 67.7 %shard_map.177 = (f32[2,1664,768]{2,1,0:T(8,128)}, bf16[2,1664,768]{2,1,0:T(8,128)(2,1)}, f32[3,768,768]{2,1,0:T(8,128)}, f32[768,768]{1,0:T(8,128)}, f32[1,768]{1,0:T(1,128)}) custom-call(s32[1]{0:T(128)} %bitcast.refs_0_.me_ref, bf16[13,32,768]{2,1,0:T(8,128)(2,1)} %get-tuple-element.210.refs_1_, bf16[13,32,768]{2,1,0:T(8,128)(2,1)} %copy-done.12, ...), custom_call_target="tpu_custom_call" | custom-call | flops 5262458880 | bytes 1277952 | tf_op jit(solution)/shard_map/pallas_call | solution.py:478
  767.6 68.6 %shard_map.178 = (f32[2,1664,768]{2,1,0:T(8,128)}, bf16[2,1664,768]{2,1,0:T(8,128)(2,1)}, bf16[3,768,768]{2,1,0:T(8,128)(2,1)}, bf16[768,768]{1,0:T(8,128)(2,1)}, f32[1,768]{1,0:T(1,128)}) custom-call(s32[1]{0:T(128)} %bitcast.refs_0_.me_ref, bf16[13,32,768]{2,1,0:T(8,128)(2,1)} %get-tuple-element.191.refs_1_, ...), custom_call_target="tpu_custom_call", output_to_operand_aliasing={{0}: (24, {}), {1}: (25, {})} | custom-call | flops 5262458880 | bytes 1277952 | tf_op jit(solution)/shard_map/pallas_call | solution.py:478
  843.5 4.8 collective-permute-done.25
  848.3 3.0 fusion
  859.1 10.5 %collective-permute-done.26 = bf16[96,3200]{1,0:T(8,128)(2,1)} collective-permute-done((bf16[96,3200]{1,0:T(8,128)(2,1)}, bf16[96,3200]{1,0:T(8,128)(2,1)}, u32[]{:S(2)}, u32[]{:S(2)}) %collective-permute-start.26) | collective-permute-done | bytes 614432 | tf_op jit(solution)/shard_map/ppermute | solution.py:554
  869.6 13.5 %collective-permute-done.27 = bf16[96,3200]{1,0:T(8,128)(2,1)} collective-permute-done((bf16[96,3200]{1,0:T(8,128)(2,1)}, bf16[96,3200]{1,0:T(8,128)(2,1)}, u32[]{:S(2)}, u32[]{:S(2)}) %collective-permute-start.27) | collective-permute-done | bytes 614432 | tf_op jit(solution)/shard_map/ppermute | solution.py:554
  886.6 9.9 %collective-permute-start.29 = (bf16[24,3200]{1,0:T(8,128)(2,1)}, bf16[24,3200]{1,0:T(8,128)(2,1)}, u32[]{:S(2)}, u32[]{:S(2)}) collective-permute-start(bf16[24,3200]{1,0:T(8,128)(2,1)} %get-tuple-element.279), channel_id=1, source_target_pairs={{0,1},{1,0},{2,3},{3,2},{4,5},{5,4},{6,7},{7,6},{8,9},{9,8},{10,11... | collective-permute-start | bytes 460808 | tf_op jit(solution)/shard_map/ppermute | solution.py:554
  905.1 4.3 collective-permute-done.30
  (185 shorter events, 79.0 us)
Async XLA Ops:
  7.2 195.4 %all-gather.3.cloned.1.call-start = ((), (), s32[]{:S(2)}) async-start(), calls=%async_computation.4 | async-start | bytes 4866048 | tf_op jit(solution)/shard_map/all_gather | solution.py:624
  8.9 289.1 %all-gather.5.cloned.1.call-start = ((), (), s32[]{:S(2)}) async-start(), calls=%async_computation.5 | async-start | bytes 9732096 | tf_op jit(solution)/shard_map/all_gather | solution.py:625
  16.8 16.3 %collective-permute-start.1 = (bf16[24,3200]{1,0:T(8,128)(2,1)S(1)}, bf16[24,3200]{1,0:T(8,128)(2,1)S(1)}, u32[]{:S(2)}, u32[]{:S(2)}) collective-permute-start(bf16[24,3200]{1,0:T(8,128)(2,1)S(1)} %fusion.7), channel_id=1, source_target_pairs={{0,2},{1,3},{2,0},{3,1},{4,6},{5,7},{6,4},{7,5},{8,10},{9,11},{10,... | collective-permute-start | bytes 460808 | tf_op jit(solution)/shard_map/ppermute | solution.py:554
  33.1 21.1 %collective-permute-start.3 = (bf16[4,24,3200]{2,1,0:T(8,128)(2,1)S(1)}, bf16[4,24,3200]{2,1,0:T(8,128)(2,1)S(1)}, u32[]{:S(2)}, u32[]{:S(2)}) collective-permute-start(bf16[4,24,3200]{2,1,0:T(8,128)(2,1)S(1)} %bitcast_dynamic-update-slice_fusion.4), channel_id=1, source_target_pairs={{0,8},{4,12},{8,0},{12,4},{16,24},{20,28},{24,16},{28,20},{1,9},{5... | collective-permute-start | bytes 1843208 | tf_op jit(solution)/shard_map/ppermute | solution.py:554
  34.6 20.4 %collective-permute-start.4 = (bf16[4,24,3200]{2,1,0:T(8,128)(2,1)S(1)}, bf16[4,24,3200]{2,1,0:T(8,128)(2,1)S(1)}, u32[]{:S(2)}, u32[]{:S(2)}) collective-permute-start(bf16[4,24,3200]{2,1,0:T(8,128)(2,1)S(1)} %bitcast_dynamic-update-slice_fusion.4), channel_id=1, source_target_pairs={{0,16},{4,20},{8,24},{12,28},{16,0},{20,4},{24,8},{28,12},{1,17},{... | collective-permute-start | bytes 1843208 | tf_op jit(solution)/shard_map/ppermute | solution.py:554
  36.2 27.5 %collective-permute-start.5 = (bf16[4,24,3200]{2,1,0:T(8,128)(2,1)S(1)}, bf16[4,24,3200]{2,1,0:T(8,128)(2,1)S(1)}, u32[]{:S(2)}, u32[]{:S(2)}) collective-permute-start(bf16[4,24,3200]{2,1,0:T(8,128)(2,1)S(1)} %bitcast_dynamic-update-slice_fusion.4), channel_id=1, source_target_pairs={{0,24},{4,28},{8,16},{12,20},{16,8},{20,12},{24,0},{28,4},{1,25},{... | collective-permute-start | bytes 1843208 | tf_op jit(solution)/shard_map/ppermute | solution.py:554
  68.4 76.4 %all-to-all-start = ((bf16[4,13,32,768]{3,2,1,0:T(8,128)(2,1)}), bf16[4,13,32,768]{3,2,1,0:T(8,128)(2,1)S(1)}, u32[]{:S(2)}, u32[]{:S(2)}) async-start(bf16[4,13,32,768]{3,2,1,0:T(8,128)(2,1)} %bitcast.136), calls=%async_computation | async-start | bytes 5111808 | tf_op jit(solution)/shard_map/all_to_all | solution.py:619
  133.5 65.6 %collective-permute-start.7 = (bf16[13,32,768]{2,1,0:T(8,128)(2,1)}, bf16[13,32,768]{2,1,0:T(8,128)(2,1)S(1)}, u32[]{:S(2)}, u32[]{:S(2)}) collective-permute-start(bf16[13,32,768]{2,1,0:T(8,128)(2,1)} %get-tuple-element.126), channel_id=1, source_target_pairs={{0,1},{1,0},{2,3},{3,2},{4,5},{5,4},{6,7},{7,6},{8,9},{9,8},{10,11... | collective-permute-start | bytes 1916936 | tf_op jit(solution)/shard_map/ppermute | solution.py:554
  135.6 67.0 %collective-permute-start.8 = (bf16[13,32,768]{2,1,0:T(8,128)(2,1)}, bf16[13,32,768]{2,1,0:T(8,128)(2,1)}, u32[]{:S(2)}, u32[]{:S(2)}) collective-permute-start(bf16[13,32,768]{2,1,0:T(8,128)(2,1)} %get-tuple-element.127), channel_id=1, source_target_pairs={{0,2},{1,3},{2,0},{3,1},{4,6},{5,7},{6,4},{7,5},{8,10},{9,11},{10,... | collective-permute-start | bytes 1916936 | tf_op jit(solution)/shard_map/ppermute | solution.py:554
  138.0 64.6 %collective-permute-start.9 = (bf16[13,32,768]{2,1,0:T(8,128)(2,1)}, bf16[13,32,768]{2,1,0:T(8,128)(2,1)}, u32[]{:S(2)}, u32[]{:S(2)}) collective-permute-start(bf16[13,32,768]{2,1,0:T(8,128)(2,1)} %get-tuple-element.128), channel_id=1, source_target_pairs={{0,3},{1,2},{2,1},{3,0},{4,7},{5,6},{6,5},{7,4},{8,11},{9,10},{10,... | collective-permute-start | bytes 1916936 | tf_op jit(solution)/shard_map/ppermute | solution.py:554
  197.4 61.3 %collective-permute-start.10 = (bf16[13,32,768]{2,1,0:T(8,128)(2,1)}, bf16[13,32,768]{2,1,0:T(8,128)(2,1)}, u32[]{:S(2)}, u32[]{:S(2)}) collective-permute-start(bf16[13,32,768]{2,1,0:T(8,128)(2,1)} %get-tuple-element.131), channel_id=1, source_target_pairs={{0,1},{1,0},{2,3},{3,2},{4,5},{5,4},{6,7},{7,6},{8,9},{9,8},{10,11... | collective-permute-start | bytes 1916936 | tf_op jit(solution)/shard_map/ppermute | solution.py:554
  197.5 81.1 %collective-permute-start.11 = (bf16[13,32,768]{2,1,0:T(8,128)(2,1)}, bf16[13,32,768]{2,1,0:T(8,128)(2,1)}, u32[]{:S(2)}, u32[]{:S(2)}) collective-permute-start(bf16[13,32,768]{2,1,0:T(8,128)(2,1)} %get-tuple-element.132), channel_id=1, source_target_pairs={{0,2},{1,3},{2,0},{3,1},{4,6},{5,7},{6,4},{7,5},{8,10},{9,11},{10,... | collective-permute-start | bytes 1916936 | tf_op jit(solution)/shard_map/ppermute | solution.py:554
  199.0 79.6 %collective-permute-start.12 = (bf16[13,32,768]{2,1,0:T(8,128)(2,1)}, bf16[13,32,768]{2,1,0:T(8,128)(2,1)}, u32[]{:S(2)}, u32[]{:S(2)}) collective-permute-start(bf16[13,32,768]{2,1,0:T(8,128)(2,1)} %get-tuple-element.133), channel_id=1, source_target_pairs={{0,3},{1,2},{2,1},{3,0},{4,7},{5,6},{6,5},{7,4},{8,11},{9,10},{10,... | collective-permute-start | bytes 1916936 | tf_op jit(solution)/shard_map/ppermute | solution.py:554
  280.6 112.4 %all-to-all-start.1 = ((bf16[4,13,32,768]{3,2,1,0:T(8,128)(2,1)}), bf16[4,13,32,768]{3,2,1,0:T(8,128)(2,1)S(1)}, u32[]{:S(2)}, u32[]{:S(2)}) async-start(bf16[4,13,32,768]{3,2,1,0:T(8,128)(2,1)} %bitcast.135), calls=%async_computation.1 | async-start | bytes 5111808 | tf_op jit(solution)/shard_map/all_to_all | solution.py:619
  296.1 469.2 %reduce-scatter.3.cloned.1.call-start = ((), (), s32[]{:S(2)}) async-start(), calls=%async_computation.6 | async-start | bytes 9732096 | tf_op jit(solution)/shard_map/reduce_scatter | solution.py:645
  388.1 60.3 %collective-permute-start.13 = (bf16[13,32,768]{2,1,0:T(8,128)(2,1)}, bf16[13,32,768]{2,1,0:T(8,128)(2,1)S(1)}, u32[]{:S(2)}, u32[]{:S(2)}) collective-permute-start(bf16[13,32,768]{2,1,0:T(8,128)(2,1)} %get-tuple-element.147), channel_id=1, source_target_pairs={{0,1},{1,0},{2,3},{3,2},{4,5},{5,4},{6,7},{7,6},{8,9},{9,8},{10,11... | collective-permute-start | bytes 1916936 | tf_op jit(solution)/shard_map/ppermute | solution.py:554
  390.6 57.9 %collective-permute-start.14 = (bf16[13,32,768]{2,1,0:T(8,128)(2,1)}, bf16[13,32,768]{2,1,0:T(8,128)(2,1)}, u32[]{:S(2)}, u32[]{:S(2)}) collective-permute-start(bf16[13,32,768]{2,1,0:T(8,128)(2,1)} %get-tuple-element.148), channel_id=1, source_target_pairs={{0,2},{1,3},{2,0},{3,1},{4,6},{5,7},{6,4},{7,5},{8,10},{9,11},{10,... | collective-permute-start | bytes 1916936 | tf_op jit(solution)/shard_map/ppermute | solution.py:554
  392.5 56.0 %collective-permute-start.15 = (bf16[13,32,768]{2,1,0:T(8,128)(2,1)}, bf16[13,32,768]{2,1,0:T(8,128)(2,1)}, u32[]{:S(2)}, u32[]{:S(2)}) collective-permute-start(bf16[13,32,768]{2,1,0:T(8,128)(2,1)} %get-tuple-element.149), channel_id=1, source_target_pairs={{0,3},{1,2},{2,1},{3,0},{4,7},{5,6},{6,5},{7,4},{8,11},{9,10},{10,... | collective-permute-start | bytes 1916936 | tf_op jit(solution)/shard_map/ppermute | solution.py:554
  548.4 307.7 %reduce-scatter.5.cloned.1.call-start = ((), (), s32[]{:S(2)}) async-start(), calls=%async_computation.7 | async-start | bytes 4866048 | tf_op jit(solution)/shard_map/reduce_scatter | solution.py:645
  548.6 73.1 %collective-permute-start.16 = (bf16[13,32,768]{2,1,0:T(8,128)(2,1)}, bf16[13,32,768]{2,1,0:T(8,128)(2,1)S(1)}, u32[]{:S(2)}, u32[]{:S(2)}) collective-permute-start(bf16[13,32,768]{2,1,0:T(8,128)(2,1)} %get-tuple-element.161), channel_id=1, source_target_pairs={{0,1},{1,0},{2,3},{3,2},{4,5},{5,4},{6,7},{7,6},{8,9},{9,8},{10,11... | collective-permute-start | bytes 1916936 | tf_op jit(solution)/shard_map/ppermute | solution.py:554
  549.7 72.5 %collective-permute-start.17 = (bf16[13,32,768]{2,1,0:T(8,128)(2,1)}, bf16[13,32,768]{2,1,0:T(8,128)(2,1)S(1)}, u32[]{:S(2)}, u32[]{:S(2)}) collective-permute-start(bf16[13,32,768]{2,1,0:T(8,128)(2,1)} %get-tuple-element.162), channel_id=1, source_target_pairs={{0,2},{1,3},{2,0},{3,1},{4,6},{5,7},{6,4},{7,5},{8,10},{9,11},{10,... | collective-permute-start | bytes 1916936 | tf_op jit(solution)/shard_map/ppermute | solution.py:554
  552.6 69.6 %collective-permute-start.18 = (bf16[13,32,768]{2,1,0:T(8,128)(2,1)}, bf16[13,32,768]{2,1,0:T(8,128)(2,1)S(1)}, u32[]{:S(2)}, u32[]{:S(2)}) collective-permute-start(bf16[13,32,768]{2,1,0:T(8,128)(2,1)} %get-tuple-element.163), channel_id=1, source_target_pairs={{0,3},{1,2},{2,1},{3,0},{4,7},{5,6},{6,5},{7,4},{8,11},{9,10},{10,... | collective-permute-start | bytes 1916936 | tf_op jit(solution)/shard_map/ppermute | solution.py:554
  617.7 76.0 %collective-permute-start.22 = (bf16[13,32,768]{2,1,0:T(8,128)(2,1)}, bf16[13,32,768]{2,1,0:T(8,128)(2,1)S(1)}, u32[]{:S(2)}, u32[]{:S(2)}) collective-permute-start(bf16[13,32,768]{2,1,0:T(8,128)(2,1)} %get-tuple-element.206), channel_id=1, source_target_pairs={{0,1},{1,0},{2,3},{3,2},{4,5},{5,4},{6,7},{7,6},{8,9},{9,8},{10,11... | collective-permute-start | bytes 1916936 | tf_op jit(solution)/shard_map/ppermute | solution.py:554
  617.8 79.0 %collective-permute-start.23 = (bf16[13,32,768]{2,1,0:T(8,128)(2,1)}, bf16[13,32,768]{2,1,0:T(8,128)(2,1)S(1)}, u32[]{:S(2)}, u32[]{:S(2)}) collective-permute-start(bf16[13,32,768]{2,1,0:T(8,128)(2,1)} %get-tuple-element.207), channel_id=1, source_target_pairs={{0,2},{1,3},{2,0},{3,1},{4,6},{5,7},{6,4},{7,5},{8,10},{9,11},{10,... | collective-permute-start | bytes 1916936 | tf_op jit(solution)/shard_map/ppermute | solution.py:554
  621.8 75.0 %collective-permute-start.24 = (bf16[13,32,768]{2,1,0:T(8,128)(2,1)}, bf16[13,32,768]{2,1,0:T(8,128)(2,1)}, u32[]{:S(2)}, u32[]{:S(2)}) collective-permute-start(bf16[13,32,768]{2,1,0:T(8,128)(2,1)} %get-tuple-element.208), channel_id=1, source_target_pairs={{0,3},{1,2},{2,1},{3,0},{4,7},{5,6},{6,5},{7,4},{8,11},{9,10},{10,... | collective-permute-start | bytes 1916936 | tf_op jit(solution)/shard_map/ppermute | solution.py:554
  687.4 78.9 %collective-permute-start.19 = (bf16[13,32,768]{2,1,0:T(8,128)(2,1)}, bf16[13,32,768]{2,1,0:T(8,128)(2,1)S(1)}, u32[]{:S(2)}, u32[]{:S(2)}) collective-permute-start(bf16[13,32,768]{2,1,0:T(8,128)(2,1)} %get-tuple-element.186), channel_id=1, source_target_pairs={{0,1},{1,0},{2,3},{3,2},{4,5},{5,4},{6,7},{7,6},{8,9},{9,8},{10,11... | collective-permute-start | bytes 1916936 | tf_op jit(solution)/shard_map/ppermute | solution.py:554
  687.7 78.6 %collective-permute-start.20 = (bf16[13,32,768]{2,1,0:T(8,128)(2,1)}, bf16[13,32,768]{2,1,0:T(8,128)(2,1)S(1)}, u32[]{:S(2)}, u32[]{:S(2)}) collective-permute-start(bf16[13,32,768]{2,1,0:T(8,128)(2,1)} %get-tuple-element.187), channel_id=1, source_target_pairs={{0,2},{1,3},{2,0},{3,1},{4,6},{5,7},{6,4},{7,5},{8,10},{9,11},{10,... | collective-permute-start | bytes 1916936 | tf_op jit(solution)/shard_map/ppermute | solution.py:554
  693.8 72.5 %collective-permute-start.21 = (bf16[13,32,768]{2,1,0:T(8,128)(2,1)}, bf16[13,32,768]{2,1,0:T(8,128)(2,1)S(1)}, u32[]{:S(2)}, u32[]{:S(2)}) collective-permute-start(bf16[13,32,768]{2,1,0:T(8,128)(2,1)} %get-tuple-element.188), channel_id=1, source_target_pairs={{0,3},{1,2},{2,1},{3,0},{4,7},{5,6},{6,5},{7,4},{8,11},{9,10},{10,... | collective-permute-start | bytes 1916936 | tf_op jit(solution)/shard_map/ppermute | solution.py:554
  852.6 17.0 %collective-permute-start.26 = (bf16[96,3200]{1,0:T(8,128)(2,1)}, bf16[96,3200]{1,0:T(8,128)(2,1)}, u32[]{:S(2)}, u32[]{:S(2)}) collective-permute-start(bf16[96,3200]{1,0:T(8,128)(2,1)} %get-tuple-element.276), channel_id=1, source_target_pairs={{0,8},{4,12},{8,0},{12,4},{16,24},{20,28},{24,16},{28,20},{1,9},{5... | collective-permute-start | bytes 1843208 | tf_op jit(solution)/shard_map/ppermute | solution.py:554
  854.1 29.1 %collective-permute-start.27 = (bf16[96,3200]{1,0:T(8,128)(2,1)}, bf16[96,3200]{1,0:T(8,128)(2,1)}, u32[]{:S(2)}, u32[]{:S(2)}) collective-permute-start(bf16[96,3200]{1,0:T(8,128)(2,1)} %get-tuple-element.278), channel_id=1, source_target_pairs={{0,16},{4,20},{8,24},{12,28},{16,0},{20,4},{24,8},{28,12},{1,17},{... | collective-permute-start | bytes 1843208 | tf_op jit(solution)/shard_map/ppermute | solution.py:554
  854.4 28.8 %collective-permute-start.28 = (bf16[96,3200]{1,0:T(8,128)(2,1)}, bf16[96,3200]{1,0:T(8,128)(2,1)}, u32[]{:S(2)}, u32[]{:S(2)}) collective-permute-start(bf16[96,3200]{1,0:T(8,128)(2,1)} %get-tuple-element.277), channel_id=1, source_target_pairs={{0,24},{4,28},{8,16},{12,20},{16,8},{20,12},{24,0},{28,4},{1,25},{... | collective-permute-start | bytes 1843208 | tf_op jit(solution)/shard_map/ppermute | solution.py:554
  886.6 18.6 %collective-permute-start.29 = (bf16[24,3200]{1,0:T(8,128)(2,1)}, bf16[24,3200]{1,0:T(8,128)(2,1)}, u32[]{:S(2)}, u32[]{:S(2)}) collective-permute-start(bf16[24,3200]{1,0:T(8,128)(2,1)} %get-tuple-element.279), channel_id=1, source_target_pairs={{0,1},{1,0},{2,3},{3,2},{4,5},{5,4},{6,7},{7,6},{8,9},{9,8},{10,11... | collective-permute-start | bytes 460808 | tf_op jit(solution)/shard_map/ppermute | solution.py:554
  (32 other events, 732.7 us)
Sparse Core Ops, SparseCore 0:
  11.4 89.8 all-gather.2
  104.6 169.5 all-gather.4
  548.5 164.3 reduce-scatter.2
  719.2 132.0 reduce-scatter.4

commit v3 on v2

--- a/solution.py
+++ b/solution.py
@@ -13,8 +13,9 @@
 EPSILON = 1e-06
 LOW = jnp.bfloat16
 F32 = jnp.float32
-VMEM_LIMIT = 60 * 1024 * 1024
+VMEM_LIMIT = 62 * 1024 * 1024
 COST_SHARE = 10
+EARLY = 3
 GELU_A = 0.7978845608028654
 GELU_B = 0.044715
 
@@ -44,6 +45,29 @@
         body(pl.ds(pl.multiple_of(step * size, size), size))
 
 
+def loop_tiles(tiles, tile, joint, body):
+    def spots(first, count):
+        found = []
+        for t in range(count):
+            for pair in range(2):
+                start = pl.multiple_of((first + t) * tile, tile)
+                kept = pl.multiple_of(((first + t) * 2 + pair) * 2 * tile, 2 * tile)
+                found.append((pl.ds(start, tile), pl.ds(pair * PAIR, PAIR), pl.ds(kept, 2 * tile)))
+        return found
+
+    joint = min(joint, tiles)
+
+    @pl.loop(0, tiles // joint)
+    def _(step):
+        body(spots(step * joint, joint))
+    if tiles % joint:
+        body(spots(tiles - tiles % joint, tiles % joint))
+
+
+TILES_FWD_SPACE, TILES_FWD_TIME, TILES_BWD_SPACE, TILES_BWD_TIME = 8, 13, 8, 13
+SMALL, UNROLL_PIECES, UNROLL_SPANS = 208, 16, 2
+
+
 def normalise(v):
     centered = v - jnp.mean(v, axis=-1, keepdims=True)
     spread = jnp.mean(centered * centered, axis=-1, keepdims=True)
@@ -83,7 +107,7 @@
     for at, piece_ref in enumerate(pieces):
         starts = plan.starts(lax.bitwise_xor(me, at))
 
-        @pl.loop(0, plan.groups)
+        @pl.loop(0, plan.groups, unroll=min(UNROLL_PIECES, plan.groups))
         def _(group):
             for low in range(0, plan.frames, plan.joint):
                 rows = [source_ref[pl.ds(pl.multiple_of(starts[low + more] + group * plan.group, plan.group), plan.group), :] for more in range(plan.joint)]
@@ -94,7 +118,7 @@
     for at, piece_ref in enumerate(pieces):
         starts = plan.starts(lax.bitwise_xor(me, at))
 
-        @pl.loop(0, plan.groups)
+        @pl.loop(0, plan.groups, unroll=min(UNROLL_PIECES, plan.groups))
         def _(group):
             for low in range(0, plan.frames, plan.joint):
                 rows = piece_ref[group, pl.ds(low * plan.group, 16), :].astype(F32)
@@ -150,7 +174,7 @@
     step, steps = pl.program_id(0), pl.num_programs(0)
     rows = n_ref.shape[0]
     rb = row_block(rows)
-    small = row_block(rows, 64)
+    small = row_block(rows, SMALL)
 
     @pl.when(step == 0)
     def _():
@@ -164,7 +188,7 @@
         if space:
             loop_rows(rows, small, lambda at: take(at, x_ref[at, :]))
         else:
-            @pl.loop(0, plan.groups)
+            @pl.loop(0, plan.groups, unroll=min(UNROLL_SPANS, plan.groups))
             def _(group):
                 for k, piece_ref in enumerate(pieces):
                     take(pl.ds(pl.multiple_of(group * tile + k * plan.span, 16), plan.span), piece_ref[group])
@@ -177,17 +201,15 @@
         v_ref[at, :] = dot(n, wv_ref[...]).astype(LOW)
     loop_rows(rows, rb, project)
 
-    @pl.loop(0, rows // tile)
-    def _(t):
-        at = pl.ds(pl.multiple_of(t * tile, tile), tile)
-        for pair in range(2):
-            cols = pl.ds(pair * PAIR, PAIR)
-            qs = spread_pair(q_ref[at, cols])
-            s = dot_nt(qs, k_ref[at, cols]) + bias_ref[...]
-            e = jnp.exp(s - jnp.max(s, axis=-1, keepdims=True))
-            p = (e * (1.0 / jnp.sum(e, axis=-1, keepdims=True))).astype(LOW)
-            p_ref[0, pl.ds(pl.multiple_of((t * 2 + pair) * 2 * tile, 2 * tile), 2 * tile), :] = p
-            att_ref[at, cols] = join_pair(dot(p, v_ref[at, cols])).astype(LOW)
+    def attend(spots):
+        scores = [dot_nt(spread_pair(q_ref[at, cols]), k_ref[at, cols]) + bias_ref[...] for at, cols, _ in spots]
+        scores = [jnp.exp(score - jnp.max(score, axis=-1, keepdims=True)) for score in scores]
+        scores = [(score * (1.0 / jnp.sum(score, axis=-1, keepdims=True))).astype(LOW) for score in scores]
+        results = [dot(score, v_ref[at, cols]) for score, (at, cols, _) in zip(scores, spots)]
+        for score, result, (at, cols, kept) in zip(scores, results, spots):
+            p_ref[0, kept, :] = score
+            att_ref[at, cols] = join_pair(result).astype(LOW)
+    loop_tiles(rows // tile, tile, TILES_FWD_SPACE if space else TILES_FWD_TIME, attend)
 
     def project_out(at):
         acc_ref[at, :] += dot(att_ref[at, :], wo_ref[...])
@@ -201,11 +223,13 @@
             out_ref[...] = acc_ref[...]
 
 
-def attend_bwd(plan, space, prior, again, *refs):
+def attend_bwd(plan, space, prior, again, deliver, *refs):
     parts = plan.parts
     if space:
         tile = plan.slots
-        me_ref, g_pieces, done_pieces, x_ref, refs = refs[0], refs[1:1 + parts], refs[1 + parts:1 + 2 * parts], refs[1 + 2 * parts].at[0], refs[2 + 2 * parts:]
+        me_ref, g_pieces, x_ref, refs = refs[0], refs[1:1 + parts], refs[1 + parts].at[0], refs[2 + parts:]
+        if deliver:
+            done_pieces, refs = refs[:parts], refs[parts:]
     else:
         tile = plan.tile_time
         g_ref, x_pieces, refs = refs[0], refs[1:1 + parts], refs[1 + parts:]
@@ -215,16 +239,18 @@
         old_ref, oldo_ref, oldg_ref = refs[:3]
         refs = refs[3:]
     if again:
-        refs = refs[2:]
+        refs = refs[1:]
     if space:
-        gx_ref, done_ref, refs = refs[0].at[0], refs[1].at[0], refs[2:]
+        gx_ref, refs = refs[0].at[0], refs[1:]
+        if deliver:
+            done_ref, refs = refs[0].at[0], refs[1:]
     else:
         out_pieces, refs = refs[:parts], refs[parts:]
     dw_ref, dwo_ref, dgain_ref, low_ref, do_ref, dq_ref, dk_ref, dv_ref, acc_ref, gain_ref = refs
     step, steps = pl.program_id(0), pl.num_programs(0)
     rows, width = acc_ref.shape
     rb = row_block(rows)
-    small = row_block(rows, 64)
+    small = row_block(rows, SMALL)
 
     @pl.when(step == 0)
     def _():
@@ -247,19 +273,21 @@
         total += oldo_ref[...]
     dwo_ref[...] = total.astype(dwo_ref.dtype)
 
-    @pl.loop(0, rows // tile)
-    def _(t):
-        at = pl.ds(pl.multiple_of(t * tile, tile), tile)
-        for pair in range(2):
-            cols = pl.ds(pair * PAIR, PAIR)
-            dos = spread_pair(do_ref[at, cols])
-            att = att_ref[at, cols].astype(F32)
-            inner = jnp.sum(dos.astype(F32) * jnp.concatenate([att, att], axis=0), axis=-1, keepdims=True)
-            p = p_ref[0, pl.ds(pl.multiple_of((t * 2 + pair) * 2 * tile, 2 * tile), 2 * tile), :]
-            ds = (p.astype(F32) * (dot_nt(dos, v_ref[at, cols]) - inner)).astype(LOW)
-            dq_ref[at, cols] = (join_pair(dot(ds, k_ref[at, cols])) * (HEAD_DIM ** -0.5)).astype(LOW)
-            dk_ref[at, cols] = dot_tn(ds, spread_pair(q_ref[at, cols])).astype(LOW)
-            dv_ref[at, cols] = dot_tn(p, dos).astype(LOW)
+    def attend(spots):
+        outs = [spread_pair(do_ref[at, cols]) for at, cols, _ in spots]
+        atts = [att_ref[at, cols].astype(F32) for at, cols, _ in spots]
+        inners = [jnp.sum(out.astype(F32) * jnp.concatenate([att, att], axis=0), axis=-1, keepdims=True) for out, att in zip(outs, atts)]
+        probs = [p_ref[0, kept, :] for _, _, kept in spots]
+        values = [dot_tn(prob, out).astype(LOW) for prob, out in zip(probs, outs)]
+        scores = [dot_nt(out, v_ref[at, cols]) for out, (at, cols, _) in zip(outs, spots)]
+        scores = [(prob.astype(F32) * (score - inner)).astype(LOW) for prob, score, inner in zip(probs, scores, inners)]
+        queries = [(join_pair(dot(score, k_ref[at, cols])) * (HEAD_DIM ** -0.5)).astype(LOW) for score, (at, cols, _) in zip(scores, spots)]
+        keys = [dot_tn(score, spread_pair(q_ref[at, cols])).astype(LOW) for score, (at, cols, _) in zip(scores, spots)]
+        for query, key, value, (at, cols, _) in zip(queries, keys, values, spots):
+            dq_ref[at, cols] = query
+            dk_ref[at, cols] = key
+            dv_ref[at, cols] = value
+    loop_tiles(rows // tile, tile, TILES_BWD_SPACE if space else TILES_BWD_TIME, attend)
 
     def back_in(at):
         part = dot_nt(dq_ref[at, :], wq_ref[...]) + dot_nt(dk_ref[at, :], wk_ref[...]) + dot_nt(dv_ref[at, :], wv_ref[...])
@@ -291,13 +319,14 @@
                 dgain_ref[...] += gains
                 gx_ref[at, :] += back
             loop_rows(rows, small, finish)
-            load_pieces(me_ref[0], done_pieces, acc_ref, plan)
-
-            def lower(at):
-                done_ref[at, :] = acc_ref[at, :].astype(LOW)
-            loop_rows(rows, small, lower)
+            if deliver:
+                load_pieces(me_ref[0], done_pieces, acc_ref, plan)
+
+                def lower(at):
+                    done_ref[at, :] = acc_ref[at, :].astype(LOW)
+                loop_rows(rows, small, lower)
         else:
-            @pl.loop(0, plan.groups)
+            @pl.loop(0, plan.groups, unroll=min(UNROLL_SPANS, plan.groups))
             def _(group):
                 for k in range(parts):
                     at = pl.ds(pl.multiple_of(group * tile + k * plan.span, 16), plan.span)
@@ -306,8 +335,9 @@
                     out_pieces[k][group] = (g_ref[at, :] + back).astype(LOW)
 
 
-def mlp_both(plan, prior, me_ref, second_ref, cot_ref, *refs):
+def mlp_both(plan, prior, second_ref, *refs):
     parts = plan.parts
+    cot_pieces, refs = refs[:parts], refs[parts:]
     keep_ref, gains_ref, w1_ref, w2_ref = refs[:4]
     refs = refs[4:]
     if prior:
@@ -318,10 +348,10 @@
     acc_ref = grad_ref
     step, steps = pl.program_id(0), pl.num_programs(0)
     rows = second_ref.shape[0]
-    rb = row_block(rows, 256)
+    rb = row_block(rows)
 
     def each_span(body):
-        @pl.loop(0, plan.groups)
+        @pl.loop(0, plan.groups, unroll=min(UNROLL_SPANS, plan.groups))
         def _(group):
             for k in range(parts):
                 body(group, k, pl.ds(pl.multiple_of(group * plan.tile_time + k * plan.span, 16), plan.span))
@@ -333,7 +363,7 @@
         def start(group, k, at):
             v = second_ref[at, :]
             n_ref[at, :] = (normalise(v)[0] * gain_ref[...]).astype(LOW)
-            up_ref[at, :] = (cot_ref[lax.bitwise_xor(me_ref[0], k), group].astype(F32) * keep_ref[at, :]).astype(LOW)
+            up_ref[at, :] = (cot_pieces[k][group].astype(F32) * keep_ref[at, :]).astype(LOW)
             sum_ref[at, :] = v
             acc_ref[at, :] = jnp.zeros_like(v)
         each_span(start)
@@ -458,10 +488,11 @@
     cost = pl.CostEstimate(flops=rows * 4 // COST_SHARE * width * (8 * width + 20 * tile), bytes_accessed=rows * width, transcendentals=0)
     weight_out = [pl.BlockSpec((3, width, QUAD), lambda i: (0, 0, i)), spec_rows((QUAD, width)), whole((1, width))]
     token = whole((rows, width))
-    lead_specs = [scalar()] + piece_specs(plan, width) * 2 + [whole((1, rows, width), (micro, 0, 0))] if space else [token] + piece_specs(plan, width)
+    deliver = space and micro + 1 < micros
+    lead_specs = [scalar()] + piece_specs(plan, width) + [whole((1, rows, width), (micro, 0, 0))] + (piece_specs(plan, width) if deliver else []) if space else [token] + piece_specs(plan, width)
     if space:
-        out_specs = [whole((1, rows, width), (micro, 0, 0))] * 2
-        out_shape = [jax.ShapeDtypeStruct((micros, rows, width), F32), jax.ShapeDtypeStruct((micros, rows, width), LOW)]
+        out_specs = [whole((1, rows, width), (micro, 0, 0))] * (1 + deliver)
+        out_shape = [jax.ShapeDtypeStruct((micros, rows, width), kind) for kind in ((F32, LOW) if deliver else (F32,))]
     else:
         out_specs, out_shape = piece_specs(plan, width), piece_shapes(plan, width)
     operands = [*lead, gain, *saved, weights, weights, weights, weights]
@@ -472,11 +503,11 @@
         in_specs = in_specs + weight_out
     aliases = {}
     if shared is not None:
-        aliases = {len(operands): 0, len(operands) + 1: 1}
-        operands += shared
-        in_specs = in_specs + [pl.BlockSpec(memory_space=pl.ANY)] * 2
+        aliases = {len(operands): 0}
+        operands += shared[:1]
+        in_specs = in_specs + [pl.BlockSpec(memory_space=pl.ANY)]
     result = pl.pallas_call(
-        functools.partial(attend_bwd, plan, space, old is not None, shared is not None),
+        functools.partial(attend_bwd, plan, space, old is not None, shared is not None, deliver),
         grid=(quads,),
         in_specs=in_specs,
         out_specs=out_specs + weight_out,
@@ -494,7 +525,7 @@
 UNITS = 256
 
 
-def run_mlp(plan, me, second, cot, keep, gain, weights, last, old=None):
+def run_mlp(plan, second, cots, keep, gain, weights, last, old=None):
     rows, width = second.shape
     hidden = weights.shape[1] // 2
     steps = hidden // FF_TILE
@@ -510,7 +541,7 @@
     result = pl.pallas_call(
         functools.partial(mlp_both, plan, old is not None),
         grid=(steps,),
-        in_specs=[scalar(), token, whole(cot.shape), whole((rows, 1)), gains_spec(gain),
+        in_specs=[token] + piece_specs(plan, width) + [whole((rows, 1)), gains_spec(gain),
                   spec_cols((width, FF_TILE)), second_spec(hidden)] + ([] if old is None else weight_out),
         out_specs=piece_specs(plan, width) + [token] + weight_out,
         out_shape=piece_shapes(plan, width) + [jax.ShapeDtypeStruct((rows, width), F32),
@@ -521,7 +552,7 @@
                         pltpu.VMEM((rows, FF_TILE), LOW), pltpu.VMEM((rows, FF_TILE), LOW), pltpu.VMEM((1, width), F32)],
         compiler_params=params(),
         cost_estimate=cost,
-    )(me, second, cot, keep, gain, weights, weights, *([] if old is None else old))
+    )(second, *cots, keep, gain, weights, weights, *([] if old is None else old))
     return list(result[:plan.parts]), result[plan.parts], list(result[plan.parts + 1:])
 
 
@@ -579,15 +610,11 @@
     return total
 
 
-def gather_rows(v, dp, seq):
-    rows, width = v.shape
-    device, place = lax.axis_index("dp"), lax.axis_index("seq")
-    v = collect(v, "seq", seq, place)
-    v = collect(v, "dp", dp // 2, device // 2, 2)
+def join_cores(v, dp):
     other = swap(v, "dp", dp, 1)
-    core = (device % 2) == 0
+    core = (lax.axis_index("dp") % 2) == 0
     v = jnp.stack([jnp.where(core, v, other), jnp.where(core, other, v)], axis=1)
-    return v.reshape(dp * seq * rows, width)
+    return v.reshape(-1, v.shape[-1])
 
 
 def scatter_rows(v, dp, seq):
@@ -603,7 +630,6 @@
 
 
 def shards(dp, seq, frames_in, qkv_spatial, out_spatial, qkv_temporal, out_temporal, mlp_in, mlp_out, gains, place_mask, cotangent):
-    both = ("dp", "seq")
     micros, clips, local_frames, slots, width = frames_in.shape
     hidden = mlp_in.shape[1]
     plan = Plan(seq, clips, local_frames, slots)
@@ -613,17 +639,19 @@
     units = Units(dp * seq, width, hidden)
     after = lax.optimization_barrier
 
-    def send_cot(v):
+    def cot_pieces(v):
         v = plan.fill(v).transpose(0, 2, 1, 3, 4).reshape(seq, local_frames, plan.groups, plan.group, width)
-        v = v.transpose(0, 2, 1, 3, 4).reshape(seq, plan.groups, plan.span, width)
-        return lax.all_to_all(v, "seq", split_axis=0, concat_axis=0, tiled=True)
+        return [pick(v, lax.bitwise_xor(place, at)).transpose(1, 0, 2, 3).reshape(plan.groups, plan.span, width) for at in range(seq)]
 
     padded_gains = jnp.pad(gains, ((0, 0), (0, LANES - gains.shape[1])))
-    cots = [send_cot(cotangent[0])]
-    space = gather_rows(jnp.concatenate([qkv_spatial, out_spatial, padded_gains], axis=1), dp, seq)
-    time = lax.all_gather(jnp.concatenate([qkv_temporal, out_temporal], axis=1), both, axis=0, tiled=True)
-    mlp = lax.all_gather(jnp.concatenate([units.first_in(mlp_in), units.second_in(mlp_out)], axis=1), both, axis=0, tiled=True)
-
+    space = jnp.concatenate([qkv_spatial, out_spatial, padded_gains], axis=1)
+    rest = lax.all_gather(jnp.concatenate([qkv_temporal, out_temporal, units.first_in(mlp_in), units.second_in(mlp_out)], axis=1), "seq", axis=0, tiled=True)
+    cots = [exchange(cot_pieces(cotangent[0]))]
+    space = collect(space, "seq", seq, place)
+    device = lax.axis_index("dp")
+    space = collect(space, "dp", dp // 2, device // 2, 2)
+    space, cots[0][:EARLY] = after((space, cots[0][:EARLY]))
+    space = join_cores(space, dp)
     bias_space = jnp.where(place_mask > 0, 0.0, -1000000000.0).astype(F32).reshape(plan.per_clip, plan.places)
     bias_space = jnp.pad(bias_space, ((0, 0), (0, plan.room - plan.places)), constant_values=-1000000000.0).reshape(1, plan.slots)
     spot = jnp.arange(plan.tile_time) % plan.group
@@ -640,45 +668,64 @@
         space_saved.append(saved)
         across.append(exchange(out))
         if m == 0:
+            rest, _ = after((rest, out[0]))
+            time = lax.all_gather(rest[:, :4 * width], "dp", axis=0, tiled=True)
+            mlp = lax.all_gather(rest[:, 4 * width:], "dp", axis=0, tiled=True)
             me, cots[0] = after((me, cots[0]))
+
     def scatter(parts):
-        return lax.psum_scatter(jnp.concatenate(parts, axis=1), both, scatter_dimension=0, tiled=True).astype(F32)
+        v = lax.psum_scatter(jnp.concatenate(parts, axis=1), "dp", scatter_dimension=0, tiled=True)
+        return reduce_blocks(v.reshape(seq, v.shape[0] // seq, -1), "seq", seq, place)
 
     def attend_parts(old):
         return [old[0][0], old[0][1], old[0][2], old[1]]
 
     done, afters, time_saved, grads = [], [], [], []
     old_mlp = old_time = old_space = shared = None
+    outs = []
     for m in range(micros):
         (second,), saved = run_attend_fwd(plan, False, m, across[m], space, bias_time, time)
         time_saved.append(saved)
         if m > 0:
-            second, done[m - 1] = after((second, done[m - 1]))
+            second, outs[m - 1] = after((second, outs[m - 1]))
+            done.append(exchange(outs[m - 1]))
         if m + 1 < micros:
-            second, across, cot = after((second, across, cotangent[m + 1]))
-            cots.append(send_cot(cot))
-            across[m + 1], cots[m + 1] = after((across[m + 1], cots[m + 1]))
-        out, grad, old_mlp = run_mlp(plan, me, second, cots[m], keep, space, mlp, m == micros - 1, old_mlp)
-        done.append(exchange(out))
+            second, across[m + 1], cot = after((second, across[m + 1], cotangent[m + 1]))
+            cots.append(exchange(cot_pieces(cot)))
+        out, grad, old_mlp = run_mlp(plan, second, cots[m], keep, space, mlp, m == micros - 1, old_mlp)
+        outs.append(out)
         grads.append(grad)
+        if m + 1 < micros:
+            across[m + 1], cots[m + 1], old_mlp[2] = after((across[m + 1], cots[m + 1], old_mlp[2]))
+    old_mlp, done = after((old_mlp, done))
     owned_mlp = scatter(old_mlp[:2])
     for m in range(micros):
-        grads[m], old_mlp[2] = after((grads[m], old_mlp[2]))
-        if m > 0:
-            grads[m], done[-1] = after((grads[m], done[-1]))
+        grads[m], old_mlp[2], done = after((grads[m], old_mlp[2], done))
         back, old_time = run_attend_bwd(plan, False, [grads[m], *across[m]], space, time_saved[m], time, m, micros, old_time)
         afters.append(exchange(back))
+    old_time, afters[0] = after((old_time, afters[0]))
     owned_time = scatter(attend_parts(old_time))
-    afters[0], old_time[2] = after((afters[0], old_time[2]))
     for m in range(micros):
         if m == micros - 1:
             afters[m], owned_mlp = after((afters[m], owned_mlp))
-        shared, old_space = run_attend_bwd(plan, True, [me, *afters[m], *done[m], inputs], space, space_saved[m], space, m, micros, old_space, shared)
+        result, old_space = run_attend_bwd(plan, True, [me, *afters[m], inputs] + (done[m] if m + 1 < micros else []), space, space_saved[m], space, m, micros, old_space, shared)
+        shared = result + (shared or [])[1:]
+        if m + 1 == micros - 1:
+            old_space[2], outs[-1] = after((old_space[2], outs[-1]))
+            final = exchange(outs[-1])
+
+    old_space, final = after((old_space, final))
+    final = jnp.stack(final).reshape(seq, plan.groups, local_frames, plan.group, width).transpose(0, 2, 1, 3, 4)
+    for at in range(seq.bit_length() - 1):
+        final = final.reshape(seq >> (at + 1), 2, 1 << at, local_frames, plan.room, width)
+        final = jnp.where(((place >> at) & 1) == 1, final[:, ::-1], final)
+    final = final.reshape(clips, plan.per_clip, local_frames, plan.room, width).transpose(0, 2, 1, 3, 4).reshape(plan.rows, width)
+    frames_out = lax.dynamic_update_index_in_dim(shared[1], final, micros - 1, 0)
 
     gain_grads = jnp.concatenate([old_space[2], old_time[2], old_mlp[2]], axis=0).T.astype(LOW)
     owned = scatter_rows(jnp.concatenate(attend_parts(old_space) + [jnp.pad(gain_grads, ((0, 0), (0, LANES - gain_grads.shape[1])))], axis=1), dp, seq)
     return (
-        plan.strip(shared[1], (micros, clips)),
+        plan.strip(frames_out, (micros, clips)),
         plan.strip(shared[0], (micros, clips)),
         owned[:, :3 * width],
         owned[:, 3 * width:4 * width],

time: 924 us -> 836 us (0.905)
  Pallas kernels: 662 us -> 474 us
  starting transfers between devices: 76.4 us -> 124 us
  local copies, waits for them, and re-layouts: 41.1 us -> 68.7 us
  waiting for transfers between devices: 96.2 us -> 114 us
    pallas_call x4, Pallas kernels: 215 us -> 121 us  [run_attend_fwd(): pl.pallas_call(functools.partial(attend_fwd, plan, space), grid=(quads,),...]
    ppermute x32 -> x44, starting transfers between devices: 52.5 us -> 124 us  [swap(): return lax.ppermute(v, axis, [(i, i ^ by) for i in range(size)])]
    pallas_call x4, Pallas kernels: 266 us -> 196 us  [run_attend_bwd(): pl.pallas_call(functools.partial(attend_bwd, plan, space, old is not None...]
    pallas_call x2, Pallas kernels: 181 us -> 156 us  [run_mlp(): pl.pallas_call(functools.partial(mlp_both, plan, old is not None), grid=(...]
    ppermute x32 -> x44, waiting for transfers between devices: 89.4 us -> 113 us  [swap(): return lax.ppermute(v, axis, [(i, i ^ by) for i in range(size)])]
    all_to_all x2 -> x0, starting transfers between devices: 23.1 us -> none  [send_cot(): return lax.all_to_all(v, 'seq', split_axis=0, concat_axis=0, tiled=True)]
  transfers between devices with their start and end apart: 38 -> 49, of which waited for: 10 -> 12; matrix products, arithmetic and copies ran while one was open for 5% -> 9% of each run, Pallas kernels for 62% -> 54%
where the time goes in v3:
time: 836 us; the launch traced here: 827 us
  Pallas kernels  474 us (57%)
  starting transfers between devices  124 us (15%)
  waiting for transfers between devices  114 us (14%)
  local copies, waits for them, and re-layouts  68.7 us (8%)
  other arithmetic  30.6 us (4%)
  between operations  14.9 us (2%)
    pallas_call x4, Pallas kernels, run_attend_bwd(): pl.pallas_call(functools.partial(attend_bwd, plan, space, old is not None...  196 us
    pallas_call x2, Pallas kernels, run_mlp(): pl.pallas_call(functools.partial(mlp_both, plan, old is not None), grid=(...  156 us
    ppermute x44, starting transfers between devices, swap(): return lax.ppermute(v, axis, [(i, i ^ by) for i in range(size)])  124 us
    pallas_call x4, Pallas kernels, run_attend_fwd(): pl.pallas_call(functools.partial(attend_fwd, plan, space), grid=(quads,),...  121 us
    ppermute x44, waiting for transfers between devices, swap(): return lax.ppermute(v, axis, [(i, i ^ by) for i in range(size)])  113 us
  transfers between devices with their start and end apart: 49, of which 12 were waited for; matrix products, arithmetic and copies ran while one was open for 9% of the time, Pallas kernels for 54%

profile of v3, /device:TPU:0, one launch (start us, length us, event | category | flops | bytes accessed | tf_op | source)
XLA Modules:
  0.0 826.7 jit_solution(9469022561036078627)
XLA Ops:
  8.9 3.1 collective-permute-start
  14.6 4.3 slice_bitcast_fusion
  22.9 3.5 collective-permute-start.7
  37.5 12.2 %collective-permute-done.3 = bf16[4,24,3200]{2,1,0:T(8,128)(2,1)S(1)} collective-permute-done((bf16[4,24,3200]{2,1,0:T(8,128)(2,1)}, bf16[4,24,3200]{2,1,0:T(8,128)(2,1)S(1)}, u32[]{:S(2)}, u32[]{:S(2)}) %collective-permute-start.3) | collective-permute-done | bytes 614432 | tf_op jit(solution)/shard_map/ppermute | solution.py:585
  49.7 11.7 %collective-permute-done.4 = bf16[4,24,3200]{2,1,0:T(8,128)(2,1)S(1)} collective-permute-done((bf16[4,24,3200]{2,1,0:T(8,128)(2,1)}, bf16[4,24,3200]{2,1,0:T(8,128)(2,1)S(1)}, u32[]{:S(2)}, u32[]{:S(2)}) %collective-permute-start.4) | collective-permute-done | bytes 614432 | tf_op jit(solution)/shard_map/ppermute | solution.py:585
  73.0 31.4 %shard_map.169 = (bf16[13,32,768]{2,1,0:T(8,128)(2,1)}, bf16[13,32,768]{2,1,0:T(8,128)(2,1)}, bf16[13,32,768]{2,1,0:T(8,128)(2,1)}, bf16[13,32,768]{2,1,0:T(8,12...) custom-call(s32[1]{0:T(128)} %bitcast.refs_0_, ...), custom_call_target="tpu_custom_call" | custom-call | flops 2418769920 | bytes 1277952 | tf_op jit(solution)/shard_map/pallas_call | solution.py:467
  111.0 17.2 %collective-permute-done.8.refs_3_ = bf16[13,32,768]{2,1,0:T(8,128)(2,1)S(1)} collective-permute-done((bf16[13,32,768]{2,1,0:T(8,128)(2,1)S(1)}, bf16[13,32,768]{2,1,0:T(8,128)(2,1)S(1)}, u32[]{:S(2)}, u32[]{:S(2)}) %collective-permute-start.8) | collective-permute-done | bytes 639008 | tf_op jit(solution)/shard_map/ppermute | solution.py:585
  128.2 12.0 %collective-permute-start.11 = (bf16[13,32,768]{2,1,0:T(8,128)(2,1)}, bf16[13,32,768]{2,1,0:T(8,128)(2,1)S(1)}, u32[]{:S(2)}, u32[]{:S(2)}) collective-permute-start(bf16[13,32,768]{2,1,0:T(8,128)(2,1)} %get-tuple-element.162), channel_id=1, source_target_pairs={{0,2},{1,3},{2,0},{3,1},{4,6},{5,7},{6,4},{7,5},{8,10},{9,11},{10,... | collective-permute-start | bytes 1916936 | tf_op jit(solution)/shard_map/ppermute | solution.py:585
  141.5 31.4 %shard_map.171 = (bf16[13,32,768]{2,1,0:T(8,128)(2,1)}, bf16[13,32,768]{2,1,0:T(8,128)(2,1)}, bf16[13,32,768]{2,1,0:T(8,128)(2,1)}, bf16[13,32,768]{2,1,0:T(8,12...) custom-call(s32[1]{0:T(128)} %bitcast.refs_0_, ...), custom_call_target="tpu_custom_call" | custom-call | flops 2418769920 | bytes 1277952 | tf_op jit(solution)/shard_map/pallas_call | solution.py:467
  173.2 3.0 collective-permute-start.14
  178.2 4.3 collective-permute-done.11.refs_2_.refs_3_
  183.5 29.0 %shard_map.170 = (f32[1664,768]{1,0:T(8,128)}, bf16[768,1664]{1,0:T(8,128)(2,1)}, bf16[1664,768]{1,0:T(8,128)(2,1)}, bf16[1664,768]{1,0:T(8,128)(2,1)}, bf16[166...) custom-call(bf16[13,32,768]{2,1,0:T(8,128)(2,1)} %get-tuple-element.160.refs_0_.refs_1_, ...), custom_call_target="tpu_custom_call" | custom-call | flops 2091909120 | bytes 1277952 | tf_op jit(solution)/shard_map/pallas_call | solution.py:467
  212.5 24.8 %collective-permute-done.14.refs_2_.refs_3_ = bf16[13,32,768]{2,1,0:T(8,128)(2,1)} collective-permute-done((bf16[13,32,768]{2,1,0:T(8,128)(2,1)}, bf16[13,32,768]{2,1,0:T(8,128)(2,1)}, u32[]{:S(2)}, u32[]{:S(2)}) %collective-permute-start.14) | collective-permute-done | bytes 639008 | tf_op jit(solution)/shard_map/ppermute | solution.py:585
  240.3 16.6 %collective-permute-start.16 = (bf16[13,32,768]{2,1,0:T(8,128)(2,1)}, bf16[13,32,768]{2,1,0:T(8,128)(2,1)S(1)}, u32[]{:S(2)}, u32[]{:S(2)}) collective-permute-start(bf16[13,32,768]{2,1,0:T(8,128)(2,1)} %bitcast.179), channel_id=1, source_target_pairs={{0,1},{1,0},{2,3},{3,2},{4,5},{5,4},{6,7},{7,6},{8,9},{9,8},{10,11... | collective-permute-start | bytes 1916936 | tf_op jit(solution)/shard_map/ppermute | solution.py:585
  263.5 77.8 %shard_map.172 = (bf16[13,32,768]{2,1,0:T(8,128)(2,1)}, bf16[13,32,768]{2,1,0:T(8,128)(2,1)}, bf16[13,32,768]{2,1,0:T(8,128)(2,1)}, bf16[13,32,768]{2,1,0:T(8,12...) custom-call(f32[1664,768]{1,0:T(8,128)} %get-tuple-element.175.second_ref, ...), custom_call_target="tpu_custom_call" | custom-call | flops 5494800384 | bytes 1277952 | tf_op jit(solution)/shard_map/pallas_call | solution.py:541
  341.3 29.6 %shard_map.173 = (f32[1664,768]{1,0:T(8,128)}, bf16[768,1664]{1,0:T(8,128)(2,1)}, bf16[1664,768]{1,0:T(8,128)(2,1)}, bf16[1664,768]{1,0:T(8,128)(2,1)}, bf16[166...) custom-call(bf16[13,32,768]{2,1,0:T(8,128)(2,1)} %get-tuple-element.181.refs_0_.refs_1_, ...), custom_call_target="tpu_custom_call" | custom-call | flops 2091909120 | bytes 1277952 | tf_op jit(solution)/shard_map/pallas_call | solution.py:467
  375.4 78.6 %shard_map.174 = (bf16[13,32,768]{2,1,0:T(8,128)(2,1)}, bf16[13,32,768]{2,1,0:T(8,128)(2,1)}, bf16[13,32,768]{2,1,0:T(8,128)(2,1)}, bf16[13,32,768]{2,1,0:T(8,12...) custom-call(f32[1664,768]{1,0:T(8,128)} %get-tuple-element.190.second_r, ...), custom_call_target="tpu_custom_call" | custom-call | flops 5494800384 | bytes 1277952 | tf_op jit(solution)/shard_map/pallas_call | solution.py:541
  454.1 9.6 %pad_maximum_fusion = bf16[768,6144]{1,0:T(8,128)(2,1)} fusion(bf16[768,3072]{1,0:T(8,128)(2,1)} %get-tuple-element.261, bf16[768,3072]{1,0:T(8,128)(2,1)} %get-tuple-element.260), kind=kLoop, calls=%fused_computation | loop fusion | flops 18874368 | bytes 18874368 | tf_op jit(solution)/shard_map/concatenate | solution.py:677
  463.9 45.7 %shard_map.175 = (bf16[13,32,768]{2,1,0:T(8,128)(2,1)}, bf16[13,32,768]{2,1,0:T(8,128)(2,1)}, bf16[13,32,768]{2,1,0:T(8,128)(2,1)}, bf16[13,32,768]{2,1,0:T(8,12...) custom-call(f32[1664,768]{1,0:T(8,128)} %get-tuple-element.224.refs_0_, ...), custom_call_target="tpu_custom_call" | custom-call | flops 4445306880 | bytes 1277952 | tf_op jit(solution)/shard_map/pallas_call | solution.py:509
  514.0 45.1 %shard_map.176 = (bf16[13,32,768]{2,1,0:T(8,128)(2,1)}, bf16[13,32,768]{2,1,0:T(8,128)(2,1)}, bf16[13,32,768]{2,1,0:T(8,128)(2,1)}, bf16[13,32,768]{2,1,0:T(8,12...) custom-call(f32[1664,768]{1,0:T(8,128)} %get-tuple-element.217.refs_0_, ...), custom_call_target="tpu_custom_call" | custom-call | flops 4445306880 | bytes 1277952 | tf_op jit(solution)/shard_map/pallas_call | solution.py:509
  564.7 4.7 collective-permute-start.25
  575.2 54.4 %shard_map.177 = (f32[2,1664,768]{2,1,0:T(8,128)}, bf16[2,1664,768]{2,1,0:T(8,128)(2,1)}, f32[3,768,768]{2,1,0:T(8,128)}, f32[768,768]{1,0:T(8,128)}, f32[1,768]{1,0:T(1,128)}) custom-call(s32[1]{0:T(128)} %bitcast.refs_0_, bf16[13,32,768]{2,1,0:T(8,128)(2,1)} %get-tuple-element.241.refs_1_, bf16[13,32,768]{2,1,0:T(8,128)(2,1)} %copy-done.17, ...), custom_call_target="tpu_custom_call" | custom-call | flops 5262458880 | bytes 1277952 | tf_op jit(solution)/shard_map/pallas_call | solution.py:509
  638.0 11.2 %collective-permute-done.27.refs_4_ = bf16[13,32,768]{2,1,0:T(8,128)(2,1)} collective-permute-done((bf16[13,32,768]{2,1,0:T(8,128)(2,1)}, bf16[13,32,768]{2,1,0:T(8,128)(2,1)}, u32[]{:S(2)}, u32[]{:S(2)}) %collective-permute-start.27) | collective-permute-done | bytes 639008 | tf_op jit(solution)/shard_map/ppermute | solution.py:585
  649.2 51.1 %shard_map.178 = (f32[2,1664,768]{2,1,0:T(8,128)}, bf16[3,768,768]{2,1,0:T(8,128)(2,1)}, bf16[768,768]{1,0:T(8,128)(2,1)}, f32[1,768]{1,0:T(1,128)}) custom-call(s32[1]{0:T(128)} %bitcast.refs_0_, bf16[13,32,768]{2,1,0:T(8,128)(2,1)} %get-tuple-element.262.refs_1_, bf16[13,32,768]{2,1,0:T(8,128)(2,1)} %copy-done.20, ...), custom_call_target="tpu_custom_call", output_to_operand_aliasing={{0}: (20, {})} | custom-call | flops 5262458880 | bytes 1277952 | tf_op jit(solution)/shard_map/pallas_call | solution.py:509
  710.0 33.9 %collective-permute-start.41 = (bf16[24,3072]{1,0:T(8,128)(2,1)S(1)}, bf16[24,3072]{1,0:T(8,128)(2,1)S(1)}, u32[]{:S(2)}, u32[]{:S(2)}) collective-permute-start(bf16[24,3072]{1,0:T(8,128)(2,1)S(1)} %get-tuple-element.357), channel_id=1, source_target_pairs={{0,1},{1,0},{2,3},{3,2},{4,5},{5,4},{6,7},{7,6},{8,9},{9,8},{10,11... | collective-permute-start | bytes 442376 | tf_op jit(solution)/shard_map/ppermute | solution.py:585
  746.3 4.6 collective-permute-done.41
  750.9 6.9 collective-permute-done.42
  779.1 3.8 copy.77
  782.9 4.0 reshape.201
  787.6 11.3 %collective-permute-done.36 = bf16[96,3200]{1,0:T(8,128)(2,1)} collective-permute-done((bf16[96,3200]{1,0:T(8,128)(2,1)}, bf16[96,3200]{1,0:T(8,128)(2,1)}, u32[]{:S(2)}, u32[]{:S(2)}) %collective-permute-start.36) | collective-permute-done | bytes 614432 | tf_op jit(solution)/shard_map/ppermute | solution.py:585
  800.9 4.0 collective-permute-start.38
  809.8 8.1 collective-permute-done.39
  (237 shorter events, 123.0 us)
Async XLA Ops:
  7.2 98.2 %all-gather.4.cloned.1.call-start = ((), (), s32[]{:S(2)}) async-start(), calls=%async_computation.2 | async-start | bytes 2211840 | tf_op jit(solution)/shard_map/all_gather | solution.py:648
  21.0 40.5 %collective-permute-start.6 = (bf16[13,32,768]{2,1,0:T(8,128)(2,1)}, bf16[13,32,768]{2,1,0:T(8,128)(2,1)}, u32[]{:S(2)}, u32[]{:S(2)}) collective-permute-start(bf16[13,32,768]{2,1,0:T(8,128)(2,1)} %bitcast.183), channel_id=1, source_target_pairs={{0,1},{1,0},{2,3},{3,2},{4,5},{5,4},{6,7},{7,6},{8,9},{9,8},{10,11... | collective-permute-start | bytes 1916936 | tf_op jit(solution)/shard_map/ppermute | solution.py:585
  22.9 38.7 %collective-permute-start.7 = (bf16[13,32,768]{2,1,0:T(8,128)(2,1)}, bf16[13,32,768]{2,1,0:T(8,128)(2,1)}, u32[]{:S(2)}, u32[]{:S(2)}) collective-permute-start(bf16[13,32,768]{2,1,0:T(8,128)(2,1)} %bitcast.182), channel_id=1, source_target_pairs={{0,2},{1,3},{2,0},{3,1},{4,6},{5,7},{6,4},{7,5},{8,10},{9,11},{10,... | collective-permute-start | bytes 1916936 | tf_op jit(solution)/shard_map/ppermute | solution.py:585
  67.5 114.9 %all-gather.6.cloned.1.call-start = ((), (), s32[]{:S(2)}) async-start(), calls=%async_computation.3 | async-start | bytes 5308416 | tf_op jit(solution)/shard_map/all_gather | solution.py:672
  107.5 156.0 %all-gather.8.cloned.1.call-start = ((), (), s32[]{:S(2)}) async-start(), calls=%async_computation.4 | async-start | bytes 10616832 | tf_op jit(solution)/shard_map/all_gather | solution.py:673
  108.7 460.8 %reduce-scatter.3.cloned.1.call-start = ((), (), s32[]{:S(2)}) async-start(), calls=%async_computation.5 | async-start | bytes 10616832 | tf_op jit(solution)/shard_map/reduce_scatter | solution.py:677
  110.6 65.6 %collective-permute-start.10 = (bf16[13,32,768]{2,1,0:T(8,128)(2,1)}, bf16[13,32,768]{2,1,0:T(8,128)(2,1)S(1)}, u32[]{:S(2)}, u32[]{:S(2)}) collective-permute-start(bf16[13,32,768]{2,1,0:T(8,128)(2,1)} %get-tuple-element.161), channel_id=1, source_target_pairs={{0,1},{1,0},{2,3},{3,2},{4,5},{5,4},{6,7},{7,6},{8,9},{9,8},{10,11... | collective-permute-start | bytes 1916936 | tf_op jit(solution)/shard_map/ppermute | solution.py:585
  128.2 54.2 %collective-permute-start.11 = (bf16[13,32,768]{2,1,0:T(8,128)(2,1)}, bf16[13,32,768]{2,1,0:T(8,128)(2,1)S(1)}, u32[]{:S(2)}, u32[]{:S(2)}) collective-permute-start(bf16[13,32,768]{2,1,0:T(8,128)(2,1)} %get-tuple-element.162), channel_id=1, source_target_pairs={{0,2},{1,3},{2,0},{3,1},{4,6},{5,7},{6,4},{7,5},{8,10},{9,11},{10,... | collective-permute-start | bytes 1916936 | tf_op jit(solution)/shard_map/ppermute | solution.py:585
  140.3 42.2 %collective-permute-start.12 = (bf16[13,32,768]{2,1,0:T(8,128)(2,1)}, bf16[13,32,768]{2,1,0:T(8,128)(2,1)S(1)}, u32[]{:S(2)}, u32[]{:S(2)}) collective-permute-start(bf16[13,32,768]{2,1,0:T(8,128)(2,1)} %get-tuple-element.163), channel_id=1, source_target_pairs={{0,3},{1,2},{2,1},{3,0},{4,7},{5,6},{6,5},{7,4},{8,11},{9,10},{10,... | collective-permute-start | bytes 1916936 | tf_op jit(solution)/shard_map/ppermute | solution.py:585
  172.9 39.6 %collective-permute-start.13 = (bf16[13,32,768]{2,1,0:T(8,128)(2,1)}, bf16[13,32,768]{2,1,0:T(8,128)(2,1)}, u32[]{:S(2)}, u32[]{:S(2)}) collective-permute-start(bf16[13,32,768]{2,1,0:T(8,128)(2,1)} %get-tuple-element.167), channel_id=1, source_target_pairs={{0,1},{1,0},{2,3},{3,2},{4,5},{5,4},{6,7},{7,6},{8,9},{9,8},{10,11... | collective-permute-start | bytes 1916936 | tf_op jit(solution)/shard_map/ppermute | solution.py:585
  173.2 64.1 %collective-permute-start.14 = (bf16[13,32,768]{2,1,0:T(8,128)(2,1)}, bf16[13,32,768]{2,1,0:T(8,128)(2,1)}, u32[]{:S(2)}, u32[]{:S(2)}) collective-permute-start(bf16[13,32,768]{2,1,0:T(8,128)(2,1)} %get-tuple-element.168), channel_id=1, source_target_pairs={{0,2},{1,3},{2,0},{3,1},{4,6},{5,7},{6,4},{7,5},{8,10},{9,11},{10,... | collective-permute-start | bytes 1916936 | tf_op jit(solution)/shard_map/ppermute | solution.py:585
  176.2 61.1 %collective-permute-start.15 = (bf16[13,32,768]{2,1,0:T(8,128)(2,1)}, bf16[13,32,768]{2,1,0:T(8,128)(2,1)}, u32[]{:S(2)}, u32[]{:S(2)}) collective-permute-start(bf16[13,32,768]{2,1,0:T(8,128)(2,1)} %get-tuple-element.169), channel_id=1, source_target_pairs={{0,3},{1,2},{2,1},{3,0},{4,7},{5,6},{6,5},{7,4},{8,11},{9,10},{10,... | collective-permute-start | bytes 1916936 | tf_op jit(solution)/shard_map/ppermute | solution.py:585
  240.3 101.0 %collective-permute-start.16 = (bf16[13,32,768]{2,1,0:T(8,128)(2,1)}, bf16[13,32,768]{2,1,0:T(8,128)(2,1)S(1)}, u32[]{:S(2)}, u32[]{:S(2)}) collective-permute-start(bf16[13,32,768]{2,1,0:T(8,128)(2,1)} %bitcast.179), channel_id=1, source_target_pairs={{0,1},{1,0},{2,3},{3,2},{4,5},{5,4},{6,7},{7,6},{8,9},{9,8},{10,11... | collective-permute-start | bytes 1916936 | tf_op jit(solution)/shard_map/ppermute | solution.py:585
  257.9 83.4 %collective-permute-start.17 = (bf16[13,32,768]{2,1,0:T(8,128)(2,1)}, bf16[13,32,768]{2,1,0:T(8,128)(2,1)S(1)}, u32[]{:S(2)}, u32[]{:S(2)}) collective-permute-start(bf16[13,32,768]{2,1,0:T(8,128)(2,1)} %bitcast.178), channel_id=1, source_target_pairs={{0,2},{1,3},{2,0},{3,1},{4,6},{5,7},{6,4},{7,5},{8,10},{9,11},{10,... | collective-permute-start | bytes 1916936 | tf_op jit(solution)/shard_map/ppermute | solution.py:585
  259.3 82.0 %collective-permute-start.18 = (bf16[13,32,768]{2,1,0:T(8,128)(2,1)}, bf16[13,32,768]{2,1,0:T(8,128)(2,1)S(1)}, u32[]{:S(2)}, u32[]{:S(2)}) collective-permute-start(bf16[13,32,768]{2,1,0:T(8,128)(2,1)} %bitcast.177), channel_id=1, source_target_pairs={{0,3},{1,2},{2,1},{3,0},{4,7},{5,6},{6,5},{7,4},{8,11},{9,10},{10,... | collective-permute-start | bytes 1916936 | tf_op jit(solution)/shard_map/ppermute | solution.py:585
  371.0 83.1 %collective-permute-start.19 = (bf16[13,32,768]{2,1,0:T(8,128)(2,1)}, bf16[13,32,768]{2,1,0:T(8,128)(2,1)S(1)}, u32[]{:S(2)}, u32[]{:S(2)}) collective-permute-start(bf16[13,32,768]{2,1,0:T(8,128)(2,1)} %get-tuple-element.204), channel_id=1, source_target_pairs={{0,1},{1,0},{2,3},{3,2},{4,5},{5,4},{6,7},{7,6},{8,9},{9,8},{10,11... | collective-permute-start | bytes 1916936 | tf_op jit(solution)/shard_map/ppermute | solution.py:585
  372.2 81.9 %collective-permute-start.20 = (bf16[13,32,768]{2,1,0:T(8,128)(2,1)}, bf16[13,32,768]{2,1,0:T(8,128)(2,1)S(1)}, u32[]{:S(2)}, u32[]{:S(2)}) collective-permute-start(bf16[13,32,768]{2,1,0:T(8,128)(2,1)} %get-tuple-element.205), channel_id=1, source_target_pairs={{0,2},{1,3},{2,0},{3,1},{4,6},{5,7},{6,4},{7,5},{8,10},{9,11},{10,... | collective-permute-start | bytes 1916936 | tf_op jit(solution)/shard_map/ppermute | solution.py:585
  373.6 80.5 %collective-permute-start.21 = (bf16[13,32,768]{2,1,0:T(8,128)(2,1)}, bf16[13,32,768]{2,1,0:T(8,128)(2,1)S(1)}, u32[]{:S(2)}, u32[]{:S(2)}) collective-permute-start(bf16[13,32,768]{2,1,0:T(8,128)(2,1)} %get-tuple-element.206), channel_id=1, source_target_pairs={{0,3},{1,2},{2,1},{3,0},{4,7},{5,6},{6,5},{7,4},{8,11},{9,10},{10,... | collective-permute-start | bytes 1916936 | tf_op jit(solution)/shard_map/ppermute | solution.py:585
  463.8 245.1 %reduce-scatter.5.cloned.1.call-start = ((), (), s32[]{:S(2)}) async-start(), calls=%async_computation.6 | async-start | bytes 5308416 | tf_op jit(solution)/shard_map/reduce_scatter | solution.py:677
  509.6 49.6 %collective-permute-start.22 = (bf16[13,32,768]{2,1,0:T(8,128)(2,1)}, bf16[13,32,768]{2,1,0:T(8,128)(2,1)S(1)}, u32[]{:S(2)}, u32[]{:S(2)}) collective-permute-start(bf16[13,32,768]{2,1,0:T(8,128)(2,1)} %get-tuple-element.238), channel_id=1, source_target_pairs={{0,1},{1,0},{2,3},{3,2},{4,5},{5,4},{6,7},{7,6},{8,9},{9,8},{10,11... | collective-permute-start | bytes 1916936 | tf_op jit(solution)/shard_map/ppermute | solution.py:585
  509.7 49.5 %collective-permute-start.23 = (bf16[13,32,768]{2,1,0:T(8,128)(2,1)}, bf16[13,32,768]{2,1,0:T(8,128)(2,1)S(1)}, u32[]{:S(2)}, u32[]{:S(2)}) collective-permute-start(bf16[13,32,768]{2,1,0:T(8,128)(2,1)} %get-tuple-element.239), channel_id=1, source_target_pairs={{0,2},{1,3},{2,0},{3,1},{4,6},{5,7},{6,4},{7,5},{8,10},{9,11},{10,... | collective-permute-start | bytes 1916936 | tf_op jit(solution)/shard_map/ppermute | solution.py:585
  511.5 47.7 %collective-permute-start.24 = (bf16[13,32,768]{2,1,0:T(8,128)(2,1)}, bf16[13,32,768]{2,1,0:T(8,128)(2,1)S(1)}, u32[]{:S(2)}, u32[]{:S(2)}) collective-permute-start(bf16[13,32,768]{2,1,0:T(8,128)(2,1)} %get-tuple-element.240), channel_id=1, source_target_pairs={{0,3},{1,2},{2,1},{3,0},{4,7},{5,6},{6,5},{7,4},{8,11},{9,10},{10,... | collective-permute-start | bytes 1916936 | tf_op jit(solution)/shard_map/ppermute | solution.py:585
  564.7 64.9 %collective-permute-start.25 = (bf16[13,32,768]{2,1,0:T(8,128)(2,1)}, bf16[13,32,768]{2,1,0:T(8,128)(2,1)S(1)}, u32[]{:S(2)}, u32[]{:S(2)}) collective-permute-start(bf16[13,32,768]{2,1,0:T(8,128)(2,1)} %get-tuple-element.257), channel_id=1, source_target_pairs={{0,1},{1,0},{2,3},{3,2},{4,5},{5,4},{6,7},{7,6},{8,9},{9,8},{10,11... | collective-permute-start | bytes 1916936 | tf_op jit(solution)/shard_map/ppermute | solution.py:585
  569.4 68.6 %collective-permute-start.26 = (bf16[13,32,768]{2,1,0:T(8,128)(2,1)}, bf16[13,32,768]{2,1,0:T(8,128)(2,1)}, u32[]{:S(2)}, u32[]{:S(2)}) collective-permute-start(bf16[13,32,768]{2,1,0:T(8,128)(2,1)} %get-tuple-element.258), channel_id=1, source_target_pairs={{0,2},{1,3},{2,0},{3,1},{4,6},{5,7},{6,4},{7,5},{8,10},{9,11},{10,... | collective-permute-start | bytes 1916936 | tf_op jit(solution)/shard_map/ppermute | solution.py:585
  570.7 61.6 %collective-permute-start.28 = (bf16[24,6144]{1,0:T(8,128)(2,1)S(1)}, bf16[24,6144]{1,0:T(8,128)(2,1)S(1)}, u32[]{:S(2)}, u32[]{:S(2)}) collective-permute-start(bf16[24,6144]{1,0:T(8,128)(2,1)S(1)} %get-tuple-element.349), channel_id=1, source_target_pairs={{0,1},{1,0},{2,3},{3,2},{4,5},{5,4},{6,7},{7,6},{8,9},{9,8},{10,11... | collective-permute-start | bytes 884744 | tf_op jit(solution)/shard_map/ppermute | solution.py:585
  572.7 59.7 %collective-permute-start.29 = (bf16[24,6144]{1,0:T(8,128)(2,1)S(1)}, bf16[24,6144]{1,0:T(8,128)(2,1)}, u32[]{:S(2)}, u32[]{:S(2)}) collective-permute-start(bf16[24,6144]{1,0:T(8,128)(2,1)S(1)} %get-tuple-element.351), channel_id=1, source_target_pairs={{0,2},{1,3},{2,0},{3,1},{4,6},{5,7},{6,4},{7,5},{8,10},{9,11},{10,... | collective-permute-start | bytes 884744 | tf_op jit(solution)/shard_map/ppermute | solution.py:585
  573.7 60.4 %collective-permute-start.30 = (bf16[24,6144]{1,0:T(8,128)(2,1)S(1)}, bf16[24,6144]{1,0:T(8,128)(2,1)}, u32[]{:S(2)}, u32[]{:S(2)}) collective-permute-start(bf16[24,6144]{1,0:T(8,128)(2,1)S(1)} %get-tuple-element.350), channel_id=1, source_target_pairs={{0,3},{1,2},{2,1},{3,0},{4,7},{5,6},{6,5},{7,4},{8,11},{9,10},{10,... | collective-permute-start | bytes 884744 | tf_op jit(solution)/shard_map/ppermute | solution.py:585
  632.3 67.9 %collective-permute-start.31 = (bf16[13,32,768]{2,1,0:T(8,128)(2,1)}, bf16[13,32,768]{2,1,0:T(8,128)(2,1)S(1)}, u32[]{:S(2)}, u32[]{:S(2)}) collective-permute-start(bf16[13,32,768]{2,1,0:T(8,128)(2,1)} %get-tuple-element.285), channel_id=1, source_target_pairs={{0,1},{1,0},{2,3},{3,2},{4,5},{5,4},{6,7},{7,6},{8,9},{9,8},{10,11... | collective-permute-start | bytes 1916936 | tf_op jit(solution)/shard_map/ppermute | solution.py:585
  632.4 67.9 %collective-permute-start.32 = (bf16[13,32,768]{2,1,0:T(8,128)(2,1)}, bf16[13,32,768]{2,1,0:T(8,128)(2,1)}, u32[]{:S(2)}, u32[]{:S(2)}) collective-permute-start(bf16[13,32,768]{2,1,0:T(8,128)(2,1)} %get-tuple-element.286), channel_id=1, source_target_pairs={{0,2},{1,3},{2,0},{3,1},{4,6},{5,7},{6,4},{7,5},{8,10},{9,11},{10,... | collective-permute-start | bytes 1916936 | tf_op jit(solution)/shard_map/ppermute | solution.py:585
  634.1 66.2 %collective-permute-start.33 = (bf16[13,32,768]{2,1,0:T(8,128)(2,1)}, bf16[13,32,768]{2,1,0:T(8,128)(2,1)}, u32[]{:S(2)}, u32[]{:S(2)}) collective-permute-start(bf16[13,32,768]{2,1,0:T(8,128)(2,1)} %get-tuple-element.287), channel_id=1, source_target_pairs={{0,3},{1,2},{2,1},{3,0},{4,7},{5,6},{6,5},{7,4},{8,11},{9,10},{10,... | collective-permute-start | bytes 1916936 | tf_op jit(solution)/shard_map/ppermute | solution.py:585
  708.9 54.3 %collective-permute-start.34 = (bf16[4,96,3200]{2,1,0:T(8,128)(2,1)}, bf16[4,96,3200]{2,1,0:T(8,128)(2,1)}, u32[]{:S(2)}, u32[]{:S(2)}) collective-permute-start(bf16[4,96,3200]{2,1,0:T(8,128)(2,1)} %dynamic-slice_bitcast_fusion), channel_id=1, source_target_pairs={{0,4},{4,0},{8,12},{12,8},{16,20},{20,16},{24,28},{28,24},{1,5},{5... | collective-permute-start | bytes 7372808 | tf_op jit(solution)/shard_map/ppermute | solution.py:585
  710.0 41.0 %collective-permute-start.41 = (bf16[24,3072]{1,0:T(8,128)(2,1)S(1)}, bf16[24,3072]{1,0:T(8,128)(2,1)S(1)}, u32[]{:S(2)}, u32[]{:S(2)}) collective-permute-start(bf16[24,3072]{1,0:T(8,128)(2,1)S(1)} %get-tuple-element.357), channel_id=1, source_target_pairs={{0,1},{1,0},{2,3},{3,2},{4,5},{5,4},{6,7},{7,6},{8,9},{9,8},{10,11... | collective-permute-start | bytes 442376 | tf_op jit(solution)/shard_map/ppermute | solution.py:585
  (49 other events, 640.5 us)
Sparse Core Ops, SparseCore 0:
  67.6 37.7 all-gather.3
  107.7 37.7 all-gather.5
  147.4 58.8 all-gather.7
  463.9 76.0 reduce-scatter.2
  564.8 56.2 reduce-scatter.4

commit v4 on v3

--- a/solution.py
+++ b/solution.py
@@ -239,7 +239,7 @@
         old_ref, oldo_ref, oldg_ref = refs[:3]
         refs = refs[3:]
     if again:
-        refs = refs[1:]
+        refs = refs[2:]
     if space:
         gx_ref, refs = refs[0].at[0], refs[1:]
         if deliver:
@@ -488,7 +488,7 @@
     cost = pl.CostEstimate(flops=rows * 4 // COST_SHARE * width * (8 * width + 20 * tile), bytes_accessed=rows * width, transcendentals=0)
     weight_out = [pl.BlockSpec((3, width, QUAD), lambda i: (0, 0, i)), spec_rows((QUAD, width)), whole((1, width))]
     token = whole((rows, width))
-    deliver = space and micro + 1 < micros
+    deliver = space
     lead_specs = [scalar()] + piece_specs(plan, width) + [whole((1, rows, width), (micro, 0, 0))] + (piece_specs(plan, width) if deliver else []) if space else [token] + piece_specs(plan, width)
     if space:
         out_specs = [whole((1, rows, width), (micro, 0, 0))] * (1 + deliver)
@@ -503,9 +503,9 @@
         in_specs = in_specs + weight_out
     aliases = {}
     if shared is not None:
-        aliases = {len(operands): 0}
-        operands += shared[:1]
-        in_specs = in_specs + [pl.BlockSpec(memory_space=pl.ANY)]
+        aliases = {len(operands): 0, len(operands) + 1: 1}
+        operands += shared
+        in_specs = in_specs + [pl.BlockSpec(memory_space=pl.ANY)] * 2
     result = pl.pallas_call(
         functools.partial(attend_bwd, plan, space, old is not None, shared is not None, deliver),
         grid=(quads,),
@@ -645,7 +645,9 @@
 
     padded_gains = jnp.pad(gains, ((0, 0), (0, LANES - gains.shape[1])))
     space = jnp.concatenate([qkv_spatial, out_spatial, padded_gains], axis=1)
-    rest = lax.all_gather(jnp.concatenate([qkv_temporal, out_temporal, units.first_in(mlp_in), units.second_in(mlp_out)], axis=1), "seq", axis=0, tiled=True)
+    rest = jnp.concatenate([qkv_temporal, out_temporal, units.first_in(mlp_in), units.second_in(mlp_out)], axis=1)
+    space, rest = after((space, rest))
+    rest = lax.all_gather(rest, "seq", axis=0, tiled=True)
     cots = [exchange(cot_pieces(cotangent[0]))]
     space = collect(space, "seq", seq, place)
     device = lax.axis_index("dp")
@@ -674,7 +676,7 @@
             me, cots[0] = after((me, cots[0]))
 
     def scatter(parts):
-        v = lax.psum_scatter(jnp.concatenate(parts, axis=1), "dp", scatter_dimension=0, tiled=True)
+        v = lax.psum_scatter(parts, "dp", scatter_dimension=0, tiled=True)
         return reduce_blocks(v.reshape(seq, v.shape[0] // seq, -1), "seq", seq, place)
 
     def attend_parts(old):
@@ -698,34 +700,27 @@
         if m + 1 < micros:
             across[m + 1], cots[m + 1], old_mlp[2] = after((across[m + 1], cots[m + 1], old_mlp[2]))
     old_mlp, done = after((old_mlp, done))
-    owned_mlp = scatter(old_mlp[:2])
+    bundle = jnp.concatenate(old_mlp[:2], axis=1)
+    grads[0], bundle = after((grads[0], bundle))
+    owned_mlp = scatter(bundle)
     for m in range(micros):
         grads[m], old_mlp[2], done = after((grads[m], old_mlp[2], done))
+        if m == 0:
+            done.append(exchange(outs[-1]))
         back, old_time = run_attend_bwd(plan, False, [grads[m], *across[m]], space, time_saved[m], time, m, micros, old_time)
         afters.append(exchange(back))
     old_time, afters[0] = after((old_time, afters[0]))
-    owned_time = scatter(attend_parts(old_time))
+    owned_time = scatter(jnp.concatenate(attend_parts(old_time), axis=1))
     for m in range(micros):
         if m == micros - 1:
             afters[m], owned_mlp = after((afters[m], owned_mlp))
-        result, old_space = run_attend_bwd(plan, True, [me, *afters[m], inputs] + (done[m] if m + 1 < micros else []), space, space_saved[m], space, m, micros, old_space, shared)
-        shared = result + (shared or [])[1:]
-        if m + 1 == micros - 1:
-            old_space[2], outs[-1] = after((old_space[2], outs[-1]))
-            final = exchange(outs[-1])
-
-    old_space, final = after((old_space, final))
-    final = jnp.stack(final).reshape(seq, plan.groups, local_frames, plan.group, width).transpose(0, 2, 1, 3, 4)
-    for at in range(seq.bit_length() - 1):
-        final = final.reshape(seq >> (at + 1), 2, 1 << at, local_frames, plan.room, width)
-        final = jnp.where(((place >> at) & 1) == 1, final[:, ::-1], final)
-    final = final.reshape(clips, plan.per_clip, local_frames, plan.room, width).transpose(0, 2, 1, 3, 4).reshape(plan.rows, width)
-    frames_out = lax.dynamic_update_index_in_dim(shared[1], final, micros - 1, 0)
+        shared, old_space = run_attend_bwd(plan, True, [me, *afters[m], inputs, *done[m]], space, space_saved[m], space, m, micros, old_space, shared)
+    old_space, owned_time = after((old_space, owned_time))
 
     gain_grads = jnp.concatenate([old_space[2], old_time[2], old_mlp[2]], axis=0).T.astype(LOW)
     owned = scatter_rows(jnp.concatenate(attend_parts(old_space) + [jnp.pad(gain_grads, ((0, 0), (0, LANES - gain_grads.shape[1])))], axis=1), dp, seq)
     return (
-        plan.strip(frames_out, (micros, clips)),
+        plan.strip(shared[1], (micros, clips)),
         plan.strip(shared[0], (micros, clips)),
         owned[:, :3 * width],
         owned[:, 3 * width:4 * width],

time: 836 us -> 897 us (1.073)
  waiting for transfers between devices: 114 us -> 211 us
  starting transfers between devices: 124 us -> 106 us
  local copies, waits for them, and re-layouts: 68.7 us -> 55 us
    reduce_scatter x2, waiting for transfers between devices: 0.01 us -> 69.7 us  [scatter(): v = lax.psum_scatter(parts, 'dp', scatter_dimension=0, tiled=True)]
    ppermute x44, waiting for transfers between devices: 113 us -> 140 us  [swap(): return lax.ppermute(v, axis, [(i, i ^ by) for i in range(size)])]
    ppermute x44, starting transfers between devices: 124 us -> 106 us  [swap(): return lax.ppermute(v, axis, [(i, i ^ by) for i in range(size)])]
  transfers between devices with their start and end apart: 49 -> 49, of which waited for: 12 -> 13; matrix products, arithmetic and copies ran while one was open for 9% -> 6% of each run, Pallas kernels for 54% -> 44%
where the time goes in v4:
time: 897 us; the launch traced here: 888 us
  Pallas kernels  475 us (53%)
  waiting for transfers between devices  211 us (24%)
  starting transfers between devices  106 us (12%)
  local copies, waits for them, and re-layouts  55 us (6%)
  other arithmetic  25.8 us (3%)
  between operations  14.8 us (2%)
    pallas_call x4, Pallas kernels, run_attend_bwd(): pl.pallas_call(functools.partial(attend_bwd, plan, space, old is not None...  198 us
    pallas_call x2, Pallas kernels, run_mlp(): pl.pallas_call(functools.partial(mlp_both, plan, old is not None), grid=(...  156 us
    ppermute x44, waiting for transfers between devices, swap(): return lax.ppermute(v, axis, [(i, i ^ by) for i in range(size)])  140 us
    pallas_call x4, Pallas kernels, run_attend_fwd(): pl.pallas_call(functools.partial(attend_fwd, plan, space), grid=(quads,),...  121 us
    ppermute x44, starting transfers between devices, swap(): return lax.ppermute(v, axis, [(i, i ^ by) for i in range(size)])  106 us
    reduce_scatter x2, waiting for transfers between devices, scatter(): v = lax.psum_scatter(parts, 'dp', scatter_dimension=0, tiled=True)  69.7 us
  transfers between devices with their start and end apart: 49, of which 13 were waited for; matrix products, arithmetic and copies ran while one was open for 6% of the time, Pallas kernels for 44%

profile of v4, /device:TPU:0, one launch (start us, length us, event | category | flops | bytes accessed | tf_op | source)
XLA Modules:
  0.0 888.3 jit_solution(9276776850625869318)
XLA Ops:
  12.1 3.0 collective-permute-start
  17.7 4.3 slice_bitcast_fusion
  25.9 3.5 collective-permute-start.7
  40.5 12.2 %collective-permute-done.3 = bf16[4,24,3200]{2,1,0:T(8,128)(2,1)S(1)} collective-permute-done((bf16[4,24,3200]{2,1,0:T(8,128)(2,1)}, bf16[4,24,3200]{2,1,0:T(8,128)(2,1)S(1)}, u32[]{:S(2)}, u32[]{:S(2)}) %collective-permute-start.3) | collective-permute-done | bytes 614432 | tf_op jit(solution)/shard_map/ppermute | solution.py:585
  52.8 11.7 %collective-permute-done.4 = bf16[4,24,3200]{2,1,0:T(8,128)(2,1)S(1)} collective-permute-done((bf16[4,24,3200]{2,1,0:T(8,128)(2,1)}, bf16[4,24,3200]{2,1,0:T(8,128)(2,1)S(1)}, u32[]{:S(2)}, u32[]{:S(2)}) %collective-permute-start.4) | collective-permute-done | bytes 614432 | tf_op jit(solution)/shard_map/ppermute | solution.py:585
  65.4 4.1 collective-permute-done.9
  74.5 31.4 %shard_map.169 = (bf16[13,32,768]{2,1,0:T(8,128)(2,1)}, bf16[13,32,768]{2,1,0:T(8,128)(2,1)}, bf16[13,32,768]{2,1,0:T(8,128)(2,1)}, bf16[13,32,768]{2,1,0:T(8,12...) custom-call(s32[1]{0:T(128)} %bitcast.refs_0_, ...), custom_call_target="tpu_custom_call" | custom-call | flops 2418769920 | bytes 1277952 | tf_op jit(solution)/shard_map/pallas_call | solution.py:467
  110.3 18.3 %collective-permute-done.8.refs_3_ = bf16[13,32,768]{2,1,0:T(8,128)(2,1)S(1)} collective-permute-done((bf16[13,32,768]{2,1,0:T(8,128)(2,1)S(1)}, bf16[13,32,768]{2,1,0:T(8,128)(2,1)S(1)}, u32[]{:S(2)}, u32[]{:S(2)}) %collective-permute-start.8) | collective-permute-done | bytes 639008 | tf_op jit(solution)/shard_map/ppermute | solution.py:585
  128.6 11.2 %collective-permute-start.11 = (bf16[13,32,768]{2,1,0:T(8,128)(2,1)}, bf16[13,32,768]{2,1,0:T(8,128)(2,1)S(1)}, u32[]{:S(2)}, u32[]{:S(2)}) collective-permute-start(bf16[13,32,768]{2,1,0:T(8,128)(2,1)} %get-tuple-element.164), channel_id=1, source_target_pairs={{0,2},{1,3},{2,0},{3,1},{4,6},{5,7},{6,4},{7,5},{8,10},{9,11},{10,... | collective-permute-start | bytes 1916936 | tf_op jit(solution)/shard_map/ppermute | solution.py:585
  142.3 31.4 %shard_map.171 = (bf16[13,32,768]{2,1,0:T(8,128)(2,1)}, bf16[13,32,768]{2,1,0:T(8,128)(2,1)}, bf16[13,32,768]{2,1,0:T(8,128)(2,1)}, bf16[13,32,768]{2,1,0:T(8,12...) custom-call(s32[1]{0:T(128)} %bitcast.refs_0_, ...), custom_call_target="tpu_custom_call" | custom-call | flops 2418769920 | bytes 1277952 | tf_op jit(solution)/shard_map/pallas_call | solution.py:467
  178.9 3.9 collective-permute-done.11.refs_2_.refs_3_
  183.9 29.1 %shard_map.170 = (f32[1664,768]{1,0:T(8,128)}, bf16[768,1664]{1,0:T(8,128)(2,1)}, bf16[1664,768]{1,0:T(8,128)(2,1)}, bf16[1664,768]{1,0:T(8,128)(2,1)}, bf16[166...) custom-call(bf16[13,32,768]{2,1,0:T(8,128)(2,1)} %get-tuple-element.162.refs_0_.refs_1_, ...), custom_call_target="tpu_custom_call" | custom-call | flops 2091909120 | bytes 1277952 | tf_op jit(solution)/shard_map/pallas_call | solution.py:467
  213.0 24.7 %collective-permute-done.14.refs_2_.refs_3_ = bf16[13,32,768]{2,1,0:T(8,128)(2,1)} collective-permute-done((bf16[13,32,768]{2,1,0:T(8,128)(2,1)}, bf16[13,32,768]{2,1,0:T(8,128)(2,1)}, u32[]{:S(2)}, u32[]{:S(2)}) %collective-permute-start.14) | collective-permute-done | bytes 639008 | tf_op jit(solution)/shard_map/ppermute | solution.py:585
  240.6 16.6 %collective-permute-start.16 = (bf16[13,32,768]{2,1,0:T(8,128)(2,1)}, bf16[13,32,768]{2,1,0:T(8,128)(2,1)S(1)}, u32[]{:S(2)}, u32[]{:S(2)}) collective-permute-start(bf16[13,32,768]{2,1,0:T(8,128)(2,1)} %bitcast.165), channel_id=1, source_target_pairs={{0,1},{1,0},{2,3},{3,2},{4,5},{5,4},{6,7},{7,6},{8,9},{9,8},{10,11... | collective-permute-start | bytes 1916936 | tf_op jit(solution)/shard_map/ppermute | solution.py:585
  263.7 77.8 %shard_map.172 = (bf16[13,32,768]{2,1,0:T(8,128)(2,1)}, bf16[13,32,768]{2,1,0:T(8,128)(2,1)}, bf16[13,32,768]{2,1,0:T(8,128)(2,1)}, bf16[13,32,768]{2,1,0:T(8,12...) custom-call(f32[1664,768]{1,0:T(8,128)} %get-tuple-element.178.second_ref, ...), custom_call_target="tpu_custom_call" | custom-call | flops 5494800384 | bytes 1277952 | tf_op jit(solution)/shard_map/pallas_call | solution.py:541
  341.6 29.6 %shard_map.173 = (f32[1664,768]{1,0:T(8,128)}, bf16[768,1664]{1,0:T(8,128)(2,1)}, bf16[1664,768]{1,0:T(8,128)(2,1)}, bf16[1664,768]{1,0:T(8,128)(2,1)}, bf16[166...) custom-call(bf16[13,32,768]{2,1,0:T(8,128)(2,1)} %get-tuple-element.184.refs_0_.refs_1_, ...), custom_call_target="tpu_custom_call" | custom-call | flops 2091909120 | bytes 1277952 | tf_op jit(solution)/shard_map/pallas_call | solution.py:467
  375.7 78.5 %shard_map.174 = (bf16[13,32,768]{2,1,0:T(8,128)(2,1)}, bf16[13,32,768]{2,1,0:T(8,128)(2,1)}, bf16[13,32,768]{2,1,0:T(8,128)(2,1)}, bf16[13,32,768]{2,1,0:T(8,12...) custom-call(f32[1664,768]{1,0:T(8,128)} %get-tuple-element.193.second_r, ...), custom_call_target="tpu_custom_call" | custom-call | flops 5494800384 | bytes 1277952 | tf_op jit(solution)/shard_map/pallas_call | solution.py:541
  459.5 9.0 %pad_maximum_fusion = bf16[768,6144]{1,0:T(8,128)(2,1)} fusion(bf16[768,3072]{1,0:T(8,128)(2,1)} %get-tuple-element.211, bf16[768,3072]{1,0:T(8,128)(2,1)} %get-tuple-element.210), kind=kLoop, calls=%fused_computation | loop fusion | flops 18874368 | bytes 18874368 | tf_op jit(solution)/shard_map/concatenate | solution.py:703
  468.5 44.2 %shard_map.175 = (bf16[13,32,768]{2,1,0:T(8,128)(2,1)}, bf16[13,32,768]{2,1,0:T(8,128)(2,1)}, bf16[13,32,768]{2,1,0:T(8,128)(2,1)}, bf16[13,32,768]{2,1,0:T(8,12...) custom-call(f32[1664,768]{1,0:T(8,128)} %get-tuple-element.234.refs_0_, ...), custom_call_target="tpu_custom_call" | custom-call | flops 4445306880 | bytes 1277952 | tf_op jit(solution)/shard_map/pallas_call | solution.py:509
  517.2 45.1 %shard_map.176 = (bf16[13,32,768]{2,1,0:T(8,128)(2,1)}, bf16[13,32,768]{2,1,0:T(8,128)(2,1)}, bf16[13,32,768]{2,1,0:T(8,128)(2,1)}, bf16[13,32,768]{2,1,0:T(8,12...) custom-call(f32[1664,768]{1,0:T(8,128)} %get-tuple-element.227.refs_0_, ...), custom_call_target="tpu_custom_call" | custom-call | flops 4445306880 | bytes 1277952 | tf_op jit(solution)/shard_map/pallas_call | solution.py:509
  567.7 5.2 collective-permute-start.25
  573.9 55.0 %shard_map.177 = (f32[2,1664,768]{2,1,0:T(8,128)}, bf16[2,1664,768]{2,1,0:T(8,128)(2,1)}, f32[3,768,768]{2,1,0:T(8,128)}, f32[768,768]{1,0:T(8,128)}, f32[1,768]{1,0:T(1,128)}) custom-call(s32[1]{0:T(128)} %bitcast.refs_0_, bf16[13,32,768]{2,1,0:T(8,128)(2,1)} %get-tuple-element.270.refs_1_, bf16[13,32,768]{2,1,0:T(8,128)(2,1)} %collective-permute-done.31.refs_2_, ...), custom_call_target="tpu_custom_call" | custom-call | flops 5262458880 | bytes 1277952 | tf_op jit(solution)/shard_map/pallas_call | solution.py:509
  634.6 69.7 %reduce-scatter.3.cloned.1.call-done = bf16[96,6144]{1,0:T(8,128)(2,1)} async-done(((bf16[768,6144]{1,0:T(8,128)(2,1)}), bf16[96,6144]{1,0:T(8,128)(2,1)}) %reduce-scatter.3.cloned.1.call-update) | async-done | bytes 1179664 | tf_op jit(solution)/shard_map/reduce_scatter | solution.py:679
  710.9 8.9 collective-permute-done.28
  722.7 21.5 %collective-permute-done.29 = bf16[24,6144]{1,0:T(8,128)(2,1)S(1)} collective-permute-done((bf16[24,6144]{1,0:T(8,128)(2,1)S(1)}, bf16[24,6144]{1,0:T(8,128)(2,1)S(1)}, u32[]{:S(2)}, u32[]{:S(2)}) %collective-permute-start.29) | collective-permute-done | bytes 294944 | tf_op jit(solution)/shard_map/ppermute | solution.py:585
  746.2 53.4 %shard_map.178 = (f32[2,1664,768]{2,1,0:T(8,128)}, bf16[2,1664,768]{2,1,0:T(8,128)(2,1)}, bf16[3,768,768]{2,1,0:T(8,128)(2,1)}, bf16[768,768]{1,0:T(8,128)(2,1)}, f32[1,768]{1,0:T(1,128)}) custom-call(s32[1]{0:T(128)} %bitcast.refs_0_, bf16[13,32,768]{2,1,0:T(8,128)(2,1)} %get-tuple-element.249.refs_1_, ...), custom_call_target="tpu_custom_call", output_to_operand_aliasing={{0}: (24, {}), {1}: (25, {})} | custom-call | flops 5262458880 | bytes 1277952 | tf_op jit(solution)/shard_map/pallas_call | solution.py:509
  806.8 4.8 collective-permute-done.37
  811.6 3.0 fusion
  818.3 13.2 %collective-permute-done.38 = bf16[96,3200]{1,0:T(8,128)(2,1)S(1)} collective-permute-done((bf16[96,3200]{1,0:T(8,128)(2,1)S(1)}, bf16[96,3200]{1,0:T(8,128)(2,1)S(1)}, u32[]{:S(2)}, u32[]{:S(2)}) %collective-permute-start.38) | collective-permute-done | bytes 614432 | tf_op jit(solution)/shard_map/ppermute | solution.py:585
  831.5 13.4 %collective-permute-done.39 = bf16[96,3200]{1,0:T(8,128)(2,1)S(1)} collective-permute-done((bf16[96,3200]{1,0:T(8,128)(2,1)S(1)}, bf16[96,3200]{1,0:T(8,128)(2,1)S(1)}, u32[]{:S(2)}, u32[]{:S(2)}) %collective-permute-start.39) | collective-permute-done | bytes 614432 | tf_op jit(solution)/shard_map/ppermute | solution.py:585
  846.9 17.3 %collective-permute-start.41 = (bf16[24,3200]{1,0:T(8,128)(2,1)}, bf16[24,3200]{1,0:T(8,128)(2,1)}, u32[]{:S(2)}, u32[]{:S(2)}) collective-permute-start(bf16[24,3200]{1,0:T(8,128)(2,1)} %get-tuple-element.354), channel_id=1, source_target_pairs={{0,1},{1,0},{2,3},{3,2},{4,5},{5,4},{6,7},{7,6},{8,9},{9,8},{10,11... | collective-permute-start | bytes 460808 | tf_op jit(solution)/shard_map/ppermute | solution.py:585
  874.7 3.6 collective-permute-done.42
  (224 shorter events, 114.9 us)
Async XLA Ops:
  7.2 98.6 %all-gather.4.cloned.1.call-start = ((), (), s32[]{:S(2)}) async-start(), calls=%async_computation.2 | async-start | bytes 2211840 | tf_op jit(solution)/shard_map/all_gather | solution.py:650
  24.1 40.6 %collective-permute-start.6 = (bf16[13,32,768]{2,1,0:T(8,128)(2,1)}, bf16[13,32,768]{2,1,0:T(8,128)(2,1)}, u32[]{:S(2)}, u32[]{:S(2)}) collective-permute-start(bf16[13,32,768]{2,1,0:T(8,128)(2,1)} %bitcast.169), channel_id=1, source_target_pairs={{0,1},{1,0},{2,3},{3,2},{4,5},{5,4},{6,7},{7,6},{8,9},{9,8},{10,11... | collective-permute-start | bytes 1916936 | tf_op jit(solution)/shard_map/ppermute | solution.py:585
  25.9 38.8 %collective-permute-start.7 = (bf16[13,32,768]{2,1,0:T(8,128)(2,1)}, bf16[13,32,768]{2,1,0:T(8,128)(2,1)}, u32[]{:S(2)}, u32[]{:S(2)}) collective-permute-start(bf16[13,32,768]{2,1,0:T(8,128)(2,1)} %bitcast.168), channel_id=1, source_target_pairs={{0,2},{1,3},{2,0},{3,1},{4,6},{5,7},{6,4},{7,5},{8,10},{9,11},{10,... | collective-permute-start | bytes 1916936 | tf_op jit(solution)/shard_map/ppermute | solution.py:585
  64.8 118.0 %all-gather.6.cloned.1.call-start = ((), (), s32[]{:S(2)}) async-start(), calls=%async_computation.3 | async-start | bytes 5308416 | tf_op jit(solution)/shard_map/all_gather | solution.py:674
  108.0 155.8 %all-gather.8.cloned.1.call-start = ((), (), s32[]{:S(2)}) async-start(), calls=%async_computation.4 | async-start | bytes 10616832 | tf_op jit(solution)/shard_map/all_gather | solution.py:675
  109.2 519.8 %reduce-scatter.5.cloned.1.call-start = ((), (), s32[]{:S(2)}) async-start(), calls=%async_computation.6 | async-start | bytes 5308416 | tf_op jit(solution)/shard_map/reduce_scatter | solution.py:679
  109.7 65.9 %collective-permute-start.10 = (bf16[13,32,768]{2,1,0:T(8,128)(2,1)}, bf16[13,32,768]{2,1,0:T(8,128)(2,1)S(1)}, u32[]{:S(2)}, u32[]{:S(2)}) collective-permute-start(bf16[13,32,768]{2,1,0:T(8,128)(2,1)} %get-tuple-element.163), channel_id=1, source_target_pairs={{0,1},{1,0},{2,3},{3,2},{4,5},{5,4},{6,7},{7,6},{8,9},{9,8},{10,11... | collective-permute-start | bytes 1916936 | tf_op jit(solution)/shard_map/ppermute | solution.py:585
  128.6 54.1 %collective-permute-start.11 = (bf16[13,32,768]{2,1,0:T(8,128)(2,1)}, bf16[13,32,768]{2,1,0:T(8,128)(2,1)S(1)}, u32[]{:S(2)}, u32[]{:S(2)}) collective-permute-start(bf16[13,32,768]{2,1,0:T(8,128)(2,1)} %get-tuple-element.164), channel_id=1, source_target_pairs={{0,2},{1,3},{2,0},{3,1},{4,6},{5,7},{6,4},{7,5},{8,10},{9,11},{10,... | collective-permute-start | bytes 1916936 | tf_op jit(solution)/shard_map/ppermute | solution.py:585
  139.9 42.9 %collective-permute-start.12 = (bf16[13,32,768]{2,1,0:T(8,128)(2,1)}, bf16[13,32,768]{2,1,0:T(8,128)(2,1)S(1)}, u32[]{:S(2)}, u32[]{:S(2)}) collective-permute-start(bf16[13,32,768]{2,1,0:T(8,128)(2,1)} %get-tuple-element.165), channel_id=1, source_target_pairs={{0,3},{1,2},{2,1},{3,0},{4,7},{5,6},{6,5},{7,4},{8,11},{9,10},{10,... | collective-permute-start | bytes 1916936 | tf_op jit(solution)/shard_map/ppermute | solution.py:585
  173.7 39.3 %collective-permute-start.13 = (bf16[13,32,768]{2,1,0:T(8,128)(2,1)}, bf16[13,32,768]{2,1,0:T(8,128)(2,1)}, u32[]{:S(2)}, u32[]{:S(2)}) collective-permute-start(bf16[13,32,768]{2,1,0:T(8,128)(2,1)} %get-tuple-element.170), channel_id=1, source_target_pairs={{0,1},{1,0},{2,3},{3,2},{4,5},{5,4},{6,7},{7,6},{8,9},{9,8},{10,11... | collective-permute-start | bytes 1916936 | tf_op jit(solution)/shard_map/ppermute | solution.py:585
  173.8 63.9 %collective-permute-start.14 = (bf16[13,32,768]{2,1,0:T(8,128)(2,1)}, bf16[13,32,768]{2,1,0:T(8,128)(2,1)}, u32[]{:S(2)}, u32[]{:S(2)}) collective-permute-start(bf16[13,32,768]{2,1,0:T(8,128)(2,1)} %get-tuple-element.171), channel_id=1, source_target_pairs={{0,2},{1,3},{2,0},{3,1},{4,6},{5,7},{6,4},{7,5},{8,10},{9,11},{10,... | collective-permute-start | bytes 1916936 | tf_op jit(solution)/shard_map/ppermute | solution.py:585
  175.6 62.0 %collective-permute-start.15 = (bf16[13,32,768]{2,1,0:T(8,128)(2,1)}, bf16[13,32,768]{2,1,0:T(8,128)(2,1)}, u32[]{:S(2)}, u32[]{:S(2)}) collective-permute-start(bf16[13,32,768]{2,1,0:T(8,128)(2,1)} %get-tuple-element.172), channel_id=1, source_target_pairs={{0,3},{1,2},{2,1},{3,0},{4,7},{5,6},{6,5},{7,4},{8,11},{9,10},{10,... | collective-permute-start | bytes 1916936 | tf_op jit(solution)/shard_map/ppermute | solution.py:585
  240.6 101.0 %collective-permute-start.16 = (bf16[13,32,768]{2,1,0:T(8,128)(2,1)}, bf16[13,32,768]{2,1,0:T(8,128)(2,1)S(1)}, u32[]{:S(2)}, u32[]{:S(2)}) collective-permute-start(bf16[13,32,768]{2,1,0:T(8,128)(2,1)} %bitcast.165), channel_id=1, source_target_pairs={{0,1},{1,0},{2,3},{3,2},{4,5},{5,4},{6,7},{7,6},{8,9},{9,8},{10,11... | collective-permute-start | bytes 1916936 | tf_op jit(solution)/shard_map/ppermute | solution.py:585
  258.1 83.5 %collective-permute-start.17 = (bf16[13,32,768]{2,1,0:T(8,128)(2,1)}, bf16[13,32,768]{2,1,0:T(8,128)(2,1)S(1)}, u32[]{:S(2)}, u32[]{:S(2)}) collective-permute-start(bf16[13,32,768]{2,1,0:T(8,128)(2,1)} %bitcast.164), channel_id=1, source_target_pairs={{0,2},{1,3},{2,0},{3,1},{4,6},{5,7},{6,4},{7,5},{8,10},{9,11},{10,... | collective-permute-start | bytes 1916936 | tf_op jit(solution)/shard_map/ppermute | solution.py:585
  259.9 81.7 %collective-permute-start.18 = (bf16[13,32,768]{2,1,0:T(8,128)(2,1)}, bf16[13,32,768]{2,1,0:T(8,128)(2,1)S(1)}, u32[]{:S(2)}, u32[]{:S(2)}) collective-permute-start(bf16[13,32,768]{2,1,0:T(8,128)(2,1)} %bitcast.163), channel_id=1, source_target_pairs={{0,3},{1,2},{2,1},{3,0},{4,7},{5,6},{6,5},{7,4},{8,11},{9,10},{10,... | collective-permute-start | bytes 1916936 | tf_op jit(solution)/shard_map/ppermute | solution.py:585
  371.2 85.9 %collective-permute-start.19 = (bf16[13,32,768]{2,1,0:T(8,128)(2,1)}, bf16[13,32,768]{2,1,0:T(8,128)(2,1)S(1)}, u32[]{:S(2)}, u32[]{:S(2)}) collective-permute-start(bf16[13,32,768]{2,1,0:T(8,128)(2,1)} %get-tuple-element.207), channel_id=1, source_target_pairs={{0,1},{1,0},{2,3},{3,2},{4,5},{5,4},{6,7},{7,6},{8,9},{9,8},{10,11... | collective-permute-start | bytes 1916936 | tf_op jit(solution)/shard_map/ppermute | solution.py:585
  372.4 87.1 %collective-permute-start.20 = (bf16[13,32,768]{2,1,0:T(8,128)(2,1)}, bf16[13,32,768]{2,1,0:T(8,128)(2,1)}, u32[]{:S(2)}, u32[]{:S(2)}) collective-permute-start(bf16[13,32,768]{2,1,0:T(8,128)(2,1)} %get-tuple-element.208), channel_id=1, source_target_pairs={{0,2},{1,3},{2,0},{3,1},{4,6},{5,7},{6,4},{7,5},{8,10},{9,11},{10,... | collective-permute-start | bytes 1916936 | tf_op jit(solution)/shard_map/ppermute | solution.py:585
  374.2 85.3 %collective-permute-start.21 = (bf16[13,32,768]{2,1,0:T(8,128)(2,1)}, bf16[13,32,768]{2,1,0:T(8,128)(2,1)}, u32[]{:S(2)}, u32[]{:S(2)}) collective-permute-start(bf16[13,32,768]{2,1,0:T(8,128)(2,1)} %get-tuple-element.209), channel_id=1, source_target_pairs={{0,3},{1,2},{2,1},{3,0},{4,7},{5,6},{6,5},{7,4},{8,11},{9,10},{10,... | collective-permute-start | bytes 1916936 | tf_op jit(solution)/shard_map/ppermute | solution.py:585
  454.2 61.5 %collective-permute-start.22 = (bf16[13,32,768]{2,1,0:T(8,128)(2,1)}, bf16[13,32,768]{2,1,0:T(8,128)(2,1)S(1)}, u32[]{:S(2)}, u32[]{:S(2)}) collective-permute-start(bf16[13,32,768]{2,1,0:T(8,128)(2,1)} %get-tuple-element.224), channel_id=1, source_target_pairs={{0,1},{1,0},{2,3},{3,2},{4,5},{5,4},{6,7},{7,6},{8,9},{9,8},{10,11... | collective-permute-start | bytes 1916936 | tf_op jit(solution)/shard_map/ppermute | solution.py:585
  454.5 62.7 %collective-permute-start.23 = (bf16[13,32,768]{2,1,0:T(8,128)(2,1)}, bf16[13,32,768]{2,1,0:T(8,128)(2,1)S(1)}, u32[]{:S(2)}, u32[]{:S(2)}) collective-permute-start(bf16[13,32,768]{2,1,0:T(8,128)(2,1)} %get-tuple-element.225), channel_id=1, source_target_pairs={{0,2},{1,3},{2,0},{3,1},{4,6},{5,7},{6,4},{7,5},{8,10},{9,11},{10,... | collective-permute-start | bytes 1916936 | tf_op jit(solution)/shard_map/ppermute | solution.py:585
  458.0 59.1 %collective-permute-start.24 = (bf16[13,32,768]{2,1,0:T(8,128)(2,1)}, bf16[13,32,768]{2,1,0:T(8,128)(2,1)S(1)}, u32[]{:S(2)}, u32[]{:S(2)}) collective-permute-start(bf16[13,32,768]{2,1,0:T(8,128)(2,1)} %get-tuple-element.226), channel_id=1, source_target_pairs={{0,3},{1,2},{2,1},{3,0},{4,7},{5,6},{6,5},{7,4},{8,11},{9,10},{10,... | collective-permute-start | bytes 1916936 | tf_op jit(solution)/shard_map/ppermute | solution.py:585
  512.7 49.6 %collective-permute-start.31 = (bf16[13,32,768]{2,1,0:T(8,128)(2,1)}, bf16[13,32,768]{2,1,0:T(8,128)(2,1)}, u32[]{:S(2)}, u32[]{:S(2)}) collective-permute-start(bf16[13,32,768]{2,1,0:T(8,128)(2,1)} %get-tuple-element.267), channel_id=1, source_target_pairs={{0,1},{1,0},{2,3},{3,2},{4,5},{5,4},{6,7},{7,6},{8,9},{9,8},{10,11... | collective-permute-start | bytes 1916936 | tf_op jit(solution)/shard_map/ppermute | solution.py:585
  512.8 49.5 %collective-permute-start.32 = (bf16[13,32,768]{2,1,0:T(8,128)(2,1)}, bf16[13,32,768]{2,1,0:T(8,128)(2,1)}, u32[]{:S(2)}, u32[]{:S(2)}) collective-permute-start(bf16[13,32,768]{2,1,0:T(8,128)(2,1)} %get-tuple-element.268), channel_id=1, source_target_pairs={{0,2},{1,3},{2,0},{3,1},{4,6},{5,7},{6,4},{7,5},{8,10},{9,11},{10,... | collective-permute-start | bytes 1916936 | tf_op jit(solution)/shard_map/ppermute | solution.py:585
  515.7 46.6 %collective-permute-start.33 = (bf16[13,32,768]{2,1,0:T(8,128)(2,1)}, bf16[13,32,768]{2,1,0:T(8,128)(2,1)}, u32[]{:S(2)}, u32[]{:S(2)}) collective-permute-start(bf16[13,32,768]{2,1,0:T(8,128)(2,1)} %get-tuple-element.269), channel_id=1, source_target_pairs={{0,3},{1,2},{2,1},{3,0},{4,7},{5,6},{6,5},{7,4},{8,11},{9,10},{10,... | collective-permute-start | bytes 1916936 | tf_op jit(solution)/shard_map/ppermute | solution.py:585
  567.1 137.1 %reduce-scatter.3.cloned.1.call-start = ((), (), s32[]{:S(2)}) async-start(), calls=%async_computation.5 | async-start | bytes 10616832 | tf_op jit(solution)/shard_map/reduce_scatter | solution.py:679
  567.7 177.6 %collective-permute-start.25 = (bf16[13,32,768]{2,1,0:T(8,128)(2,1)}, bf16[13,32,768]{2,1,0:T(8,128)(2,1)S(1)}, u32[]{:S(2)}, u32[]{:S(2)}) collective-permute-start(bf16[13,32,768]{2,1,0:T(8,128)(2,1)} %get-tuple-element.245), channel_id=1, source_target_pairs={{0,1},{1,0},{2,3},{3,2},{4,5},{5,4},{6,7},{7,6},{8,9},{9,8},{10,11... | collective-permute-start | bytes 1916936 | tf_op jit(solution)/shard_map/ppermute | solution.py:585
  572.9 172.4 %collective-permute-start.26 = (bf16[13,32,768]{2,1,0:T(8,128)(2,1)}, bf16[13,32,768]{2,1,0:T(8,128)(2,1)}, u32[]{:S(2)}, u32[]{:S(2)}) collective-permute-start(bf16[13,32,768]{2,1,0:T(8,128)(2,1)} %get-tuple-element.246), channel_id=1, source_target_pairs={{0,2},{1,3},{2,0},{3,1},{4,6},{5,7},{6,4},{7,5},{8,10},{9,11},{10,... | collective-permute-start | bytes 1916936 | tf_op jit(solution)/shard_map/ppermute | solution.py:585
  630.1 75.4 %collective-permute-start.34 = (bf16[24,3072]{1,0:T(8,128)(2,1)S(1)}, bf16[24,3072]{1,0:T(8,128)(2,1)S(1)}, u32[]{:S(2)}, u32[]{:S(2)}) collective-permute-start(bf16[24,3072]{1,0:T(8,128)(2,1)S(1)} %get-tuple-element.359), channel_id=1, source_target_pairs={{0,1},{1,0},{2,3},{3,2},{4,5},{5,4},{6,7},{7,6},{8,9},{9,8},{10,11... | collective-permute-start | bytes 442376 | tf_op jit(solution)/shard_map/ppermute | solution.py:585
  632.1 74.9 %collective-permute-start.35 = (bf16[24,3072]{1,0:T(8,128)(2,1)S(1)}, bf16[24,3072]{1,0:T(8,128)(2,1)S(1)}, u32[]{:S(2)}, u32[]{:S(2)}) collective-permute-start(bf16[24,3072]{1,0:T(8,128)(2,1)S(1)} %get-tuple-element.361), channel_id=1, source_target_pairs={{0,2},{1,3},{2,0},{3,1},{4,6},{5,7},{6,4},{7,5},{8,10},{9,11},{10,... | collective-permute-start | bytes 442376 | tf_op jit(solution)/shard_map/ppermute | solution.py:585
  632.1 77.3 %collective-permute-start.36 = (bf16[24,3072]{1,0:T(8,128)(2,1)S(1)}, bf16[24,3072]{1,0:T(8,128)(2,1)S(1)}, u32[]{:S(2)}, u32[]{:S(2)}) collective-permute-start(bf16[24,3072]{1,0:T(8,128)(2,1)S(1)} %get-tuple-element.360), channel_id=1, source_target_pairs={{0,3},{1,2},{2,1},{3,0},{4,7},{5,6},{6,5},{7,4},{8,11},{9,10},{10,... | collective-permute-start | bytes 442376 | tf_op jit(solution)/shard_map/ppermute | solution.py:585
  707.0 37.2 %collective-permute-start.29 = (bf16[24,6144]{1,0:T(8,128)(2,1)S(1)}, bf16[24,6144]{1,0:T(8,128)(2,1)S(1)}, u32[]{:S(2)}, u32[]{:S(2)}) collective-permute-start(bf16[24,6144]{1,0:T(8,128)(2,1)S(1)} %get-tuple-element.353), channel_id=1, source_target_pairs={{0,2},{1,3},{2,0},{3,1},{4,6},{5,7},{6,4},{7,5},{8,10},{9,11},{10,... | collective-permute-start | bytes 884744 | tf_op jit(solution)/shard_map/ppermute | solution.py:585
  709.5 34.8 %collective-permute-start.30 = (bf16[24,6144]{1,0:T(8,128)(2,1)S(1)}, bf16[24,6144]{1,0:T(8,128)(2,1)S(1)}, u32[]{:S(2)}, u32[]{:S(2)}) collective-permute-start(bf16[24,6144]{1,0:T(8,128)(2,1)S(1)} %get-tuple-element.352), channel_id=1, source_target_pairs={{0,3},{1,2},{2,1},{3,0},{4,7},{5,6},{6,5},{7,4},{8,11},{9,10},{10,... | collective-permute-start | bytes 884744 | tf_op jit(solution)/shard_map/ppermute | solution.py:585
  (46 other events, 745.1 us)
Sparse Core Ops, SparseCore 0:
  64.9 37.7 all-gather.3
  108.1 36.1 all-gather.5
  146.2 58.8 all-gather.7
  567.2 56.7 reduce-scatter.4
  627.7 76.4 reduce-scatter.2
